TPU v7x, 128 devices: a whole 4x4x4 slice. The times are simulated.
128 devices in a mesh: fsdp: 16 (over z_lo, x, core), tp: 8 (over y, z_hi).
Axes of the slice: x: 4, y: 4, z: 4 (z_hi: 2, z_lo: 2; z = z_hi * 2 + z_lo), core: 2. Of those that a mesh axis runs over, the one named last changes fastest.
Arguments:
- activations: bfloat16 [16384, 4096], P('fsdp', 'tp'), may hold values from -6 to 6
- cotangent: bfloat16 [16384, 4096], P('fsdp', 'tp'), may hold values from -6 to 6
- step_count: int32 [1], replicated, may hold values from 1 to 8
- region_of: int32 [16], replicated, may hold values from 0 to 3, never falling along the last dimension, each value on 1 to 8 neighbouring positions
- weight_master: float32 [4096, 4096], P('fsdp', 'tp'), may hold values from -0.75 to 0.75
- weight_moment: float32 [4096, 4096], P('fsdp', 'tp'), may hold values from -1.5 to 1.5
- weight_second: float32 [4096, 4096], P('fsdp', 'tp'), may hold values from 0.01 to 1
- adapter_copy: bfloat16 [2, 4, 4096, 256], P(None, None, 'tp'), may hold values from -6 to 6
- adapter_master: float32 [2, 4, 4096, 256], P(None, None, ('tp', 'fsdp')), may hold values from -0.75 to 0.75
- adapter_moment: float32 [2, 4, 4096, 256], P(None, None, ('tp', 'fsdp')), may hold values from -1.5 to 1.5
- adapter_second: float32 [2, 4, 4096, 256], P(None, None, ('tp', 'fsdp')), may hold values from 0.01 to 1
Outputs:
- new_weight: float32 [4096, 4096], P('fsdp', 'tp')
- new_weight_moment: float32 [4096, 4096], P('fsdp', 'tp')
- new_weight_second: float32 [4096, 4096], P('fsdp', 'tp')
- weight_next: bfloat16 [4096, 4096], P(None, 'tp')
- new_adapter: float32 [2, 4, 4096, 256], P(None, None, ('tp', 'fsdp'))
- new_adapter_moment: float32 [2, 4, 4096, 256], P(None, None, ('tp', 'fsdp'))
- new_adapter_second: float32 [2, 4, 4096, 256], P(None, None, ('tp', 'fsdp'))
- adapter_next: bfloat16 [2, 4, 4096, 256], P(None, None, 'tp')
Inputs may be any that keep to these rules, and one draw needn't show every extreme that they name: Never falling along the fsdp indices; region_of is nondecreasing; each of the 4 regions holds 1 to 8 consecutive fsdp indices, and one region holds exactly 8.
All inputs are finite; a program needn't handle non-finite values.
Results may differ from a plain program's by a relative error of at most 0.0049.
Values may be sent and summed in bfloat16 or wider, within the bound.
No kernel may reach another device: no remote copies, remote signals or barrier semaphores. Data moves between devices by JAX's collectives and lax.ppermute only.
A program may use at most 128 MiB of HBM per device.

v0:
```python
import math

import jax
import jax.numpy as jnp
from jax import lax
from jax.sharding import PartitionSpec as P

beta_first = 0.9
beta_second = 0.95
adam_eps = 1e-08
learn_rate = 0.1
decay_rate = 0.1


def adamw_update(param, moment, second, grad, step_count):
    step_float = step_count[0].astype(jnp.float32)
    first_fix = 1.0 - jnp.power(jnp.float32(beta_first), step_float)
    second_fix = 1.0 - jnp.power(jnp.float32(beta_second), step_float)
    moment_new = beta_first * moment + (1.0 - beta_first) * grad
    second_new = beta_second * second + (1.0 - beta_second) * grad * grad
    ratio = moment_new / first_fix / (jnp.sqrt(second_new / second_fix) + adam_eps)
    param_new = param - learn_rate * (ratio + decay_rate * param)
    return (param_new, moment_new, second_new)


def contract_rows(left, right):
    return lax.dot_general(
        left, right, (((0,), (0,)), ((), ())), preferred_element_type=jnp.float32
    )


def shards(
    activations,
    cotangent,
    step_count,
    region_of,
    weight_master,
    weight_moment,
    weight_second,
    adapter_copy,
    adapter_master,
    adapter_moment,
    adapter_second,
):
    fsdp_count = lax.axis_size("fsdp")
    tp_count = lax.axis_size("tp")
    tok_dev = activations.shape[0]
    width = activations.shape[1] * tp_count
    rank = adapter_copy.shape[3]
    region_count = adapter_copy.shape[1]
    grad_scale = math.sqrt(width / (tok_dev * fsdp_count))
    inv_width = 1.0 / math.sqrt(width)
    inv_rank = 1.0 / math.sqrt(rank)
    fsdp_index = lax.axis_index("fsdp")
    index_hot = (jnp.arange(fsdp_count, dtype=jnp.int32) == fsdp_index).astype(jnp.int32)
    own_region = jnp.sum(index_hot * region_of)
    region_hot = (jnp.arange(region_count, dtype=jnp.int32) == own_region).astype(jnp.float32)
    chosen = lax.dynamic_index_in_dim(adapter_copy, own_region, 1, keepdims=False)
    down_part = jnp.dot(activations, chosen[0], preferred_element_type=jnp.float32) * inv_width
    up_part = jnp.dot(cotangent, chosen[1], preferred_element_type=jnp.float32) * inv_rank
    low_down, low_up = lax.psum((down_part, up_part), "tp")
    low_down = low_down.astype(jnp.bfloat16)
    low_up = low_up.astype(jnp.bfloat16)
    grad_down = contract_rows(activations, low_up) * (inv_width * grad_scale)
    grad_up = contract_rows(cotangent, low_down) * (inv_rank * grad_scale)
    partial_grad = jnp.stack([grad_down, grad_up])
    padded_term = region_hot[None, :, None, None] * partial_grad[:, None]
    grad_adapter = lax.psum_scatter(padded_term, "fsdp", scatter_dimension=2, tiled=True)
    full_acts = lax.all_gather(activations, "tp", axis=1, tiled=True)
    grad_weight = lax.psum_scatter(
        contract_rows(full_acts, cotangent) * (inv_width * grad_scale),
        "fsdp",
        scatter_dimension=0,
        tiled=True,
    )
    new_weight, new_weight_moment, new_weight_second = adamw_update(
        weight_master, weight_moment, weight_second, grad_weight, step_count
    )
    new_adapter, new_adapter_moment, new_adapter_second = adamw_update(
        adapter_master, adapter_moment, adapter_second, grad_adapter, step_count
    )
    weight_next = lax.all_gather(new_weight.astype(jnp.bfloat16), "fsdp", axis=0, tiled=True)
    adapter_next = lax.all_gather(new_adapter.astype(jnp.bfloat16), "fsdp", axis=2, tiled=True)
    return (
        new_weight,
        new_weight_moment,
        new_weight_second,
        weight_next,
        new_adapter,
        new_adapter_moment,
        new_adapter_second,
        adapter_next,
    )


def solution(mesh):
    return jax.shard_map(
        shards,
        mesh=mesh,
        in_specs=(
            P("fsdp", "tp"),
            P("fsdp", "tp"),
            P(),
            P(),
            P("fsdp", "tp"),
            P("fsdp", "tp"),
            P("fsdp", "tp"),
            P(None, None, "tp", None),
            P(None, None, ("tp", "fsdp"), None),
            P(None, None, ("tp", "fsdp"), None),
            P(None, None, ("tp", "fsdp"), None),
        ),
        out_specs=(
            P("fsdp", "tp"),
            P("fsdp", "tp"),
            P("fsdp", "tp"),
            P(None, "tp"),
            P(None, None, ("tp", "fsdp"), None),
            P(None, None, ("tp", "fsdp"), None),
            P(None, None, ("tp", "fsdp"), None),
            P(None, None, "tp", None),
        ),
        check_vma=False,
    )
```

profile of v0, /device:TPU:1, one launch (start us, length us, event | category | flops | bytes accessed | tf_op | source)
XLA Modules:
  0.0 383.0 jit_solution(6098539737424900250)
XLA Ops:
  8.0 0.0 copy-start
  8.0 0.0 all-gather.4.cloned.1.call-start
  8.1 0.7 all-gather.4.cloned.1.call-update
  8.7 0.0 reduce-scatter.5.cloned.1.call-start
  8.8 1.3 fusion.8
  12.0 0.0 copy-done
  12.1 0.0 copy-start.1
  12.1 2.8 fusion
  14.8 2.7 fusion.1
  17.5 119.3 %all-reduce.2 = (bf16[1024,256]{0,1:T(8,128)(2,1)}, bf16[1024,256]{0,1:T(8,128)(2,1)}) all-reduce(f32[1024,256]{0,1:T(8,128)} %fusion, f32[1024,256]{0,1:T(8,128)} %fusion.1), channel_id=1, replica_groups=mesh['fsdp'=16,'tp'=8] {'tp'}, use_global_device_ids=true, to_apply=%region_3.4 | all-reduce | flops 524288 | bytes 3145728 | tf_op jit(solution)/shard_map/psum | solution.py:61
  136.8 1.8 fusion.2
  138.6 0.0 copy-done.1
  138.6 1.5 fusion.3
  140.1 0.1 pad_maximum_fusion
  140.2 1.3 copy.19
  141.5 0.6 compare_convert_fusion
  142.2 0.0 copy-start.2
  142.2 3.8 broadcast_multiply_fusion
  145.9 0.0 reduce-scatter.5.cloned.1.call-update
  146.0 0.0 reduce-scatter.3.cloned.1.call-start
  146.0 46.4 %all-gather.4.cloned.1.call-done = bf16[1024,4096]{1,0:T(8,128)(2,1)} async-done(((bf16[1024,512]{1,0:T(8,128)(2,1)}), bf16[1024,4096]{1,0:T(8,128)(2,1)}) %all-gather.4.cloned.1.call-update) | async-done | bytes 8388624 | tf_op jit(solution)/shard_map/all_gather | solution.py:69
  192.4 0.0 copy-done.2
  192.4 10.5 %convolution_multiply_fusion = f32[4096,512]{1,0:T(8,128)} fusion(bf16[1024,4096]{1,0:T(8,128)(2,1)} %all-gather.4.cloned.1.call-done, bf16[1024,512]{1,0:T(8,128)(2,1)S(1)} %copy-done.2), kind=kOutput, calls=%fused_computation | convolution fusion | flops 4297064448 | bytes 17825792 | tf_op jit(solution)/shard_map/dot_general | solution.py:27
  202.9 0.0 copy-start.6
  202.9 0.0 copy-start.4
  202.9 0.0 copy-start.5
  202.9 0.0 reduce-scatter.3.cloned.1.call-update
  202.9 0.0 all-gather.8.cloned.1.call-start
  203.8 11.5 %reduce-scatter.5.cloned.1.call-done = f32[2,4,32,256]{3,2,1,0:T(8,128)} async-done(((f32[2,4,512,256]{3,2,1,0:T(8,128)}), f32[2,4,32,256]{3,2,1,0:T(8,128)}) %reduce-scatter.5.cloned.1.call-update) | async-done | bytes 262160 | tf_op jit(solution)/shard_map/reduce_scatter | solution.py:68
  215.3 0.0 copy-done.6
  215.3 2.1 fusion.11
  217.4 0.0 all-gather.8.cloned.1.call-update
  217.4 0.0 all-gather.6.cloned.1.call-start
  217.5 73.0 %reduce-scatter.3.cloned.1.call-done = f32[256,512]{1,0:T(8,128)} async-done(((f32[4096,512]{1,0:T(8,128)}), f32[256,512]{1,0:T(8,128)}) %reduce-scatter.3.cloned.1.call-update) | async-done | bytes 524304 | tf_op jit(solution)/shard_map/reduce_scatter | solution.py:70
  290.5 0.0 copy-done.4
  290.5 0.0 copy-done.5
  290.5 2.7 fusion.13
  293.2 0.0 all-gather.6.cloned.1.call-update
  293.2 36.3 %all-gather.8.cloned.1.call-done = bf16[2,4,512,256]{3,2,1,0:T(8,128)(2,1)} async-done(((bf16[2,4,32,256]{3,2,1,0:T(8,128)(2,1)}), bf16[2,4,512,256]{3,2,1,0:T(8,128)(2,1)}) %all-gather.8.cloned.1.call-update) | async-done | bytes 2097168 | tf_op jit(solution)/shard_map/all_gather | solution.py:83
  329.5 40.0 %all-gather.6.cloned.1.call-done = bf16[4096,512]{1,0:T(8,128)(2,1)} async-done(((bf16[256,512]{1,0:T(8,128)(2,1)}), bf16[4096,512]{1,0:T(8,128)(2,1)}) %all-gather.6.cloned.1.call-update) | async-done | bytes 4194320 | tf_op jit(solution)/shard_map/all_gather | solution.py:82
  369.5 0.0 copy-start.3
  369.5 4.6 %copy.27 = bf16[4096,512]{1,0:T(8,128)(2,1)} copy(bf16[4096,512]{1,0:T(8,128)(2,1)} %all-gather.6.cloned.1.call-done) | data formatting | bytes 8388608
  374.1 0.0 copy-done.3
  374.1 1.3 copy.28
Async XLA Ops:
  8.0 4.0 %copy-start = (bf16[2,4,512,256]{3,2,1,0:T(8,128)(2,1)S(1)}, bf16[2,4,512,256]{3,2,1,0:T(8,128)(2,1)}, u32[]{:S(2)}) copy-start(bf16[2,4,512,256]{3,2,1,0:T(8,128)(2,1)} %param.18) | copy-start | bytes 6291460
  8.0 184.4 %all-gather.4.cloned.1.call-start = ((), (), s32[]{:S(2)}) async-start(), calls=%async_computation.2 | async-start | bytes 9437184 | tf_op jit(solution)/shard_map/all_gather | solution.py:69
  8.7 206.5 %reduce-scatter.5.cloned.1.call-start = ((), (), s32[]{:S(2)}) async-start(), calls=%async_computation.5 | async-start | bytes 4456448 | tf_op jit(solution)/shard_map/reduce_scatter | solution.py:68
  12.1 126.6 %copy-start.1 = (bf16[1024,512]{1,0:T(8,128)(2,1)S(1)}, bf16[1024,512]{1,0:T(8,128)(2,1)}, u32[]{:S(2)}) copy-start(bf16[1024,512]{1,0:T(8,128)(2,1)} %param.11) | copy-start | bytes 3145732
  142.2 50.2 %copy-start.2 = (bf16[1024,512]{1,0:T(8,128)(2,1)S(1)}, bf16[1024,512]{1,0:T(8,128)(2,1)}, u32[]{:S(2)}) copy-start(bf16[1024,512]{1,0:T(8,128)(2,1)} %param.12) | copy-start | bytes 3145732
  146.0 144.5 %reduce-scatter.3.cloned.1.call-start = ((), (), s32[]{:S(2)}) async-start(), calls=%async_computation.3 | async-start | bytes 8912896 | tf_op jit(solution)/shard_map/reduce_scatter | solution.py:70
  202.9 12.4 %copy-start.6 = (f32[2,4,32,256]{3,2,1,0:T(8,128)S(1)}, f32[2,4,32,256]{3,2,1,0:T(8,128)}, u32[]{:S(2)}) copy-start(f32[2,4,32,256]{3,2,1,0:T(8,128)} %param.19) | copy-start | bytes 786436
  202.9 87.6 %copy-start.4 = (f32[256,512]{1,0:T(8,128)S(1)}, f32[256,512]{1,0:T(8,128)}, u32[]{:S(2)}) copy-start(f32[256,512]{1,0:T(8,128)} %param.15) | copy-start | bytes 1572868
  202.9 87.6 %copy-start.5 = (f32[256,512]{1,0:T(8,128)S(1)}, f32[256,512]{1,0:T(8,128)}, u32[]{:S(2)}) copy-start(f32[256,512]{1,0:T(8,128)} %param.17) | copy-start | bytes 1572868
  202.9 126.6 %all-gather.8.cloned.1.call-start = ((), (), s32[]{:S(2)}) async-start(), calls=%async_computation.6 | async-start | bytes 2228224 | tf_op jit(solution)/shard_map/all_gather | solution.py:83
  217.4 152.0 %all-gather.6.cloned.1.call-start = ((), (), s32[]{:S(2)}) async-start(), calls=%async_computation.4 | async-start | bytes 4456448 | tf_op jit(solution)/shard_map/all_gather | solution.py:82
  369.5 4.6 %copy-start.3 = (bf16[2,4,512,256]{3,2,1,0:T(8,128)(2,1)S(1)}, bf16[2,4,512,256]{3,2,1,0:T(8,128)(2,1)}, u32[]{:S(2)}) copy-start(bf16[2,4,512,256]{3,2,1,0:T(8,128)(2,1)} %all-gather.8.cloned.1.call-done) | copy-start | bytes 6291460
Sparse Core Ops, SparseCore 0:
  11.0 181.2 all-gather.3
Sparse Core Ops, SparseCore 1:
  146.0 69.2 reduce-scatter.4
  217.5 72.9 reduce-scatter.2
  292.6 36.8 all-gather.7
  331.8 37.6 all-gather.5
where the time goes:
time: 383 us
  waiting for transfers between devices  208 us (54%)
  blocking collectives  119 us (31%)
  matrix products  19.2 us (5%)
  between operations  18.5 us (5%)
  other arithmetic  10.6 us (3%)
  local copies, waits for them, and re-layouts  7.28 us (2%)
    psum x1, blocking collectives, shards(): low_down, low_up = lax.psum((down_part, up_part), 'tp')  119 us
    reduce_scatter x1, waiting for transfers between devices, shards(): lax.psum_scatter(contract_rows(full_acts, cotangent) * (inv_width * grad_...  73 us
    all_gather x1, waiting for transfers between devices, shards(): full_acts = lax.all_gather(activations, 'tp', axis=1, tiled=True)  46.4 us
    all_gather x1, waiting for transfers between devices, shards(): lax.all_gather(new_weight.astype(jnp.bfloat16), 'fsdp', axis=0, tiled=True)  40 us
    all_gather x1, waiting for transfers between devices, shards(): lax.all_gather(new_adapter.astype(jnp.bfloat16), 'fsdp', axis=2, tiled=True)  36.3 us
    dot_general x3, matrix products, contract_rows(): lax.dot_general(left, right, (((0,), (0,)), ((), ())), preferred_element_...  13.8 us
    reduce_scatter x1, waiting for transfers between devices, shards(): lax.psum_scatter(padded_term, 'fsdp', scatter_dimension=2, tiled=True)  11.5 us
  transfers between devices with their start and end apart: 5, of which 5 were waited for; matrix products, arithmetic and copies ran while one was open for 8% of the time, Pallas kernels for 0%

commit v1 on v0

--- a/solution.py
+++ b/solution.py
@@ -10,6 +10,10 @@
 adam_eps = 1e-08
 learn_rate = 0.1
 decay_rate = 0.1
+
+AXES = ("fsdp", "tp")
+F32 = jnp.float32
+BF16 = jnp.bfloat16
 
 
 def adamw_update(param, moment, second, grad, step_count):
@@ -27,6 +31,48 @@
     return lax.dot_general(
         left, right, (((0,), (0,)), ((), ())), preferred_element_type=jnp.float32
     )
+
+
+def device_number(x, y, zl, zh, c):
+    return (zl * 8 + x * 2 + c) * 8 + (y * 2 + zh)
+
+
+def move(array, where):
+    pairs = []
+    for x in range(4):
+        for y in range(4):
+            for zl in range(2):
+                for zh in range(2):
+                    for c in range(2):
+                        a, b, d, e, g = where(x, y, zl, zh, c)
+                        pairs.append(
+                            (device_number(x, y, zl, zh, c), device_number(a % 4, b % 4, d, e, g))
+                        )
+    return lax.ppermute(array, AXES, pairs)
+
+
+def along_x(k):
+    return lambda x, y, zl, zh, c: (x + k, y, zl, zh, c)
+
+
+def along_y(k):
+    return lambda x, y, zl, zh, c: (x, y + k, zl, zh, c)
+
+
+def other_core(x, y, zl, zh, c):
+    return (x, y, zl, zh, 1 - c)
+
+
+def other_zl(x, y, zl, zh, c):
+    return (x, y, 1 - zl, zh, c)
+
+
+def other_zh(x, y, zl, zh, c):
+    return (x, y, zl, 1 - zh, c)
+
+
+def to_owner(ka, kb):
+    return lambda x, y, zl, zh, c: (2 * ((x & 1) ^ ka) + zh, y, zl ^ kb, x >> 1, c)
 
 
 def shards(
@@ -51,36 +97,103 @@
     grad_scale = math.sqrt(width / (tok_dev * fsdp_count))
     inv_width = 1.0 / math.sqrt(width)
     inv_rank = 1.0 / math.sqrt(rank)
-    fsdp_index = lax.axis_index("fsdp")
-    index_hot = (jnp.arange(fsdp_count, dtype=jnp.int32) == fsdp_index).astype(jnp.int32)
+    f = lax.axis_index("fsdp")
+    t = lax.axis_index("tp")
+    zl, x, c = f // 8, (f // 2) % 4, f % 2
+    y, zh = t // 2, t % 2
+
+    index_hot = (jnp.arange(fsdp_count, dtype=jnp.int32) == f).astype(jnp.int32)
     own_region = jnp.sum(index_hot * region_of)
-    region_hot = (jnp.arange(region_count, dtype=jnp.int32) == own_region).astype(jnp.float32)
     chosen = lax.dynamic_index_in_dim(adapter_copy, own_region, 1, keepdims=False)
-    down_part = jnp.dot(activations, chosen[0], preferred_element_type=jnp.float32) * inv_width
-    up_part = jnp.dot(cotangent, chosen[1], preferred_element_type=jnp.float32) * inv_rank
-    low_down, low_up = lax.psum((down_part, up_part), "tp")
-    low_down = low_down.astype(jnp.bfloat16)
-    low_up = low_up.astype(jnp.bfloat16)
+    down_part = jnp.dot(activations, chosen[0], preferred_element_type=F32) * inv_width
+    up_part = jnp.dot(cotangent, chosen[1], preferred_element_type=F32) * inv_rank
+    low_part = jnp.concatenate([down_part.astype(BF16), up_part.astype(BF16)], axis=1)
+    quarter = tok_dev // 4
+
+    def low_for(k):
+        return lax.dynamic_slice_in_dim(low_part, ((y + k) % 4) * quarter, quarter, 0)
+
+    low_sum = low_for(0).astype(F32)
+    for k in (1, 3, 2):
+        low_sum = low_sum + move(low_for(k), along_y(k)).astype(F32)
+    low_sum = low_sum.astype(BF16)
+    low_own = (low_sum.astype(F32) + move(low_sum, other_zh).astype(F32)).astype(BF16)
+    low = jnp.zeros((tok_dev, 2 * rank), BF16)
+    low = lax.dynamic_update_slice_in_dim(low, low_own, y * quarter, 0)
+    for k in (1, 3, 2):
+        low = lax.dynamic_update_slice_in_dim(
+            low, move(low_own, along_y(k)), ((y - k) % 4) * quarter, 0
+        )
+    low_down, low_up = low[:, :rank], low[:, rank:]
     grad_down = contract_rows(activations, low_up) * (inv_width * grad_scale)
     grad_up = contract_rows(cotangent, low_down) * (inv_rank * grad_scale)
-    partial_grad = jnp.stack([grad_down, grad_up])
-    padded_term = region_hot[None, :, None, None] * partial_grad[:, None]
-    grad_adapter = lax.psum_scatter(padded_term, "fsdp", scatter_dimension=2, tiled=True)
-    full_acts = lax.all_gather(activations, "tp", axis=1, tiled=True)
-    grad_weight = lax.psum_scatter(
-        contract_rows(full_acts, cotangent) * (inv_width * grad_scale),
-        "fsdp",
-        scatter_dimension=0,
-        tiled=True,
+    partial_grad = jnp.stack([grad_down, grad_up]).astype(BF16)
+    rows = partial_grad.shape[1] // fsdp_count
+    parts = partial_grad.reshape(2, fsdp_count, rows, rank)
+    got = lax.all_to_all(parts, "fsdp", 1, 0, tiled=False)
+    region_hot = (region_of[None, :] == jnp.arange(region_count)[:, None]).astype(BF16)
+    grad_adapter = lax.dot_general(
+        region_hot, got.reshape(fsdp_count, 2 * rows * rank), (((1,), (0,)), ((), ())),
+        preferred_element_type=F32,
+    ).reshape(region_count, 2, rows, rank).transpose(1, 0, 2, 3)
+    new_adapter, new_adapter_moment, new_adapter_second = adamw_update(
+        adapter_master, adapter_moment, adapter_second, grad_adapter, step_count
+    )
+    adapter_next = lax.all_gather(new_adapter.astype(BF16), "fsdp", axis=2, tiled=True)
+
+    half = activations.shape[1] // 2
+    act_own = lax.dynamic_slice_in_dim(activations, c * half, half, 1)
+    act_other = move(lax.dynamic_slice_in_dim(activations, (1 - c) * half, half, 1), other_core)
+    act = jnp.concatenate([act_own, act_other], axis=0)
+    act_back = move(act, along_y(1))
+    act_ahead = move(act, along_y(-1))
+    act_far = jnp.concatenate(
+        [move(act_back[:tok_dev], along_y(1)), move(act_ahead[tok_dev:], along_y(-1))], axis=0
+    )
+    cot_own = jnp.concatenate([cotangent, move(cotangent, other_core)], axis=0)
+    cot_zh = move(cotangent, other_zh)
+    cot_zh = jnp.concatenate([cot_zh, move(cot_zh, other_core)], axis=0)
+
+    def partial(left):
+        both = [contract_rows(left, cot_own), contract_rows(left, cot_zh)]
+        return (jnp.concatenate(both, axis=1) * (inv_width * grad_scale)).astype(BF16)
+
+    def sum_over_x(part):
+        wide = part.shape[1] // 4
+
+        def piece(k):
+            q = (x + k) % 4
+            start = ((q // 2) ^ zh) * (2 * wide) + (q % 2) * wide
+            return lax.dynamic_slice_in_dim(part, start, wide, 1)
+
+        total = piece(0).astype(F32)
+        for k in (1, 3, 2):
+            total = total + move(piece(k), along_x(k)).astype(F32)
+        return total.astype(BF16)
+
+    near = sum_over_x(
+        jnp.concatenate([partial(act), partial(act_ahead), partial(act_back)], axis=0)
+    )
+    far = sum_over_x(partial(act_far))
+    blocks = jnp.concatenate([near, far], axis=0).reshape(4, half, half)
+    place = jnp.array([0, 1, 3, 2], jnp.int32)
+    sums = []
+    for ka in range(2):
+        total = None
+        for kb in range(2):
+            row_y = 2 * (zl ^ kb) + ((x & 1) ^ ka)
+            block = lax.dynamic_index_in_dim(blocks, place[(row_y - y) % 4], 0, keepdims=False)
+            term = move(block, to_owner(ka, kb)).astype(F32)
+            total = term if total is None else total + term
+        sums.append(total)
+    flip = (x >> 1) == 1
+    grad_weight = jnp.concatenate(
+        [jnp.where(flip, sums[1], sums[0]), jnp.where(flip, sums[0], sums[1])], axis=1
     )
     new_weight, new_weight_moment, new_weight_second = adamw_update(
         weight_master, weight_moment, weight_second, grad_weight, step_count
     )
-    new_adapter, new_adapter_moment, new_adapter_second = adamw_update(
-        adapter_master, adapter_moment, adapter_second, grad_adapter, step_count
-    )
-    weight_next = lax.all_gather(new_weight.astype(jnp.bfloat16), "fsdp", axis=0, tiled=True)
-    adapter_next = lax.all_gather(new_adapter.astype(jnp.bfloat16), "fsdp", axis=2, tiled=True)
+    weight_next = lax.all_gather(new_weight.astype(BF16), "fsdp", axis=0, tiled=True)
     return (
         new_weight,
         new_weight_moment,

time: 383 us -> 224 us (0.58)
  waiting for transfers between devices: 208 us -> 83.1 us
  blocking collectives: 119 us -> 0 us
  starting transfers between devices: 0.21 us -> 48.3 us
  local copies, waits for them, and re-layouts: 7.28 us -> 28.7 us
  between operations: 18.5 us -> 24.9 us
  other arithmetic: 10.6 us -> 15.3 us
    psum x1 -> x0, blocking collectives: 119 us -> none  [shards(): low_down, low_up = lax.psum((down_part, up_part), 'tp')]
    reduce_scatter x2 -> x0, waiting for transfers between devices: 84.5 us -> none  [the longest x1 73 us: shards(): lax.psum_scatter(contract_rows(full_acts, cotangent) * (inv_width * grad_...]
    all_gather x3 -> x2, waiting for transfers between devices: 123 us -> 44.9 us  [the longest x1 44.9 us: shards(): lax.all_gather(new_weight.astype(BF16), 'fsdp', axis=0, tiled=True)]
    ppermute x0 -> x25, starting transfers between devices: none -> 37.8 us  [move(): return lax.ppermute(array, AXES, pairs)]
    ppermute x0 -> x25, waiting for transfers between devices: none -> 36.2 us  [move(): return lax.ppermute(array, AXES, pairs)]
    all_to_all x0 -> x1, starting transfers between devices: none -> 10.4 us  [shards(): got = lax.all_to_all(parts, 'fsdp', 1, 0, tiled=False)]
    unnamed x16 -> x46, local copies, waits for them, and re-layouts: 5.97 us -> 13.1 us
    dot_general x3 -> x10, matrix products: 13.8 us -> 18.6 us  [contract_rows(): lax.dot_general(left, right, (((0,), (0,)), ((), ())), preferred_element_...]
  transfers between devices with their start and end apart: 5 -> 28, of which waited for: 5 -> 15; matrix products, arithmetic and copies ran while one was open for 8% -> 23% of each run, Pallas kernels for 0% -> 0%
where the time goes in v1:
time: 224 us; the launch traced here: 223 us
  waiting for transfers between devices  83.1 us (37%)
  starting transfers between devices  48.3 us (22%)
  local copies, waits for them, and re-layouts  28.7 us (13%)
  between operations  24.9 us (11%)
  matrix products  22.5 us (10%)
  other arithmetic  15.3 us (7%)
    all_gather x1, waiting for transfers between devices, shards(): lax.all_gather(new_weight.astype(BF16), 'fsdp', axis=0, tiled=True)  44.9 us
    ppermute x25, starting transfers between devices, move(): return lax.ppermute(array, AXES, pairs)  37.8 us
    ppermute x25, waiting for transfers between devices, move(): return lax.ppermute(array, AXES, pairs)  36.2 us
    dot_general x10, matrix products, contract_rows(): lax.dot_general(left, right, (((0,), (0,)), ((), ())), preferred_element_...  18.6 us
    unnamed x46, local copies, waits for them, and re-layouts  13.1 us
    all_to_all x1, starting transfers between devices, shards(): got = lax.all_to_all(parts, 'fsdp', 1, 0, tiled=False)  10.4 us
  transfers between devices with their start and end apart: 28, of which 15 were waited for; matrix products, arithmetic and copies ran while one was open for 23% of the time, Pallas kernels for 0%

profile of v1, /device:TPU:1, one launch (start us, length us, event | category | flops | bytes accessed | tf_op | source)
XLA Modules:
  0.0 222.7 jit_solution(8184199063018817831)
XLA Ops:
  7.2 1.4 fusion.30
  10.7 1.7 fusion.3
  12.4 1.7 fusion.2
  14.1 0.9 fusion.20
  15.0 3.8 %collective-permute-start.20 = (bf16[256,512]{0,1:T(8,128)(2,1)}, bf16[256,512]{0,1:T(8,128)(2,1)S(1)}, u32[]{:S(2)}, u32[]{:S(2)}) collective-permute-start(bf16[256,512]{0,1:T(8,128)(2,1)} %get-tuple-element.47), channel_id=1, source_target_pairs={{0,4},{8,12},{1,5},{9,13},{64,68},{72,76},{65,69},{73,77},{2,6},{1... | collective-permute-start | bytes 786440 | tf_op jit(solution)/shard_map/ppermute | solution.py:51
  18.8 0.8 collective-permute-start.19
  20.3 4.5 %collective-permute-done.20 = bf16[256,512]{0,1:T(8,128)(2,1)S(1)} collective-permute-done((bf16[256,512]{0,1:T(8,128)(2,1)}, bf16[256,512]{0,1:T(8,128)(2,1)S(1)}, u32[]{:S(2)}, u32[]{:S(2)}) %collective-permute-start.20) | collective-permute-done | bytes 262176 | tf_op jit(solution)/shard_map/ppermute | solution.py:51
  24.8 6.1 %collective-permute-done.19 = bf16[256,512]{0,1:T(8,128)(2,1)} collective-permute-done((bf16[256,512]{0,1:T(8,128)(2,1)}, bf16[256,512]{0,1:T(8,128)(2,1)}, u32[]{:S(2)}, u32[]{:S(2)}) %collective-permute-start.19) | collective-permute-done | bytes 262176 | tf_op jit(solution)/shard_map/ppermute | solution.py:51
  31.3 1.2 add_convert_fusion.2
  32.5 3.7 %collective-permute-start.21 = (bf16[256,512]{0,1:T(8,128)(2,1)S(1)}, bf16[256,512]{0,1:T(8,128)(2,1)}, u32[]{:S(2)}, u32[]{:S(2)}) collective-permute-start(bf16[256,512]{0,1:T(8,128)(2,1)S(1)} %add_convert_fusion.2), channel_id=1, source_target_pairs={{0,1},{8,9},{1,0},{9,8},{64,65},{72,73},{65,64},{73,72},{2,3},{10,... | collective-permute-start | bytes 786440 | tf_op jit(solution)/shard_map/ppermute | solution.py:51
  36.3 0.9 constant_dynamic-slice_fusion.7
  37.1 1.4 collective-permute-start
  38.6 3.3 %collective-permute-done.21 = bf16[256,512]{0,1:T(8,128)(2,1)} collective-permute-done((bf16[256,512]{0,1:T(8,128)(2,1)S(1)}, bf16[256,512]{0,1:T(8,128)(2,1)}, u32[]{:S(2)}, u32[]{:S(2)}) %collective-permute-start.21) | collective-permute-done | bytes 262176 | tf_op jit(solution)/shard_map/ppermute | solution.py:51
  41.9 1.1 broadcast_in_dim.2
  43.0 1.8 constant_dynamic-update-slice_fusion.9
  44.8 2.0 collective-permute-start.22
  46.8 2.3 %constant_dynamic-update-slice_fusion.1 = bf16[2048,512]{1,0:T(8,128)(2,1)} fusion(bf16[1024,512]{1,0:T(8,128)(2,1)} %param.13), kind=kLoop, calls=%fused_computation.65 | loop fusion | bytes 2097152
  49.9 1.7 collective-permute-start.23
  51.6 1.6 collective-permute-start.24
  53.2 1.0 pad_maximum_fusion.1
  56.0 3.8 %collective-permute-start.4 = (bf16[2048,256]{1,0:T(8,128)(2,1)}, bf16[2048,256]{1,0:T(8,128)(2,1)}, u32[]{:S(2)}, u32[]{:S(2)}) collective-permute-start(bf16[2048,256]{1,0:T(8,128)(2,1)} %pad_maximum_fusion.1), channel_id=1, source_target_pairs={{0,6},{8,14},{1,7},{9,15},{64,70},{72,78},{65,71},{73,79},{2,0},{1... | collective-permute-start | bytes 3145736 | tf_op jit(solution)/shard_map/ppermute | solution.py:51
  61.4 2.5 %fusion.6 = bf16[512,256]{0,1:T(8,128)(2,1)} fusion(bf16[1024,512]{1,0:T(8,128)(2,1)} %param.13, bf16[1024,512]{0,1:T(8,128)(2,1)} %constant_dynamic-update-slice_fusion.6), kind=kOutput, calls=%fused_computation.19 | convolution fusion | flops 268697600 | bytes 1835008 | tf_op jit(solution)/shard_map/dot_general | solution.py:31
  63.9 1.1 copy.53
  65.0 2.2 fusion.7
  67.2 1.1 copy.52
  68.4 0.9 copy.54
  69.2 10.4 %all-to-all-start = ((bf16[1,2,16,32,256]{4,3,1,0,2:T(8,128)(2,1)}), bf16[1,2,16,32,256]{4,3,1,0,2:T(8,128)(2,1)S(1)}, u32[]{:S(2)}, u32[]{:S(2)}) async-start(bf16[1,2,16,32,256]{4,3,1,0,2:T(8,128)(2,1)} %copy.54), calls=%async_computation | async-start | bytes 1048576 | tf_op jit(solution)/shard_map/all_to_all | solution.py:133
  79.7 2.3 %constant_dynamic-update-slice_fusion.3 = bf16[2048,512]{1,0:T(8,128)(2,1)} fusion(bf16[1024,512]{1,0:T(8,128)(2,1)} %collective-permute-done.2), kind=kLoop, calls=%fused_computation.67 | loop fusion | bytes 2097152
  82.1 2.3 %constant_dynamic-update-slice_fusion = bf16[2048,512]{1,0:T(8,128)(2,1)} fusion(bf16[2048,512]{1,0:T(8,128)(2,1)} %constant_dynamic-update-slice_fusion.1, bf16[1024,512]{1,0:T(8,128)(2,1)} %collective-permute-done.1), kind=kLoop, calls=%fused_computation.64 | loop fusion | bytes 2097152 | tf_op jit(solution)/shard_map/concatenate | solution.py:153
  84.4 3.1 %fusion.32 = f32[256,512]{1,0:T(8,128)} fusion(bf16[2048,512]{1,0:T(8,128)(2,1)} %constant_dynamic-update-slice_fusion, bf16[1024,256]{1,0:T(8,128)(2,1)S(1)} %copy-done.14, bf16[1024,256]{1,0:T(8,128)(2,1)S(1)} %copy-done.6), kind=kOutput, calls=%fused_computation.90 | convolution fusion | flops 538968064 | bytes 3670016 | tf_op jit(solution)/shard_map/dot_general | solution.py:31
  87.5 2.0 all-to-all-done
  90.3 2.1 fusion.33
  92.4 1.1 slice.26
  93.5 3.5 %collective-permute-start.9 = (bf16[1024,256]{1,0:T(8,128)(2,1)S(1)}, bf16[1024,256]{1,0:T(8,128)(2,1)S(1)}, u32[]{:S(2)}, u32[]{:S(2)}) collective-permute-start(bf16[1024,256]{1,0:T(8,128)(2,1)S(1)} %slice.26), channel_id=1, source_target_pairs={{0,2},{8,10},{1,3},{9,11},{64,66},{72,74},{65,67},{73,75},{2,4},{1... | collective-permute-start | bytes 1572872 | tf_op jit(solution)/shard_map/ppermute | solution.py:51
  97.0 1.1 slice.27
  98.7 2.7 %fusion.41 = f32[256,512]{1,0:T(8,128)S(1)} fusion(bf16[2048,256]{1,0:T(8,128)(2,1)} %collective-permute-done.5, bf16[2048,512]{1,0:T(8,128)(2,1)} %constant_dynamic-update-slice_fusion), kind=kOutput, calls=%fused_computation.96 | convolution fusion | flops 536870912 | bytes 3670016 | tf_op jit(solution)/shard_map/dot_general | solution.py:31
  101.4 1.9 fusion.39
  103.3 5.2 %collective-permute-done.9 = bf16[1024,256]{1,0:T(8,128)(2,1)S(1)} collective-permute-done((bf16[1024,256]{1,0:T(8,128)(2,1)S(1)}, bf16[1024,256]{1,0:T(8,128)(2,1)S(1)}, u32[]{:S(2)}, u32[]{:S(2)}) %collective-permute-start.9) | collective-permute-done | bytes 524320 | tf_op jit(solution)/shard_map/ppermute | solution.py:51
  108.5 1.9 collective-permute-done.10
  110.5 0.7 fusion.43
  111.2 0.8 copy-done.12
  112.1 1.3 constant_dynamic-update-slice_fusion.2
  114.3 2.5 %collective-permute-start.13 = (bf16[256,256]{1,0:T(8,128)(2,1)S(1)}, bf16[256,256]{1,0:T(8,128)(2,1)S(1)}, u32[]{:S(2)}, u32[]{:S(2)}) collective-permute-start(bf16[256,256]{1,0:T(8,128)(2,1)S(1)} %get-tuple-element.57), channel_id=1, source_target_pairs={{0,32},{8,40},{1,33},{9,41},{64,96},{72,104},{65,97},{73,105},{2,3... | collective-permute-start | bytes 393224 | tf_op jit(solution)/shard_map/ppermute | solution.py:51
  116.8 2.0 fusion.42
  118.9 2.0 fusion.40
  122.3 1.1 copy-done.1
  123.4 1.0 constant_dynamic-slice_fusion.5
  124.9 2.5 %collective-permute-start.7 = (bf16[768,256]{1,0:T(8,128)(2,1)}, bf16[768,256]{1,0:T(8,128)(2,1)}, u32[]{:S(2)}, u32[]{:S(2)}) collective-permute-start(bf16[768,256]{1,0:T(8,128)(2,1)} %get-tuple-element.44), channel_id=1, source_target_pairs={{0,48},{8,56},{1,49},{9,57},{64,112},{72,120},{65,113},{73,121},{2... | collective-permute-start | bytes 1179656 | tf_op jit(solution)/shard_map/ppermute | solution.py:51
  127.4 2.7 %collective-permute-start.12 = (bf16[256,256]{1,0:T(8,128)(2,1)S(1)}, bf16[256,256]{1,0:T(8,128)(2,1)S(1)}, u32[]{:S(2)}, u32[]{:S(2)}) collective-permute-start(bf16[256,256]{1,0:T(8,128)(2,1)S(1)} %get-tuple-element.58), channel_id=1, source_target_pairs={{0,48},{8,56},{1,49},{9,57},{64,112},{72,120},{65,113},{73,121},{2... | collective-permute-start | bytes 393224 | tf_op jit(solution)/shard_map/ppermute | solution.py:51
  138.4 7.5 %collective-permute-done.12 = bf16[256,256]{1,0:T(8,128)(2,1)S(1)} collective-permute-done((bf16[256,256]{1,0:T(8,128)(2,1)S(1)}, bf16[256,256]{1,0:T(8,128)(2,1)S(1)}, u32[]{:S(2)}, u32[]{:S(2)}) %collective-permute-start.12) | collective-permute-done | bytes 131104 | tf_op jit(solution)/shard_map/ppermute | solution.py:51
  145.9 2.7 %collective-permute-done.11 = bf16[256,256]{1,0:T(8,128)(2,1)} collective-permute-done((bf16[256,256]{1,0:T(8,128)(2,1)S(1)}, bf16[256,256]{1,0:T(8,128)(2,1)}, u32[]{:S(2)}, u32[]{:S(2)}) %collective-permute-start.11) | collective-permute-done | bytes 131104 | tf_op jit(solution)/shard_map/ppermute | solution.py:51
  148.5 1.0 add_convert_fusion.3
  149.6 1.6 add_convert_fusion
  151.3 0.7 dynamic-slice_bitcast_fusion.5
  152.0 1.8 collective-permute-start.15
  153.8 2.4 %collective-permute-start.14 = (bf16[256,256]{1,0:T(8,128)(2,1)}, bf16[256,256]{1,0:T(8,128)(2,1)}, u32[]{:S(2)}, u32[]{:S(2)}) collective-permute-start(bf16[256,256]{1,0:T(8,128)(2,1)} %get-tuple-element.55), channel_id=1, source_target_pairs={{0,32},{8,40},{1,48},{9,56},{64,96},{72,104},{65,112},{73,120},{2,... | collective-permute-start | bytes 393224 | tf_op jit(solution)/shard_map/ppermute | solution.py:51
  156.2 1.3 collective-permute-start.16
  157.7 2.9 %collective-permute-done.14 = bf16[256,256]{1,0:T(8,128)(2,1)} collective-permute-done((bf16[256,256]{1,0:T(8,128)(2,1)}, bf16[256,256]{1,0:T(8,128)(2,1)}, u32[]{:S(2)}, u32[]{:S(2)}) %collective-permute-start.14) | collective-permute-done | bytes 131104 | tf_op jit(solution)/shard_map/ppermute | solution.py:51
  160.6 0.7 collective-permute-done.17
  161.3 1.1 fusion.24
  162.5 2.5 %fusion.36 = (bf16[256,512]{1,0:T(8,128)(2,1)}, f32[256,512]{1,0:T(8,128)}, f32[256,512]{1,0:T(8,128)}, f32[256,512]{1,0:T(8,128)}) fusion(f32[256,512]{1,0:T(8,128)S(1)} %copy-done.8, f32[]{:T(128)} %bitcast.10, f32[]{:T(128)} %bitcast.9, f32[256,256]{1,0:T(8,128)S(1)} %get-tuple-element.51, f32[256,256]{1,0:T(8,128)S(1)} %get-tuple-element.50, ...), kind=kLoop, calls=%fused_computation.92 | loop fusion | flops 2228224 | bytes 3932168 | tf_op jit(solution)/shard_map/convert_element_type | solution.py:196
  165.0 44.9 %all-gather.3.cloned.1.call-done = bf16[4096,512]{1,0:T(8,128)(2,1)} async-done(((bf16[256,512]{1,0:T(8,128)(2,1)}), bf16[4096,512]{1,0:T(8,128)(2,1)}) %all-gather.3.cloned.1.call-update) | async-done | bytes 4194320 | tf_op jit(solution)/shard_map/all_gather | solution.py:196
  209.9 4.6 %copy.75 = bf16[4096,512]{1,0:T(8,128)(2,1)} copy(bf16[4096,512]{1,0:T(8,128)(2,1)} %all-gather.3.cloned.1.call-done) | data formatting | bytes 8388608
  214.5 1.3 copy.76
  (88 shorter events, 9.8 us)
Async XLA Ops:
  7.2 3.5 %copy-start = (bf16[2,4,512,256]{3,2,1,0:T(8,128)(2,1)S(1)}, bf16[2,4,512,256]{3,2,1,0:T(8,128)(2,1)}, u32[]{:S(2)}) copy-start(bf16[2,4,512,256]{3,2,1,0:T(8,128)(2,1)} %param.19) | copy-start | bytes 6291460
  15.0 9.7 %collective-permute-start.20 = (bf16[256,512]{0,1:T(8,128)(2,1)}, bf16[256,512]{0,1:T(8,128)(2,1)S(1)}, u32[]{:S(2)}, u32[]{:S(2)}) collective-permute-start(bf16[256,512]{0,1:T(8,128)(2,1)} %get-tuple-element.47), channel_id=1, source_target_pairs={{0,4},{8,12},{1,5},{9,13},{64,68},{72,76},{65,69},{73,77},{2,6},{1... | collective-permute-start | bytes 786440 | tf_op jit(solution)/shard_map/ppermute | solution.py:51
  18.8 12.1 %collective-permute-start.19 = (bf16[256,512]{0,1:T(8,128)(2,1)}, bf16[256,512]{0,1:T(8,128)(2,1)}, u32[]{:S(2)}, u32[]{:S(2)}) collective-permute-start(bf16[256,512]{0,1:T(8,128)(2,1)} %get-tuple-element.46), channel_id=1, source_target_pairs={{0,6},{8,14},{1,7},{9,15},{64,70},{72,78},{65,71},{73,79},{2,0},{1... | collective-permute-start | bytes 786440 | tf_op jit(solution)/shard_map/ppermute | solution.py:51
  19.6 11.7 %collective-permute-start.18 = (bf16[256,512]{0,1:T(8,128)(2,1)}, bf16[256,512]{0,1:T(8,128)(2,1)}, u32[]{:S(2)}, u32[]{:S(2)}) collective-permute-start(bf16[256,512]{0,1:T(8,128)(2,1)} %get-tuple-element.45), channel_id=1, source_target_pairs={{0,2},{8,10},{1,3},{9,11},{64,66},{72,74},{65,67},{73,75},{2,4},{1... | collective-permute-start | bytes 786440 | tf_op jit(solution)/shard_map/ppermute | solution.py:51
  20.3 16.0 %copy-start.2 = (bf16[1024,512]{1,0:T(8,128)(2,1)S(1)}, bf16[1024,512]{1,0:T(8,128)(2,1)}, u32[]{:S(2)}) copy-start(bf16[1024,512]{1,0:T(8,128)(2,1)} %param.12) | copy-start | bytes 3145732
  24.7 6.1 %copy-start.17 = (bf16[256,512]{0,1:T(8,128)(2,1)}, bf16[256,512]{0,1:T(8,128)(2,1)S(1)}, u32[]{:S(2)}) copy-start(bf16[256,512]{0,1:T(8,128)(2,1)S(1)} %collective-permute-done.20) | copy-start | bytes 786436
  32.5 9.4 %collective-permute-start.21 = (bf16[256,512]{0,1:T(8,128)(2,1)S(1)}, bf16[256,512]{0,1:T(8,128)(2,1)}, u32[]{:S(2)}, u32[]{:S(2)}) collective-permute-start(bf16[256,512]{0,1:T(8,128)(2,1)S(1)} %add_convert_fusion.2), channel_id=1, source_target_pairs={{0,1},{8,9},{1,0},{9,8},{64,65},{72,73},{65,64},{73,72},{2,3},{10,... | collective-permute-start | bytes 786440 | tf_op jit(solution)/shard_map/ppermute | solution.py:51
  37.1 16.1 %copy-start.5 = (bf16[1024,256]{1,0:T(8,128)(2,1)}, bf16[1024,256]{1,0:T(8,128)(2,1)S(1)}, u32[]{:S(2)}) copy-start(bf16[1024,256]{1,0:T(8,128)(2,1)S(1)} %get-tuple-element.48) | copy-start | bytes 1572868
  37.1 14.5 %collective-permute-start = (bf16[1024,256]{1,0:T(8,128)(2,1)}, bf16[1024,256]{1,0:T(8,128)(2,1)S(1)}, u32[]{:S(2)}, u32[]{:S(2)}) collective-permute-start(bf16[1024,256]{1,0:T(8,128)(2,1)} %get-tuple-element.49), channel_id=1, source_target_pairs={{0,8},{8,0},{1,9},{9,1},{64,72},{72,64},{65,73},{73,65},{2,10},{10... | collective-permute-start | bytes 1572872 | tf_op jit(solution)/shard_map/ppermute | solution.py:51
  38.5 41.2 %collective-permute-start.2 = (bf16[1024,512]{1,0:T(8,128)(2,1)}, bf16[1024,512]{1,0:T(8,128)(2,1)}, u32[]{:S(2)}, u32[]{:S(2)}) collective-permute-start(bf16[1024,512]{1,0:T(8,128)(2,1)} %param.13), channel_id=1, source_target_pairs={{0,1},{8,9},{1,0},{9,8},{64,65},{72,73},{65,64},{73,72},{2,3},{10,... | collective-permute-start | bytes 3145736 | tf_op jit(solution)/shard_map/ppermute | solution.py:51
  38.5 43.6 %collective-permute-start.1 = (bf16[1024,512]{1,0:T(8,128)(2,1)}, bf16[1024,512]{1,0:T(8,128)(2,1)}, u32[]{:S(2)}, u32[]{:S(2)}) collective-permute-start(bf16[1024,512]{1,0:T(8,128)(2,1)} %param.13), channel_id=1, source_target_pairs={{0,8},{8,0},{1,9},{9,1},{64,72},{72,64},{65,73},{73,65},{2,10},{10... | collective-permute-start | bytes 3145736 | tf_op jit(solution)/shard_map/ppermute | solution.py:51
  44.8 9.5 %collective-permute-start.22 = (bf16[256,512]{0,1:T(8,128)(2,1)}, bf16[256,512]{0,1:T(8,128)(2,1)S(1)}, u32[]{:S(2)}, u32[]{:S(2)}) collective-permute-start(bf16[256,512]{0,1:T(8,128)(2,1)} %get-tuple-element.37), channel_id=1, source_target_pairs={{0,2},{8,10},{1,3},{9,11},{64,66},{72,74},{65,67},{73,75},{2,4},{1... | collective-permute-start | bytes 786440 | tf_op jit(solution)/shard_map/ppermute | solution.py:51
  49.9 6.2 %collective-permute-start.23 = (bf16[256,512]{0,1:T(8,128)(2,1)}, bf16[256,512]{0,1:T(8,128)(2,1)S(1)}, u32[]{:S(2)}, u32[]{:S(2)}) collective-permute-start(bf16[256,512]{0,1:T(8,128)(2,1)} %get-tuple-element.37), channel_id=1, source_target_pairs={{0,6},{8,14},{1,7},{9,15},{64,70},{72,78},{65,71},{73,79},{2,0},{1... | collective-permute-start | bytes 786440 | tf_op jit(solution)/shard_map/ppermute | solution.py:51
  51.6 3.1 %copy-start.13 = (bf16[1024,256]{1,0:T(8,128)(2,1)}, bf16[1024,256]{1,0:T(8,128)(2,1)S(1)}, u32[]{:S(2)}) copy-start(bf16[1024,256]{1,0:T(8,128)(2,1)S(1)} %collective-permute-done) | copy-start | bytes 1572868
  51.6 9.1 %collective-permute-start.24 = (bf16[256,512]{0,1:T(8,128)(2,1)}, bf16[256,512]{0,1:T(8,128)(2,1)S(1)}, u32[]{:S(2)}, u32[]{:S(2)}) collective-permute-start(bf16[256,512]{0,1:T(8,128)(2,1)} %get-tuple-element.37), channel_id=1, source_target_pairs={{0,4},{8,12},{1,5},{9,13},{64,68},{72,76},{65,69},{73,77},{2,6},{1... | collective-permute-start | bytes 786440 | tf_op jit(solution)/shard_map/ppermute | solution.py:51
  54.3 38.2 %collective-permute-start.5 = (bf16[2048,256]{1,0:T(8,128)(2,1)}, bf16[2048,256]{1,0:T(8,128)(2,1)}, u32[]{:S(2)}, u32[]{:S(2)}) collective-permute-start(bf16[2048,256]{1,0:T(8,128)(2,1)} %pad_maximum_fusion.1), channel_id=1, source_target_pairs={{0,2},{8,10},{1,3},{9,11},{64,66},{72,74},{65,67},{73,75},{2,4},{1... | collective-permute-start | bytes 3145736 | tf_op jit(solution)/shard_map/ppermute | solution.py:51
  54.7 10.3 %copy-start.3 = (bf16[1024,512]{1,0:T(8,128)(2,1)S(1)}, bf16[1024,512]{1,0:T(8,128)(2,1)}, u32[]{:S(2)}) copy-start(bf16[1024,512]{1,0:T(8,128)(2,1)} %param.12) | copy-start | bytes 3145732
  56.0 41.0 %collective-permute-start.4 = (bf16[2048,256]{1,0:T(8,128)(2,1)}, bf16[2048,256]{1,0:T(8,128)(2,1)}, u32[]{:S(2)}, u32[]{:S(2)}) collective-permute-start(bf16[2048,256]{1,0:T(8,128)(2,1)} %pad_maximum_fusion.1), channel_id=1, source_target_pairs={{0,6},{8,14},{1,7},{9,15},{64,70},{72,78},{65,71},{73,79},{2,0},{1... | collective-permute-start | bytes 3145736 | tf_op jit(solution)/shard_map/ppermute | solution.py:51
  69.2 20.3 %all-to-all-start = ((bf16[1,2,16,32,256]{4,3,1,0,2:T(8,128)(2,1)}), bf16[1,2,16,32,256]{4,3,1,0,2:T(8,128)(2,1)S(1)}, u32[]{:S(2)}, u32[]{:S(2)}) async-start(bf16[1,2,16,32,256]{4,3,1,0,2:T(8,128)(2,1)} %copy.54), calls=%async_computation | async-start | bytes 1048576 | tf_op jit(solution)/shard_map/all_to_all | solution.py:133
  79.6 4.8 %copy-start.6 = (bf16[1024,256]{1,0:T(8,128)(2,1)S(1)}, bf16[1024,256]{1,0:T(8,128)(2,1)}, u32[]{:S(2)}) copy-start(bf16[1024,256]{1,0:T(8,128)(2,1)} %copy-done.5) | copy-start | bytes 1572868
  79.6 85.4 %all-gather.5.cloned.1.call-start = ((), (), s32[]{:S(2)}) async-start(), calls=%async_computation.2 | async-start | bytes 2228224 | tf_op jit(solution)/shard_map/all_gather | solution.py:142
  79.7 4.7 %copy-start.14 = (bf16[1024,256]{1,0:T(8,128)(2,1)S(1)}, bf16[1024,256]{1,0:T(8,128)(2,1)}, u32[]{:S(2)}) copy-start(bf16[1024,256]{1,0:T(8,128)(2,1)} %copy-done.13) | copy-start | bytes 1572868
  82.0 29.2 %collective-permute-start.3 = (bf16[1024,512]{1,0:T(8,128)(2,1)}, bf16[1024,512]{1,0:T(8,128)(2,1)}, u32[]{:S(2)}, u32[]{:S(2)}) collective-permute-start(bf16[1024,512]{1,0:T(8,128)(2,1)} %collective-permute-done.2), channel_id=1, source_target_pairs={{0,8},{8,0},{1,9},{9,1},{64,72},{72,64},{65,73},{73,65},{2,10},{10... | collective-permute-start | bytes 3145736 | tf_op jit(solution)/shard_map/ppermute | solution.py:51
  87.5 2.3 %copy-start.19 = (s32[16]{0:T(128)S(1)}, s32[16]{0:T(128)}, u32[]{:S(2)}) copy-start(s32[16]{0:T(128)} %param.15) | copy-start | bytes 196
  87.5 2.8 %copy-start.16 = (f32[2,4,32,256]{3,2,1,0:T(8,128)S(1)}, f32[2,4,32,256]{3,2,1,0:T(8,128)}, u32[]{:S(2)}) copy-start(f32[2,4,32,256]{3,2,1,0:T(8,128)} %param.20) | copy-start | bytes 786436
  92.4 117.5 %all-gather.3.cloned.1.call-start = ((), (), s32[]{:S(2)}) async-start(), calls=%async_computation.1 | async-start | bytes 4456448 | tf_op jit(solution)/shard_map/all_gather | solution.py:196
  93.5 15.0 %collective-permute-start.9 = (bf16[1024,256]{1,0:T(8,128)(2,1)S(1)}, bf16[1024,256]{1,0:T(8,128)(2,1)S(1)}, u32[]{:S(2)}, u32[]{:S(2)}) collective-permute-start(bf16[1024,256]{1,0:T(8,128)(2,1)S(1)} %slice.26), channel_id=1, source_target_pairs={{0,2},{8,10},{1,3},{9,11},{64,66},{72,74},{65,67},{73,75},{2,4},{1... | collective-permute-start | bytes 1572872 | tf_op jit(solution)/shard_map/ppermute | solution.py:51
  98.1 3.3 %copy-start.11 = (bf16[2048,512]{1,0:T(8,128)(2,1)S(1)}, bf16[2048,512]{1,0:T(8,128)(2,1)}, u32[]{:S(2)}) copy-start(bf16[2048,512]{1,0:T(8,128)(2,1)} %constant_dynamic-update-slice_fusion) | copy-start | bytes 6291460
  98.1 12.3 %collective-permute-start.10 = (bf16[1024,256]{1,0:T(8,128)(2,1)S(1)}, bf16[1024,256]{1,0:T(8,128)(2,1)S(1)}, u32[]{:S(2)}, u32[]{:S(2)}) collective-permute-start(bf16[1024,256]{1,0:T(8,128)(2,1)S(1)} %slice.27), channel_id=1, source_target_pairs={{0,6},{8,14},{1,7},{9,15},{64,70},{72,78},{65,71},{73,79},{2,0},{1... | collective-permute-start | bytes 1572872 | tf_op jit(solution)/shard_map/ppermute | solution.py:51
  110.5 1.6 copy-start.12
  114.3 15.8 %collective-permute-start.13 = (bf16[256,256]{1,0:T(8,128)(2,1)S(1)}, bf16[256,256]{1,0:T(8,128)(2,1)S(1)}, u32[]{:S(2)}, u32[]{:S(2)}) collective-permute-start(bf16[256,256]{1,0:T(8,128)(2,1)S(1)} %get-tuple-element.57), channel_id=1, source_target_pairs={{0,32},{8,40},{1,33},{9,41},{64,96},{72,104},{65,97},{73,105},{2,3... | collective-permute-start | bytes 393224 | tf_op jit(solution)/shard_map/ppermute | solution.py:51
  118.9 2.1 copy-start.7
  118.9 2.1 copy-start.15
  121.0 1.0 copy-start.10
  122.1 8.0 %copy-start.18 = (s32[4]{0:T(128)S(1)}, s32[4]{0:T(128)}, u32[]{:S(2)}) copy-start(s32[4]{0:T(128)} %constant.259.clone) | copy-start | bytes 52
  122.3 1.1 copy-start.1
  124.5 25.1 %collective-permute-start.8 = (bf16[768,256]{1,0:T(8,128)(2,1)}, bf16[768,256]{1,0:T(8,128)(2,1)}, u32[]{:S(2)}, u32[]{:S(2)}) collective-permute-start(bf16[768,256]{1,0:T(8,128)(2,1)} %get-tuple-element.43), channel_id=1, source_target_pairs={{0,32},{8,40},{1,33},{9,41},{64,96},{72,104},{65,97},{73,105},{2,3... | collective-permute-start | bytes 1179656 | tf_op jit(solution)/shard_map/ppermute | solution.py:51
  124.9 24.6 %collective-permute-start.7 = (bf16[768,256]{1,0:T(8,128)(2,1)}, bf16[768,256]{1,0:T(8,128)(2,1)}, u32[]{:S(2)}, u32[]{:S(2)}) collective-permute-start(bf16[768,256]{1,0:T(8,128)(2,1)} %get-tuple-element.44), channel_id=1, source_target_pairs={{0,48},{8,56},{1,49},{9,57},{64,112},{72,120},{65,113},{73,121},{2... | collective-permute-start | bytes 1179656 | tf_op jit(solution)/shard_map/ppermute | solution.py:51
  127.4 22.1 %collective-permute-start.6 = (bf16[768,256]{1,0:T(8,128)(2,1)S(1)}, bf16[768,256]{1,0:T(8,128)(2,1)}, u32[]{:S(2)}, u32[]{:S(2)}) collective-permute-start(bf16[768,256]{1,0:T(8,128)(2,1)S(1)} %get-tuple-element.42), channel_id=1, source_target_pairs={{0,16},{8,24},{1,17},{9,25},{64,80},{72,88},{65,81},{73,89},{2,18}... | collective-permute-start | bytes 1179656 | tf_op jit(solution)/shard_map/ppermute | solution.py:51
  127.4 18.4 %collective-permute-start.12 = (bf16[256,256]{1,0:T(8,128)(2,1)S(1)}, bf16[256,256]{1,0:T(8,128)(2,1)S(1)}, u32[]{:S(2)}, u32[]{:S(2)}) collective-permute-start(bf16[256,256]{1,0:T(8,128)(2,1)S(1)} %get-tuple-element.58), channel_id=1, source_target_pairs={{0,48},{8,56},{1,49},{9,57},{64,112},{72,120},{65,113},{73,121},{2... | collective-permute-start | bytes 393224 | tf_op jit(solution)/shard_map/ppermute | solution.py:51
  130.1 18.4 %collective-permute-start.11 = (bf16[256,256]{1,0:T(8,128)(2,1)S(1)}, bf16[256,256]{1,0:T(8,128)(2,1)}, u32[]{:S(2)}, u32[]{:S(2)}) collective-permute-start(bf16[256,256]{1,0:T(8,128)(2,1)S(1)} %get-tuple-element.56), channel_id=1, source_target_pairs={{0,16},{8,24},{1,17},{9,25},{64,80},{72,88},{65,81},{73,89},{2,18}... | collective-permute-start | bytes 393224 | tf_op jit(solution)/shard_map/ppermute | solution.py:51
  149.5 12.9 %copy-start.8 = (f32[256,512]{1,0:T(8,128)S(1)}, f32[256,512]{1,0:T(8,128)}, u32[]{:S(2)}) copy-start(f32[256,512]{1,0:T(8,128)} %param.16) | copy-start | bytes 1572868
  149.5 12.9 %copy-start.9 = (f32[256,512]{1,0:T(8,128)S(1)}, f32[256,512]{1,0:T(8,128)}, u32[]{:S(2)}) copy-start(f32[256,512]{1,0:T(8,128)} %param.18) | copy-start | bytes 1572868
  152.0 5.7 %collective-permute-start.15 = (bf16[256,256]{1,0:T(8,128)(2,1)}, bf16[256,256]{1,0:T(8,128)(2,1)S(1)}, u32[]{:S(2)}, u32[]{:S(2)}) collective-permute-start(bf16[256,256]{1,0:T(8,128)(2,1)} %get-tuple-element.54), channel_id=1, source_target_pairs={{0,96},{8,104},{1,112},{9,120},{64,32},{72,40},{65,48},{73,56},{2,... | collective-permute-start | bytes 393224 | tf_op jit(solution)/shard_map/ppermute | solution.py:51
  153.8 6.8 %collective-permute-start.14 = (bf16[256,256]{1,0:T(8,128)(2,1)}, bf16[256,256]{1,0:T(8,128)(2,1)}, u32[]{:S(2)}, u32[]{:S(2)}) collective-permute-start(bf16[256,256]{1,0:T(8,128)(2,1)} %get-tuple-element.55), channel_id=1, source_target_pairs={{0,32},{8,40},{1,48},{9,56},{64,96},{72,104},{65,112},{73,120},{2,... | collective-permute-start | bytes 393224 | tf_op jit(solution)/shard_map/ppermute | solution.py:51
  156.2 5.1 %collective-permute-start.17 = (bf16[256,256]{1,0:T(8,128)(2,1)S(1)}, bf16[256,256]{1,0:T(8,128)(2,1)}, u32[]{:S(2)}, u32[]{:S(2)}) collective-permute-start(bf16[256,256]{1,0:T(8,128)(2,1)S(1)} %get-tuple-element.53), channel_id=1, source_target_pairs={{0,64},{8,72},{1,80},{9,88},{64,0},{72,8},{65,16},{73,24},{2,66},{... | collective-permute-start | bytes 393224 | tf_op jit(solution)/shard_map/ppermute | solution.py:51
  156.2 5.1 %collective-permute-start.16 = (bf16[256,256]{1,0:T(8,128)(2,1)S(1)}, bf16[256,256]{1,0:T(8,128)(2,1)}, u32[]{:S(2)}, u32[]{:S(2)}) collective-permute-start(bf16[256,256]{1,0:T(8,128)(2,1)S(1)} %get-tuple-element.52), channel_id=1, source_target_pairs={{0,0},{8,8},{1,16},{9,24},{64,64},{72,72},{65,80},{73,88},{2,2},{1... | collective-permute-start | bytes 393224 | tf_op jit(solution)/shard_map/ppermute | solution.py:51
  209.9 4.6 %copy-start.4 = (bf16[2,4,512,256]{3,2,1,0:T(8,128)(2,1)S(1)}, bf16[2,4,512,256]{3,2,1,0:T(8,128)(2,1)}, u32[]{:S(2)}) copy-start(bf16[2,4,512,256]{3,2,1,0:T(8,128)(2,1)} %all-gather.5.cloned.1.call-done) | copy-start | bytes 6291460
Sparse Core Ops, SparseCore 0:
  92.5 36.3 all-gather.4
  165.1 44.7 all-gather.2

commit v2 on v0

v2 whole, which is shorter than its diff:
```python
import functools
import math

import jax
import jax.numpy as jnp
from jax import lax
from jax.experimental import pallas as pl
from jax.experimental.pallas import tpu as pltpu
from jax.sharding import PartitionSpec as P

beta_first = 0.9
beta_second = 0.95
adam_eps = 1e-08
learn_rate = 0.1
decay_rate = 0.1

AXES = ("fsdp", "tp")
X, Y, ZL, ZH, CORE, REGION = range(6)
F32 = jnp.float32
BF16 = jnp.bfloat16


def contract_rows(left, right):
    return lax.dot_general(
        left, right, (((0,), (0,)), ((), ())), preferred_element_type=jnp.float32
    )


def device_number(x, y, zl, zh, c):
    return (zl * 8 + x * 2 + c) * 8 + (y * 2 + zh)


def move(array, where):
    pairs = []
    for x in range(4):
        for y in range(4):
            for zl in range(2):
                for zh in range(2):
                    for c in range(2):
                        a, b, d, e, g = where(x, y, zl, zh, c)
                        pairs.append(
                            (device_number(x, y, zl, zh, c), device_number(a % 4, b % 4, d, e, g))
                        )
    return lax.ppermute(array, AXES, pairs)


def along_x(k):
    return lambda x, y, zl, zh, c: (x + k, y, zl, zh, c)


def along_y(k):
    return lambda x, y, zl, zh, c: (x, y + k, zl, zh, c)


def other_core(x, y, zl, zh, c):
    return (x, y, zl, zh, 1 - c)


def other_zl(x, y, zl, zh, c):
    return (x, y, 1 - zl, zh, c)


def other_zh(x, y, zl, zh, c):
    return (x, y, zl, 1 - zh, c)


def to_owner(ka, kb):
    return lambda x, y, zl, zh, c: (2 * ((x & 1) ^ ka) + zh, y, zl ^ kb, x >> 1, c)


def all_x(array):
    groups = [[z * 8 + x * 2 + c for x in range(4)] for z in range(2) for c in range(2)]
    return lax.all_to_all(array, "fsdp", 0, 0, axis_index_groups=groups)


def all_y(array):
    groups = [[y * 2 + z for y in range(4)] for z in range(2)]
    return lax.all_to_all(array, "tp", 0, 0, axis_index_groups=groups)


def partials_kernel(counts, scale, where, *refs):
    acts, cots, (keep, give) = refs[: sum(counts)], refs[-4:-2], refs[-2:]
    zh, c = where[ZH], where[CORE]
    wide = keep.shape[2]
    for side in range(2):
        place = 2 * (side ^ zh)
        first = 0
        for d, count in enumerate(counts):
            total, row = None, 0
            for ref in acts[first : first + count]:
                term = contract_rows(ref[...], cots[side][pl.ds(row, ref.shape[0]), :])
                total = term if total is None else total + term
                row += ref.shape[0]
            first += count
            total = total * scale
            rows = pl.ds(d * wide, wide)
            for h in range(2):
                part = total[h * wide : (h + 1) * wide]

                @pl.when(c == h)
                def _():
                    keep[place, rows, :] = part[:, :wide].astype(BF16)
                    keep[place + 1, rows, :] = part[:, wide:].astype(BF16)

                @pl.when(c != h)
                def _():
                    give[place, rows, :] = part[:, :wide].astype(BF16)
                    give[place + 1, rows, :] = part[:, wide:].astype(BF16)


def partials(here, acts, cots, scale):
    counts = [len(parts) for parts in acts]
    flat = [part for parts in acts for part in parts]
    wide = flat[0].shape[1] // 2
    shape = (4, len(counts) * wide, wide)
    return pl.pallas_call(
        functools.partial(partials_kernel, counts, scale),
        out_shape=(jax.ShapeDtypeStruct(shape, BF16),) * 2,
        in_specs=[pl.BlockSpec(memory_space=pltpu.SMEM)]
        + [pl.BlockSpec(memory_space=pltpu.VMEM)] * (len(flat) + 2),
        out_specs=(pl.BlockSpec(memory_space=pltpu.VMEM), pl.BlockSpec(memory_space=pltpu.VMEM)),
        compiler_params=pltpu.CompilerParams(vmem_limit_bytes=48 * 1024 * 1024),
    )(here, *flat, *cots)


def low_kernel(scales, where, act, cot, adapters, keep, give):
    rows, rank = keep.shape[0], adapters.shape[3]
    for h in range(2):
        part = pl.ds(h * rows, rows)
        down = jnp.dot(act[part, :], adapters[0, 0], preferred_element_type=F32) * scales[0]
        up = jnp.dot(cot[part, :], adapters[1, 0], preferred_element_type=F32) * scales[1]

        @pl.when(where[ZH] == h)
        def _():
            keep[:, :rank] = down
            keep[:, rank:] = up

        @pl.when(where[ZH] != h)
        def _():
            give[:, :rank] = down.astype(BF16)
            give[:, rank:] = up.astype(BF16)


def low_parts(here, act, cot, adapters, scales):
    rows, rank = act.shape[0] // 2, adapters.shape[3]
    whole = pl.BlockSpec(act.shape, lambda i, where: (0, 0))
    out = pl.BlockSpec((rows, 2 * rank), lambda i, where: (0, 0))
    return pl.pallas_call(
        functools.partial(low_kernel, scales),
        out_shape=(
            jax.ShapeDtypeStruct((rows, 2 * rank), F32),
            jax.ShapeDtypeStruct((rows, 2 * rank), BF16),
        ),
        grid_spec=pltpu.PrefetchScalarGridSpec(
            num_scalar_prefetch=1,
            grid=(1,),
            in_specs=[
                whole,
                whole,
                pl.BlockSpec(
                    (2, 1) + adapters.shape[2:], lambda i, where: (0, where[REGION], 0, 0)
                ),
            ],
            out_specs=(out, out),
        ),
        compiler_params=pltpu.CompilerParams(vmem_limit_bytes=32 * 1024 * 1024),
    )(here, act, cot, adapters)


def grads_kernel(scales, where, low_half, low_other, act, cot, out):
    rows, rank = low_half.shape[0], out.shape[3]
    zh = where[ZH]
    mine = pl.ds(pl.multiple_of(zh * rows, rows), rows)
    theirs = pl.ds(pl.multiple_of((1 - zh) * rows, rows), rows)
    for side, source, start in ((0, act, rank), (1, cot, 0)):
        columns = pl.ds(start, rank)
        total = contract_rows(source[mine, :], low_half[:, columns])
        total = total + contract_rows(source[theirs, :], low_other[:, columns])
        total = (total * scales[side]).astype(BF16)
        for f in range(out.shape[0]):
            out[f, side] = total[f * out.shape[2] : (f + 1) * out.shape[2]]


def adapter_grads(here, low_half, low_other, act, cot, scales, count):
    rank = low_half.shape[1] // 2
    vmem = pl.BlockSpec(memory_space=pltpu.VMEM)
    return pl.pallas_call(
        functools.partial(grads_kernel, scales),
        out_shape=jax.ShapeDtypeStruct((count, 2, act.shape[1] // count, rank), BF16),
        in_specs=[pl.BlockSpec(memory_space=pltpu.SMEM)] + [vmem] * 4,
        out_specs=vmem,
        compiler_params=pltpu.CompilerParams(vmem_limit_bytes=32 * 1024 * 1024),
    )(here, low_half, low_other, act, cot)


def adamw_values(param, moment, second, grad, first_fix, second_fix):
    moment_new = beta_first * moment + (1.0 - beta_first) * grad
    second_new = beta_second * second + (1.0 - beta_second) * grad * grad
    ratio = moment_new / first_fix / (jnp.sqrt(second_new / second_fix) + adam_eps)
    return param - learn_rate * (ratio + decay_rate * param), moment_new, second_new


def adapter_kernel(regions, fixes, got, param, moment, second, *outs):
    new_param, new_moment, new_second, rounded = outs
    rows, rank = param.shape[2:]
    for side in range(2):
        totals = [jnp.zeros((rows, rank), F32) for _ in range(param.shape[1])]
        for f in range(got.shape[0]):
            term = got[f, side].astype(F32)
            totals = [
                total + jnp.where(regions[f] == r, 1.0, 0.0) * term
                for r, total in enumerate(totals)
            ]
        for r, total in enumerate(totals):
            p, m, v = adamw_values(
                param[side, r], moment[side, r], second[side, r], total, fixes[0], fixes[1]
            )
            new_param[side, r] = p
            new_moment[side, r] = m
            new_second[side, r] = v
            rounded[pl.ds((side * param.shape[1] + r) * rows, rows), :] = p.astype(BF16)


def adapter_update(regions, fixes, got, param, moment, second):
    vmem = pl.BlockSpec(memory_space=pltpu.VMEM)
    smem = pl.BlockSpec(memory_space=pltpu.SMEM)
    like = jax.ShapeDtypeStruct(param.shape, F32)
    rounded = jax.ShapeDtypeStruct((math.prod(param.shape[:3]), param.shape[3]), BF16)
    return pl.pallas_call(
        adapter_kernel,
        out_shape=(like, like, like, rounded),
        in_specs=[smem, smem] + [vmem] * 4,
        out_specs=(vmem,) * 4,
        compiler_params=pltpu.CompilerParams(vmem_limit_bytes=32 * 1024 * 1024),
    )(regions, fixes, got, param, moment, second)


def pick_kernel(where, near, far, *outs):
    wide = far.shape[1]
    for k, out in enumerate(outs):
        row_y = 2 * (where[ZL] ^ (k % 2)) + ((where[X] & 1) ^ (k // 2))
        away = (row_y - where[Y] + 4) & 3
        place = away ^ (away >> 1)

        @pl.when(place < 3)
        def _():
            rows = pl.ds(pl.multiple_of(jnp.minimum(place, 2) * wide, wide), wide)
            total = near[0, rows, :].astype(F32)
            for q in range(1, 4):
                total = total + near[q, rows, :].astype(F32)
            out[...] = total.astype(BF16)

        @pl.when(place == 3)
        def _():
            total = far[0].astype(F32)
            for q in range(1, 4):
                total = total + far[q].astype(F32)
            out[...] = total.astype(BF16)


def pick_blocks(here, near, far):
    vmem = pl.BlockSpec(memory_space=pltpu.VMEM)
    count = 4
    return pl.pallas_call(
        pick_kernel,
        out_shape=(jax.ShapeDtypeStruct(far.shape[1:], BF16),) * count,
        in_specs=[pl.BlockSpec(memory_space=pltpu.SMEM), vmem, vmem],
        out_specs=(vmem,) * count,
        compiler_params=pltpu.CompilerParams(vmem_limit_bytes=32 * 1024 * 1024),
    )(here, near, far)


def weight_kernel(where, fixes, *refs):
    terms, (param, moment, second, extra), outs = refs[:4], refs[4:8], refs[8:]
    new_param, new_moment, new_second, rounded = outs
    rows, wide = terms[0].shape
    for ka in range(2):
        grad = terms[2 * ka][...].astype(F32) + terms[2 * ka + 1][...].astype(F32)
        for h in range(2):

            @pl.when(((where[X] >> 1) ^ ka) == h)
            def _():
                columns = pl.ds(h * wide, wide)
                p, m, v = adamw_values(
                    param[:, columns], moment[:, columns], second[:, columns], grad,
                    fixes[0], fixes[1],
                )
                new_param[:, columns] = p
                new_moment[:, columns] = m
                new_second[:, columns] = v
                rounded[pl.ds(h * rows, rows), :] = p.astype(BF16)

    rounded[pl.ds(2 * rows, extra.shape[0]), :] = extra[...]


def weight_update(here, fixes, terms, param, moment, second, extra):
    vmem = pl.BlockSpec(memory_space=pltpu.VMEM)
    smem = pl.BlockSpec(memory_space=pltpu.SMEM)
    like = jax.ShapeDtypeStruct(param.shape, F32)
    rounded = jax.ShapeDtypeStruct((2 * param.shape[0] + extra.shape[0], extra.shape[1]), BF16)
    return pl.pallas_call(
        weight_kernel,
        out_shape=(like, like, like, rounded),
        in_specs=[smem, smem] + [vmem] * 8,
        out_specs=(vmem,) * 4,
        compiler_params=pltpu.CompilerParams(vmem_limit_bytes=32 * 1024 * 1024),
    )(here, fixes, *terms, param, moment, second, extra)


def place_kernel(where, first, second, first_peer, second_peer, weight, adapter):
    chip, c = pl.program_id(0), where[CORE]
    dx, dz = (chip - where[X]) & 3, (chip >> 2) ^ where[ZL]
    near_slot = jnp.where(dx == 0, dz, jnp.where(dx == 3, 2, 3))
    far_slot = jnp.where(dx == 3, 5, jnp.where(dx == 1, 6, 7))
    slot = jnp.where(
        dz == 0, jnp.where(dx == 2, 4, near_slot), jnp.where(dx == 0, dz, far_slot)
    )
    rows, wide = weight.shape[1], weight.shape[2] // 2

    def put(core, block):
        weight[core, :, :wide] = block[:rows]
        weight[core, :, wide:] = block[rows : 2 * rows]
        adapter[:, core] = block[2 * rows :].reshape(adapter.shape[0:1] + adapter.shape[2:])

    for here, low, high in ((c, first, second), (1 - c, first_peer, second_peer)):

        @pl.when(slot < 4)
        def _():
            put(here, low[jnp.minimum(slot, 3)])

        @pl.when(slot >= 4)
        def _():
            put(here, high[jnp.maximum(slot - 4, 0)])


def place_blocks(here, arrays, rows, groups):
    wide = arrays[0].shape[2]
    deep = (arrays[0].shape[1] - 2 * rows) // groups
    return pl.pallas_call(
        place_kernel,
        out_shape=(
            jax.ShapeDtypeStruct((16, rows, 2 * wide), BF16),
            jax.ShapeDtypeStruct((groups, 16, deep, wide), BF16),
        ),
        grid_spec=pltpu.PrefetchScalarGridSpec(
            num_scalar_prefetch=1,
            grid=(8,),
            in_specs=[pl.BlockSpec(array.shape, lambda i, where: (0, 0, 0)) for array in arrays],
            out_specs=(
                pl.BlockSpec((2, rows, 2 * wide), lambda i, where: (i, 0, 0)),
                pl.BlockSpec((groups, 2, deep, wide), lambda i, where: (0, i, 0, 0)),
            ),
        ),
        compiler_params=pltpu.CompilerParams(vmem_limit_bytes=40 * 1024 * 1024),
    )(here, *arrays)


def shards(
    activations,
    cotangent,
    step_count,
    region_of,
    weight_master,
    weight_moment,
    weight_second,
    adapter_copy,
    adapter_master,
    adapter_moment,
    adapter_second,
):
    fsdp_count = lax.axis_size("fsdp")
    tp_count = lax.axis_size("tp")
    tok_dev = activations.shape[0]
    width = activations.shape[1] * tp_count
    rank = adapter_copy.shape[3]
    region_count = adapter_copy.shape[1]
    grad_scale = math.sqrt(width / (tok_dev * fsdp_count))
    inv_width = 1.0 / math.sqrt(width)
    inv_rank = 1.0 / math.sqrt(rank)
    f = lax.axis_index("fsdp")
    t = lax.axis_index("tp")
    zl, x, c = f // 8, (f // 2) % 4, f % 2
    y, zh = t // 2, t % 2

    own_region = lax.dynamic_index_in_dim(region_of, f, 0, keepdims=False)
    here = jnp.stack([x, y, zl, zh, c, own_region]).astype(jnp.int32)
    step_float = step_count[0].astype(F32)
    fixes = jnp.stack([
        1.0 - jnp.power(F32(beta_first), step_float),
        1.0 - jnp.power(F32(beta_second), step_float),
    ])

    middle = tok_dev // 2
    half = activations.shape[1] // 2
    act_first, act_second = activations[:middle], activations[middle:]
    back_first = move(act_first, along_y(1))
    ahead_first = move(act_first, along_y(-1))
    cot_zh = move(cotangent, other_zh)
    back_second = move(act_second, along_y(1))
    ahead_second = move(act_second, along_y(-1))
    far_first = move(back_first, along_y(1))
    far_second = move(ahead_second, along_y(-1))

    low_keep, low_give = low_parts(
        here, activations, cotangent, adapter_copy, (inv_width, inv_rank)
    )
    low_give, back_first, ahead_first, cot_zh = lax.optimization_barrier(
        (low_give, back_first, ahead_first, cot_zh)
    )
    low_half = (low_keep + move(low_give, other_zh).astype(F32)).astype(BF16)
    low_half = low_half.reshape(4, tok_dev // 8, 2 * rank)
    low_half, back_second, ahead_second = lax.optimization_barrier(
        (low_half, back_second, ahead_second)
    )
    low_own = jnp.sum(all_y(low_half).astype(F32), axis=0).astype(BF16)
    low_half = all_y(jnp.broadcast_to(low_own[None], low_half.shape))
    low_half = low_half.reshape(tok_dev // 2, 2 * rank)
    low_other = move(low_half, other_zh)
    parts = adapter_grads(
        here, low_half, low_other, activations, cotangent,
        (inv_width * grad_scale, inv_rank * grad_scale), fsdp_count,
    )
    got = lax.all_to_all(parts, "fsdp", 0, 0)
    new_adapter, new_adapter_moment, new_adapter_second, adapter_rows = adapter_update(
        region_of, fixes, got, adapter_master, adapter_moment, adapter_second
    )

    scale = inv_width * grad_scale
    cots = [cotangent, cot_zh]
    near_keep, near_give = partials(
        here, [[activations], [ahead_first, ahead_second], [back_first, back_second]], cots, scale
    )
    far_first, far_second, near_give = lax.optimization_barrier(
        (far_first, far_second, near_give)
    )
    far_keep, far_give = partials(here, [[far_first, far_second]], cots, scale)

    def reduce_x(keep, give):
        both = (keep.astype(F32) + move(give, other_core).astype(F32)).astype(BF16)
        return all_x(both)

    near = reduce_x(near_keep, near_give)
    far = reduce_x(far_keep, far_give)
    blocks = pick_blocks(here, near, far)
    terms = [move(block, to_owner(k // 2, k % 2)) for k, block in enumerate(blocks)]
    new_weight, new_weight_moment, new_weight_second, piece = weight_update(
        here, fixes, terms, weight_master, weight_moment, weight_second, adapter_rows
    )

    from_zl = move(piece, other_zl)
    from_back = move(piece, along_x(1))
    from_ahead = move(piece, along_x(-1))
    from_far = move(piece, along_x(2))
    first = jnp.stack([piece, from_zl, from_back, from_ahead])
    second = jnp.stack([
        from_far,
        move(from_zl, along_x(1)),
        move(from_zl, along_x(-1)),
        move(from_far, other_zl),
    ])

    weight_next, adapter_next = place_blocks(
        here,
        [first, second, move(first, other_core), move(second, other_core)],
        new_weight.shape[0],
        2 * region_count,
    )
    weight_next = weight_next.reshape(width, -1)
    adapter_next = adapter_next.reshape(adapter_copy.shape)
    return (
        new_weight,
        new_weight_moment,
        new_weight_second,
        weight_next,
        new_adapter,
        new_adapter_moment,
        new_adapter_second,
        adapter_next,
    )


def solution(mesh):
    return jax.shard_map(
        shards,
        mesh=mesh,
        in_specs=(
            P("fsdp", "tp"),
            P("fsdp", "tp"),
            P(),
            P(),
            P("fsdp", "tp"),
            P("fsdp", "tp"),
            P("fsdp", "tp"),
            P(None, None, "tp", None),
            P(None, None, ("tp", "fsdp"), None),
            P(None, None, ("tp", "fsdp"), None),
            P(None, None, ("tp", "fsdp"), None),
        ),
        out_specs=(
            P("fsdp", "tp"),
            P("fsdp", "tp"),
            P("fsdp", "tp"),
            P(None, "tp"),
            P(None, None, ("tp", "fsdp"), None),
            P(None, None, ("tp", "fsdp"), None),
            P(None, None, ("tp", "fsdp"), None),
            P(None, None, "tp", None),
        ),
        check_vma=False,
    )
```

time: 383 us -> 190 us (0.50)
  waiting for transfers between devices: 208 us -> 62.3 us
  blocking collectives: 119 us -> 11.4 us
  starting transfers between devices: 0.21 us -> 75.3 us
  Pallas kernels: 0 us -> 25.9 us
  matrix products: 19.2 us -> 0 us
  between operations: 18.5 us -> 1.54 us
  other arithmetic: 10.6 us -> 6.06 us
    all_gather x3 -> x0, waiting for transfers between devices: 123 us -> none  [the longest x1 46.4 us: shards(): full_acts = lax.all_gather(activations, 'tp', axis=1, tiled=True)]
    psum x1 -> x0, blocking collectives: 119 us -> none  [shards(): low_down, low_up = lax.psum((down_part, up_part), 'tp')]
    reduce_scatter x2 -> x0, waiting for transfers between devices: 84.5 us -> none  [the longest x1 73 us: shards(): lax.psum_scatter(contract_rows(full_acts, cotangent) * (inv_width * grad_...]
    ppermute x0 -> x24, starting transfers between devices: none -> 54.5 us  [move(): return lax.ppermute(array, AXES, pairs)]
    ppermute x0 -> x24, waiting for transfers between devices: none -> 50 us  [move(): return lax.ppermute(array, AXES, pairs)]
    pallas_call x0 -> x8, Pallas kernels: none -> 25.9 us  [the longest x2 10.8 us: partials(): pl.pallas_call(functools.partial(partials_kernel, counts, scale), out_sha...]
    all_to_all x0 -> x4, starting transfers between devices: none -> 20.9 us  [the longest x1 9.03 us: shards(): got = lax.all_to_all(parts, 'fsdp', 0, 0)]
    dot_general x5 -> x0, matrix products: 19.2 us -> none  [the longest x3 13.8 us: contract_rows(): lax.dot_general(left, right, (((0,), (0,)), ((), ())), preferred_element_...]
  transfers between devices with their start and end apart: 5 -> 28, of which waited for: 5 -> 14; matrix products, arithmetic and copies ran while one was open for 8% -> 6% of each run, Pallas kernels for 0% -> 10%
where the time goes in v2:
time: 190 us; the launch traced here: 189 us
  starting transfers between devices  75.3 us (40%)
  waiting for transfers between devices  62.3 us (33%)
  Pallas kernels  25.9 us (14%)
  blocking collectives  11.4 us (6%)
  local copies, waits for them, and re-layouts  6.8 us (4%)
  other arithmetic  6.06 us (3%)
    ppermute x24, starting transfers between devices, move(): return lax.ppermute(array, AXES, pairs)  54.5 us
    ppermute x24, waiting for transfers between devices, move(): return lax.ppermute(array, AXES, pairs)  50 us
    all_to_all x1, blocking collectives, all_y(): return lax.all_to_all(array, 'tp', 0, 0, axis_index_groups=groups)  11.4 us
    pallas_call x2, Pallas kernels, partials(): pl.pallas_call(functools.partial(partials_kernel, counts, scale), out_sha...  10.8 us
    all_to_all x1, starting transfers between devices, shards(): got = lax.all_to_all(parts, 'fsdp', 0, 0)  9.03 us
    all_to_all x2, starting transfers between devices, all_x(): return lax.all_to_all(array, 'fsdp', 0, 0, axis_index_groups=groups)  8.35 us
    all_to_all x2, waiting for transfers between devices, all_x(): return lax.all_to_all(array, 'fsdp', 0, 0, axis_index_groups=groups)  6.94 us
    all_to_all x1, waiting for transfers between devices, all_y(): return lax.all_to_all(array, 'tp', 0, 0, axis_index_groups=groups)  5.4 us
  transfers between devices with their start and end apart: 28, of which 14 were waited for; matrix products, arithmetic and copies ran while one was open for 6% of the time, Pallas kernels for 10%

profile of v2, /device:TPU:1, one launch (start us, length us, event | category | flops | bytes accessed | tf_op | source)
XLA Modules:
  0.0 189.3 jit_solution(743901132211563281)
XLA Ops:
  0.7 4.5 %collective-permute-start.2 = (bf16[1024,512]{1,0:T(8,128)(2,1)}, bf16[1024,512]{1,0:T(8,128)(2,1)S(1)}, u32[]{:S(2)}, u32[]{:S(2)}) collective-permute-start(bf16[1024,512]{1,0:T(8,128)(2,1)} %cot.3), channel_id=1, source_target_pairs={{0,1},{8,9},{1,0},{9,8},{64,65},{72,73},{65,64},{73,72},{2,3},{10,... | collective-permute-start | bytes 3145736 | tf_op jit(solution)/shard_map/ppermute | solution.py:44
  5.2 2.2 %fusion = (bf16[512,512]{1,0:T(8,128)(2,1)}, bf16[512,512]{1,0:T(8,128)(2,1)}) fusion(bf16[1024,512]{1,0:T(8,128)(2,1)} %act.3), kind=kLoop, calls=%fused_computation.6 | loop fusion | bytes 2097152 | tf_op jit(solution)/shard_map/slice | solution.py:395
  7.4 2.7 %collective-permute-start.1 = (bf16[512,512]{1,0:T(8,128)(2,1)}, bf16[512,512]{1,0:T(8,128)(2,1)}, u32[]{:S(2)}, u32[]{:S(2)}) collective-permute-start(bf16[512,512]{1,0:T(8,128)(2,1)} %get-tuple-element.69), channel_id=1, source_target_pairs={{0,6},{8,14},{1,7},{9,15},{64,70},{72,78},{65,71},{73,79},{2,0},{1... | collective-permute-start | bytes 1572872 | tf_op jit(solution)/shard_map/ppermute | solution.py:44
  10.1 2.7 %collective-permute-start.5 = (bf16[512,512]{1,0:T(8,128)(2,1)}, bf16[512,512]{1,0:T(8,128)(2,1)}, u32[]{:S(2)}, u32[]{:S(2)}) collective-permute-start(bf16[512,512]{1,0:T(8,128)(2,1)} %get-tuple-element.68), channel_id=1, source_target_pairs={{0,6},{8,14},{1,7},{9,15},{64,70},{72,78},{65,71},{73,79},{2,0},{1... | collective-permute-start | bytes 1572872 | tf_op jit(solution)/shard_map/ppermute | solution.py:44
  12.8 0.6 dynamic_slice.4
  13.4 0.7 stack.59.where
  14.1 0.0 copy-start.2
  14.1 1.6 copy-done.2
  15.7 1.6 shard_map.170
  17.3 3.4 %collective-permute-done.1.refs_1_ = bf16[512,512]{1,0:T(8,128)(2,1)} collective-permute-done((bf16[512,512]{1,0:T(8,128)(2,1)}, bf16[512,512]{1,0:T(8,128)(2,1)}, u32[]{:S(2)}, u32[]{:S(2)}) %collective-permute-start.1) | collective-permute-done | bytes 524320 | tf_op jit(solution)/shard_map/ppermute | solution.py:44
  20.7 3.1 %collective-permute-done.refs_3_ = bf16[512,512]{1,0:T(8,128)(2,1)} collective-permute-done((bf16[512,512]{1,0:T(8,128)(2,1)}, bf16[512,512]{1,0:T(8,128)(2,1)}, u32[]{:S(2)}, u32[]{:S(2)}) %collective-permute-start) | collective-permute-done | bytes 524320 | tf_op jit(solution)/shard_map/ppermute | solution.py:44
  23.8 4.4 %collective-permute-done.2.refs_6_.refs_3_ = bf16[1024,512]{1,0:T(8,128)(2,1)S(1)} collective-permute-done((bf16[1024,512]{1,0:T(8,128)(2,1)}, bf16[1024,512]{1,0:T(8,128)(2,1)S(1)}, u32[]{:S(2)}, u32[]{:S(2)}) %collective-permute-start.2) | collective-permute-done | bytes 1048608 | tf_op jit(solution)/shard_map/ppermute | solution.py:44
  28.3 2.6 %collective-permute-start.3 = (bf16[512,512]{1,0:T(8,128)(2,1)S(1)}, bf16[512,512]{1,0:T(8,128)(2,1)S(1)}, u32[]{:S(2)}, u32[]{:S(2)}) collective-permute-start(bf16[512,512]{1,0:T(8,128)(2,1)S(1)} %get-tuple-element.41), channel_id=1, source_target_pairs={{0,1},{8,9},{1,0},{9,8},{64,65},{72,73},{65,64},{73,72},{2,3},{10,... | collective-permute-start | bytes 1572872 | tf_op jit(solution)/shard_map/ppermute | solution.py:44
  30.9 1.3 collective-permute-start.4
  32.2 3.2 %collective-permute-start.7 = (bf16[512,512]{1,0:T(8,128)(2,1)}, bf16[512,512]{1,0:T(8,128)(2,1)S(1)}, u32[]{:S(2)}, u32[]{:S(2)}) collective-permute-start(bf16[512,512]{1,0:T(8,128)(2,1)} %collective-permute-done.5.refs_2_), channel_id=1, source_target_pairs={{0,6},{8,14},{1,7},{9,15},{64,70},{72,78},{65,71},{73,79},{2,0},{1... | collective-permute-start | bytes 1572872 | tf_op jit(solution)/shard_map/ppermute | solution.py:44
  35.4 6.6 %collective-permute-done.3 = bf16[512,512]{1,0:T(8,128)(2,1)S(1)} collective-permute-done((bf16[512,512]{1,0:T(8,128)(2,1)S(1)}, bf16[512,512]{1,0:T(8,128)(2,1)S(1)}, u32[]{:S(2)}, u32[]{:S(2)}) %collective-permute-start.3) | collective-permute-done | bytes 524320 | tf_op jit(solution)/shard_map/ppermute | solution.py:44
  42.0 0.2 add_convert_fusion.2
  42.1 2.1 %collective-permute-done.4.refs_4_ = bf16[512,512]{1,0:T(8,128)(2,1)S(1)} collective-permute-done((bf16[512,512]{1,0:T(8,128)(2,1)}, bf16[512,512]{1,0:T(8,128)(2,1)S(1)}, u32[]{:S(2)}, u32[]{:S(2)}) %collective-permute-start.4) | collective-permute-done | bytes 524320 | tf_op jit(solution)/shard_map/ppermute | solution.py:44
  44.3 7.8 %shard_map.171 = (bf16[4,768,256]{2,1,0:T(8,128)(2,1)}, bf16[4,768,256]{2,1,0:T(8,128)(2,1)}) custom-call(s32[6]{0:T(128)S(1)} %stack.59.where, bf16[1024,512]{1,0:T(8,128)(2,1)S(1)} %copy-done, bf16[512,512]{1,0:T(8,128)(2,1)} %collective-permute-done.1.refs_1_, bf16[512,512]{1,0:T(8,128)(2,1)} %collective-permute-done.5.refs_2_, ...), custom_call_target="tpu_custom_call" | custom-call | tf_op jit(solution)/shard_map/pallas_call | solution.py:116
  52.1 3.4 %collective-permute-done.6.refs_0_ = bf16[512,512]{1,0:T(8,128)(2,1)S(1)} collective-permute-done((bf16[512,512]{1,0:T(8,128)(2,1)}, bf16[512,512]{1,0:T(8,128)(2,1)S(1)}, u32[]{:S(2)}, u32[]{:S(2)}) %collective-permute-start.6) | collective-permute-done | bytes 524320 | tf_op jit(solution)/shard_map/ppermute | solution.py:44
  55.5 2.6 %collective-permute-start.8 = (bf16[4,768,256]{2,1,0:T(8,128)(2,1)}, bf16[4,768,256]{2,1,0:T(8,128)(2,1)}, u32[]{:S(2)}, u32[]{:S(2)}) collective-permute-start(bf16[4,768,256]{2,1,0:T(8,128)(2,1)} %get-tuple-element.48), channel_id=1, source_target_pairs={{0,8},{8,0},{1,9},{9,1},{64,72},{72,64},{65,73},{73,65},{2,10},{10... | collective-permute-start | bytes 4718600 | tf_op jit(solution)/shard_map/ppermute | solution.py:44
  58.1 3.0 %shard_map.172 = (bf16[4,256,256]{2,1,0:T(8,128)(2,1)S(1)}, bf16[4,256,256]{2,1,0:T(8,128)(2,1)}) custom-call(s32[6]{0:T(128)S(1)} %stack.59.where, bf16[512,512]{1,0:T(8,128)(2,1)S(1)} %collective-permute-done.6.refs_0_, bf16[512,512]{1,0:T(8,128)(2,1)S(1)} %collective-permute-done.7.refs_1_, bf16[1024,512]{1,0:T(8,128)(2,1)S(1)} %copy-done.1, ...), custom_call_target="tpu_custom_call" | custom-call | tf_op jit(solution)/shard_map/pallas_call | solution.py:116
  61.0 0.8 copy-done.3
  61.8 0.0 collective-permute-start.9
  61.8 11.4 %all_to_all.25 = bf16[4,128,512]{2,1,0:T(8,128)(2,1)S(1)} all-to-all(bf16[4,128,512]{2,1,0:T(8,128)(2,1)S(1)} %bitcast.20), channel_id=1, replica_groups={{0,2,4,6},{1,3,5,7},{8,10,12,14},{9,11,13,15},{16,18,20,22},{17,19,21,2..., dimensions={0} | all-to-all | bytes 1048576 | tf_op jit(solution)/shard_map/all_to_all | solution.py:78
  73.2 0.1 reduce_sum.12
  73.3 0.8 broadcast_in_dim.2
  74.1 3.5 %all-to-all-start.3 = ((bf16[4,128,512]{2,1,0:T(8,128)(2,1)}), bf16[4,128,512]{2,1,0:T(8,128)(2,1)S(1)}, u32[]{:S(2)}, u32[]{:S(2)}) async-start(bf16[4,128,512]{2,1,0:T(8,128)(2,1)} %broadcast_in_dim.2), calls=%async_computation.3 | async-start | bytes 1048576 | tf_op jit(solution)/shard_map/all_to_all | solution.py:78
  77.6 2.0 %add_convert_fusion.1 = bf16[4,256,256]{2,1,0:T(8,128)(2,1)} fusion(bf16[4,256,256]{2,1,0:T(8,128)(2,1)} %collective-permute-done.9, bf16[4,256,256]{2,1,0:T(8,128)(2,1)S(1)} %copy-done.4), kind=kLoop, calls=%fused_computation.3 | loop fusion | flops 1048576 | bytes 1572864 | tf_op jit(solution)/shard_map/convert_element_type | solution.py:439
  79.6 5.4 %all-to-all-done.3 = bf16[4,128,512]{2,1,0:T(8,128)(2,1)S(1)} async-done(((bf16[4,128,512]{2,1,0:T(8,128)(2,1)}), bf16[4,128,512]{2,1,0:T(8,128)(2,1)S(1)}, u32[]{:S(2)}, u32[]{:S(2)}) %all-to-all-start.3) | async-done | bytes 524320 | tf_op jit(solution)/shard_map/all_to_all | solution.py:78
  85.0 4.0 %all-to-all-start.1 = ((bf16[4,256,256]{2,1,0:T(8,128)(2,1)}), bf16[4,256,256]{2,1,0:T(8,128)(2,1)S(1)}, u32[]{:S(2)}, u32[]{:S(2)}) async-start(bf16[4,256,256]{2,1,0:T(8,128)(2,1)} %add_convert_fusion.1), calls=%async_computation.1 | async-start | bytes 1048576 | tf_op jit(solution)/shard_map/all_to_all | solution.py:73
  89.0 3.4 %add_convert_fusion = bf16[4,768,256]{2,1,0:T(8,128)(2,1)} fusion(bf16[4,768,256]{2,1,0:T(8,128)(2,1)} %collective-permute-done.8, bf16[4,768,256]{2,1,0:T(8,128)(2,1)} %get-tuple-element.46), kind=kLoop, calls=%fused_computation | loop fusion | flops 3145728 | bytes 4718592 | tf_op jit(solution)/shard_map/convert_element_type | solution.py:439
  92.4 3.5 %all-to-all-done.1.far = bf16[4,256,256]{2,1,0:T(8,128)(2,1)S(1)} async-done(((bf16[4,256,256]{2,1,0:T(8,128)(2,1)}), bf16[4,256,256]{2,1,0:T(8,128)(2,1)S(1)}, u32[]{:S(2)}, u32[]{:S(2)}) %all-to-all-start.1) | async-done | bytes 524320 | tf_op jit(solution)/shard_map/all_to_all | solution.py:73
  95.9 4.3 %all-to-all-start = ((bf16[4,768,256]{2,1,0:T(8,128)(2,1)}), bf16[4,768,256]{2,1,0:T(8,128)(2,1)}, u32[]{:S(2)}, u32[]{:S(2)}) async-start(bf16[4,768,256]{2,1,0:T(8,128)(2,1)} %add_convert_fusion), calls=%async_computation | async-start | bytes 3145728 | tf_op jit(solution)/shard_map/all_to_all | solution.py:73
  100.3 0.4 collective-permute-start.14
  100.7 10.1 %collective-permute-done.14.low_other = bf16[512,512]{1,0:T(8,128)(2,1)S(1)} collective-permute-done((bf16[512,512]{1,0:T(8,128)(2,1)S(1)}, bf16[512,512]{1,0:T(8,128)(2,1)S(1)}, u32[]{:S(2)}, u32[]{:S(2)}) %collective-permute-start.14) | collective-permute-done | bytes 524320 | tf_op jit(solution)/shard_map/ppermute | solution.py:44
  110.8 2.1 %shard_map.174 = bf16[16,2,32,256]{3,2,1,0:T(8,128)(2,1)} custom-call(s32[6]{0:T(128)S(1)} %stack.59.where, bf16[512,512]{1,0:T(8,128)(2,1)S(1)} %bitcast.18, bf16[512,512]{1,0:T(8,128)(2,1)S(1)} %collective-permute-done.14.low_other, bf16[1024,512]{1,0:T(8,128)(2,1)S(1)} %copy-done, bf16[1024,512]{1,0:T(8,128)(2,1)S(1)} %copy-done.1), custom_call_target="tpu_custom_call" | custom-call | tf_op jit(solution)/shard_map/pallas_call | solution.py:187
  112.9 3.4 %all-to-all-done.near = bf16[4,768,256]{2,1,0:T(8,128)(2,1)} async-done(((bf16[4,768,256]{2,1,0:T(8,128)(2,1)}), bf16[4,768,256]{2,1,0:T(8,128)(2,1)}, u32[]{:S(2)}, u32[]{:S(2)}) %all-to-all-start) | async-done | bytes 1572896 | tf_op jit(solution)/shard_map/all_to_all | solution.py:73
  116.3 9.0 %all-to-all-start.4 = ((bf16[16,2,32,256]{3,2,1,0:T(8,128)(2,1)}), bf16[16,2,32,256]{3,2,1,0:T(8,128)(2,1)S(1)}, u32[]{:S(2)}, u32[]{:S(2)}) async-start(bf16[16,2,32,256]{3,2,1,0:T(8,128)(2,1)} %shard_map.174), calls=%async_computation.4 | async-start | bytes 1048576 | tf_op jit(solution)/shard_map/all_to_all | solution.py:423
  125.3 0.0 copy-start.6
  125.4 0.0 copy-start.7
  125.4 2.8 %shard_map.173 = (bf16[256,256]{1,0:T(8,128)(2,1)}, bf16[256,256]{1,0:T(8,128)(2,1)}, bf16[256,256]{1,0:T(8,128)(2,1)}, bf16[256,256]{1,0:T(8,128)(2,1)S(1)}) custom-call(s32[6]{0:T(128)S(1)} %stack.59.where, bf16[4,768,256]{2,1,0:T(8,128)(2,1)} %all-to-all-done.near, bf16[4,256,256]{2,1,0:T(8,128)(2,1)S(1)} %all-to-all-done.1.far), custom_call_target="tpu_custom_call" | custom-call | tf_op jit(solution)/shard_map/pallas_call | solution.py:264
  128.2 1.6 collective-permute-start.10
  129.7 1.4 collective-permute-start.11
  131.1 6.4 %collective-permute-start.12 = (bf16[256,256]{1,0:T(8,128)(2,1)}, bf16[256,256]{1,0:T(8,128)(2,1)S(1)}, u32[]{:S(2)}, u32[]{:S(2)}) collective-permute-start(bf16[256,256]{1,0:T(8,128)(2,1)} %get-tuple-element.55), channel_id=1, source_target_pairs={{0,32},{8,40},{1,48},{9,56},{64,96},{72,104},{65,112},{73,120},{2,... | collective-permute-start | bytes 393224 | tf_op jit(solution)/shard_map/ppermute | solution.py:44
  137.6 0.6 collective-permute-start.13
  138.8 0.1 pad_maximum_fusion.2.fixes
  138.9 1.9 %shard_map.175 = (f32[2,4,32,256]{3,2,1,0:T(8,128)}, f32[2,4,32,256]{3,2,1,0:T(8,128)}, f32[2,4,32,256]{3,2,1,0:T(8,128)}, bf16[256,256]{1,0:T(8,128)(2,1)S(1)}) custom-call(s32[16]{0:T(128)S(1)} %copy-done.11, f32[2]{0:T(128)S(1)} %pad_maximum_fusion.2.fixes, bf16[16,2,32,256]{3,2,1,0:T(8,128)(2,1)S(1)} %all-to-all-done.4.got, ...), custom_call_target="tpu_custom_call" | custom-call | tf_op jit(solution)/shard_map/pallas_call | solution.py:229
  140.9 2.1 %collective-permute-done.13.refs_3_ = bf16[256,256]{1,0:T(8,128)(2,1)S(1)} collective-permute-done((bf16[256,256]{1,0:T(8,128)(2,1)S(1)}, bf16[256,256]{1,0:T(8,128)(2,1)S(1)}, u32[]{:S(2)}, u32[]{:S(2)}) %collective-permute-start.13) | collective-permute-done | bytes 131104 | tf_op jit(solution)/shard_map/ppermute | solution.py:44
  143.0 2.2 %shard_map.176 = (f32[256,512]{1,0:T(8,128)}, f32[256,512]{1,0:T(8,128)}, f32[256,512]{1,0:T(8,128)}, bf16[768,256]{1,0:T(8,128)(2,1)S(1)}) custom-call(s32[6]{0:T(128)S(1)} %stack.59.where, f32[2]{0:T(128)S(1)} %pad_maximum_fusion.2.fixes, bf16[256,256]{1,0:T(8,128)(2,1)S(1)} %collective-permute-done.10.refs_0_, ...), custom_call_target="tpu_custom_call" | custom-call | tf_op jit(solution)/shard_map/pallas_call | solution.py:301
  145.2 3.2 %collective-permute-start.18 = (bf16[768,256]{1,0:T(8,128)(2,1)S(1)}, bf16[768,256]{1,0:T(8,128)(2,1)S(1)}, u32[]{:S(2)}, u32[]{:S(2)}) collective-permute-start(bf16[768,256]{1,0:T(8,128)(2,1)S(1)} %get-tuple-element.62), channel_id=1, source_target_pairs={{0,32},{8,40},{1,33},{9,41},{64,96},{72,104},{65,97},{73,105},{2,3... | collective-permute-start | bytes 1179656 | tf_op jit(solution)/shard_map/ppermute | solution.py:44
  148.3 2.5 %collective-permute-start.15 = (bf16[768,256]{1,0:T(8,128)(2,1)S(1)}, bf16[768,256]{1,0:T(8,128)(2,1)S(1)}, u32[]{:S(2)}, u32[]{:S(2)}) collective-permute-start(bf16[768,256]{1,0:T(8,128)(2,1)S(1)} %get-tuple-element.62), channel_id=1, source_target_pairs={{0,64},{8,72},{1,65},{9,73},{64,0},{72,8},{65,1},{73,9},{2,66},{10... | collective-permute-start | bytes 1179656 | tf_op jit(solution)/shard_map/ppermute | solution.py:44
  150.8 3.2 %collective-permute-start.17 = (bf16[768,256]{1,0:T(8,128)(2,1)S(1)}, bf16[768,256]{1,0:T(8,128)(2,1)S(1)}, u32[]{:S(2)}, u32[]{:S(2)}) collective-permute-start(bf16[768,256]{1,0:T(8,128)(2,1)S(1)} %get-tuple-element.62), channel_id=1, source_target_pairs={{0,48},{8,56},{1,49},{9,57},{64,112},{72,120},{65,113},{73,121},{2... | collective-permute-start | bytes 1179656 | tf_op jit(solution)/shard_map/ppermute | solution.py:44
  154.0 0.5 collective-permute-start.16
  154.5 5.5 %collective-permute-start.21 = (bf16[768,256]{1,0:T(8,128)(2,1)S(1)}, bf16[768,256]{1,0:T(8,128)(2,1)S(1)}, u32[]{:S(2)}, u32[]{:S(2)}) collective-permute-start(bf16[768,256]{1,0:T(8,128)(2,1)S(1)} %collective-permute-done.18), channel_id=1, source_target_pairs={{0,64},{8,72},{1,65},{9,73},{64,0},{72,8},{65,1},{73,9},{2,66},{10... | collective-permute-start | bytes 1179656 | tf_op jit(solution)/shard_map/ppermute | solution.py:44
  160.0 5.5 %collective-permute-start.20 = (bf16[768,256]{1,0:T(8,128)(2,1)S(1)}, bf16[768,256]{1,0:T(8,128)(2,1)S(1)}, u32[]{:S(2)}, u32[]{:S(2)}) collective-permute-start(bf16[768,256]{1,0:T(8,128)(2,1)S(1)} %collective-permute-done.15), channel_id=1, source_target_pairs={{0,48},{8,56},{1,49},{9,57},{64,112},{72,120},{65,113},{73,121},{2... | collective-permute-start | bytes 1179656 | tf_op jit(solution)/shard_map/ppermute | solution.py:44
  165.5 6.0 %collective-permute-done.17 = bf16[768,256]{1,0:T(8,128)(2,1)S(1)} collective-permute-done((bf16[768,256]{1,0:T(8,128)(2,1)S(1)}, bf16[768,256]{1,0:T(8,128)(2,1)S(1)}, u32[]{:S(2)}, u32[]{:S(2)}) %collective-permute-start.17) | collective-permute-done | bytes 393248 | tf_op jit(solution)/shard_map/ppermute | solution.py:44
  171.6 0.2 pad_maximum_fusion.first
  171.8 2.6 %collective-permute-start.22 = (bf16[4,768,256]{2,1,0:T(8,128)(2,1)S(1)}, bf16[4,768,256]{2,1,0:T(8,128)(2,1)S(1)}, u32[]{:S(2)}, u32[]{:S(2)}) collective-permute-start(bf16[4,768,256]{2,1,0:T(8,128)(2,1)S(1)} %pad_maximum_fusion.first), channel_id=1, source_target_pairs={{0,8},{8,0},{1,9},{9,1},{64,72},{72,64},{65,73},{73,65},{2,10},{10... | collective-permute-start | bytes 4718600 | tf_op jit(solution)/shard_map/ppermute | solution.py:44
  174.4 5.6 %collective-permute-done.20 = bf16[768,256]{1,0:T(8,128)(2,1)S(1)} collective-permute-done((bf16[768,256]{1,0:T(8,128)(2,1)S(1)}, bf16[768,256]{1,0:T(8,128)(2,1)S(1)}, u32[]{:S(2)}, u32[]{:S(2)}) %collective-permute-start.20) | collective-permute-done | bytes 393248 | tf_op jit(solution)/shard_map/ppermute | solution.py:44
  180.0 0.2 pad_maximum_fusion.1.second
  180.2 1.5 collective-permute-start.23
  181.7 3.0 %collective-permute-done.23.second_peer = bf16[4,768,256]{2,1,0:T(8,128)(2,1)S(1)} collective-permute-done((bf16[4,768,256]{2,1,0:T(8,128)(2,1)S(1)}, bf16[4,768,256]{2,1,0:T(8,128)(2,1)S(1)}, u32[]{:S(2)}, u32[]{:S(2)}) %collective-permute-start.23) | collective-permute-done | bytes 1572896 | tf_op jit(solution)/shard_map/ppermute | solution.py:44
  184.8 4.6 %shard_map.177 = (bf16[16,256,512]{2,1,0:T(8,128)(2,1)}, bf16[8,16,32,256]{3,2,1,0:T(8,128)(2,1)}) custom-call(s32[6]{0:T(128)S(1)} %stack.59.where, bf16[4,768,256]{2,1,0:T(8,128)(2,1)S(1)} %pad_maximum_fusion.first, bf16[4,768,256]{2,1,0:T(8,128)(2,1)S(1)} %pad_maximum_fusion.1.second, bf16[4,768,256]{2,1,0:T(8,128)(2,1)S(1)} %collective-permute-done.22.first_peer, ...), custom_call_target="tpu_custom_call" | custom-call | tf_op jit(solution)/shard_map/pallas_call | solution.py:339
  (36 shorter events, 0.1 us)
Async XLA Ops:
  0.6 13.5 %copy-start.1 = (bf16[1024,512]{1,0:T(8,128)(2,1)S(1)}, bf16[1024,512]{1,0:T(8,128)(2,1)}, u32[]{:S(2)}) copy-start(bf16[1024,512]{1,0:T(8,128)(2,1)} %cot.3) | copy-start | bytes 3145732
  0.6 13.5 %copy-start = (bf16[1024,512]{1,0:T(8,128)(2,1)S(1)}, bf16[1024,512]{1,0:T(8,128)(2,1)}, u32[]{:S(2)}) copy-start(bf16[1024,512]{1,0:T(8,128)(2,1)} %act.3) | copy-start | bytes 3145732
  0.7 12.2 %copy-start.11 = (s32[16]{0:T(128)S(1)}, s32[16]{0:T(128)}, u32[]{:S(2)}) copy-start(s32[16]{0:T(128)} %regions.1) | copy-start | bytes 196
  0.7 27.6 %collective-permute-start.2 = (bf16[1024,512]{1,0:T(8,128)(2,1)}, bf16[1024,512]{1,0:T(8,128)(2,1)S(1)}, u32[]{:S(2)}, u32[]{:S(2)}) collective-permute-start(bf16[1024,512]{1,0:T(8,128)(2,1)} %cot.3), channel_id=1, source_target_pairs={{0,1},{8,9},{1,0},{9,8},{64,65},{72,73},{65,64},{73,72},{2,3},{10,... | collective-permute-start | bytes 3145736 | tf_op jit(solution)/shard_map/ppermute | solution.py:44
  7.4 13.3 %collective-permute-start.1 = (bf16[512,512]{1,0:T(8,128)(2,1)}, bf16[512,512]{1,0:T(8,128)(2,1)}, u32[]{:S(2)}, u32[]{:S(2)}) collective-permute-start(bf16[512,512]{1,0:T(8,128)(2,1)} %get-tuple-element.69), channel_id=1, source_target_pairs={{0,6},{8,14},{1,7},{9,15},{64,70},{72,78},{65,71},{73,79},{2,0},{1... | collective-permute-start | bytes 1572872 | tf_op jit(solution)/shard_map/ppermute | solution.py:44
  10.1 13.7 %collective-permute-start = (bf16[512,512]{1,0:T(8,128)(2,1)}, bf16[512,512]{1,0:T(8,128)(2,1)}, u32[]{:S(2)}, u32[]{:S(2)}) collective-permute-start(bf16[512,512]{1,0:T(8,128)(2,1)} %get-tuple-element.69), channel_id=1, source_target_pairs={{0,2},{8,10},{1,3},{9,11},{64,66},{72,74},{65,67},{73,75},{2,4},{1... | collective-permute-start | bytes 1572872 | tf_op jit(solution)/shard_map/ppermute | solution.py:44
  10.1 22.1 %collective-permute-start.5 = (bf16[512,512]{1,0:T(8,128)(2,1)}, bf16[512,512]{1,0:T(8,128)(2,1)}, u32[]{:S(2)}, u32[]{:S(2)}) collective-permute-start(bf16[512,512]{1,0:T(8,128)(2,1)} %get-tuple-element.68), channel_id=1, source_target_pairs={{0,6},{8,14},{1,7},{9,15},{64,70},{72,78},{65,71},{73,79},{2,0},{1... | collective-permute-start | bytes 1572872 | tf_op jit(solution)/shard_map/ppermute | solution.py:44
  14.1 1.6 copy-start.2
  28.3 13.7 %collective-permute-start.3 = (bf16[512,512]{1,0:T(8,128)(2,1)S(1)}, bf16[512,512]{1,0:T(8,128)(2,1)S(1)}, u32[]{:S(2)}, u32[]{:S(2)}) collective-permute-start(bf16[512,512]{1,0:T(8,128)(2,1)S(1)} %get-tuple-element.41), channel_id=1, source_target_pairs={{0,1},{8,9},{1,0},{9,8},{64,65},{72,73},{65,64},{73,72},{2,3},{10,... | collective-permute-start | bytes 1572872 | tf_op jit(solution)/shard_map/ppermute | solution.py:44
  30.9 13.3 %collective-permute-start.4 = (bf16[512,512]{1,0:T(8,128)(2,1)}, bf16[512,512]{1,0:T(8,128)(2,1)S(1)}, u32[]{:S(2)}, u32[]{:S(2)}) collective-permute-start(bf16[512,512]{1,0:T(8,128)(2,1)} %get-tuple-element.68), channel_id=1, source_target_pairs={{0,2},{8,10},{1,3},{9,11},{64,66},{72,74},{65,67},{73,75},{2,4},{1... | collective-permute-start | bytes 1572872 | tf_op jit(solution)/shard_map/ppermute | solution.py:44
  32.2 19.9 %collective-permute-start.7 = (bf16[512,512]{1,0:T(8,128)(2,1)}, bf16[512,512]{1,0:T(8,128)(2,1)S(1)}, u32[]{:S(2)}, u32[]{:S(2)}) collective-permute-start(bf16[512,512]{1,0:T(8,128)(2,1)} %collective-permute-done.5.refs_2_), channel_id=1, source_target_pairs={{0,6},{8,14},{1,7},{9,15},{64,70},{72,78},{65,71},{73,79},{2,0},{1... | collective-permute-start | bytes 1572872 | tf_op jit(solution)/shard_map/ppermute | solution.py:44
  35.4 20.1 %collective-permute-start.6 = (bf16[512,512]{1,0:T(8,128)(2,1)}, bf16[512,512]{1,0:T(8,128)(2,1)S(1)}, u32[]{:S(2)}, u32[]{:S(2)}) collective-permute-start(bf16[512,512]{1,0:T(8,128)(2,1)} %collective-permute-done.refs_3_), channel_id=1, source_target_pairs={{0,2},{8,10},{1,3},{9,11},{64,66},{72,74},{65,67},{73,75},{2,4},{1... | collective-permute-start | bytes 1572872 | tf_op jit(solution)/shard_map/ppermute | solution.py:44
  55.5 33.5 %collective-permute-start.8 = (bf16[4,768,256]{2,1,0:T(8,128)(2,1)}, bf16[4,768,256]{2,1,0:T(8,128)(2,1)}, u32[]{:S(2)}, u32[]{:S(2)}) collective-permute-start(bf16[4,768,256]{2,1,0:T(8,128)(2,1)} %get-tuple-element.48), channel_id=1, source_target_pairs={{0,8},{8,0},{1,9},{9,1},{64,72},{72,64},{65,73},{73,65},{2,10},{10... | collective-permute-start | bytes 4718600 | tf_op jit(solution)/shard_map/ppermute | solution.py:44
  61.0 0.8 copy-start.3
  61.8 15.8 %copy-start.4 = (bf16[4,256,256]{2,1,0:T(8,128)(2,1)S(1)}, bf16[4,256,256]{2,1,0:T(8,128)(2,1)}, u32[]{:S(2)}) copy-start(bf16[4,256,256]{2,1,0:T(8,128)(2,1)} %copy-done.3) | copy-start | bytes 1572868
  61.8 15.8 %collective-permute-start.9 = (bf16[4,256,256]{2,1,0:T(8,128)(2,1)}, bf16[4,256,256]{2,1,0:T(8,128)(2,1)}, u32[]{:S(2)}, u32[]{:S(2)}) collective-permute-start(bf16[4,256,256]{2,1,0:T(8,128)(2,1)} %get-tuple-element.52), channel_id=1, source_target_pairs={{0,8},{8,0},{1,9},{9,1},{64,72},{72,64},{65,73},{73,65},{2,10},{10... | collective-permute-start | bytes 1572872 | tf_op jit(solution)/shard_map/ppermute | solution.py:44
  74.1 10.9 %all-to-all-start.3 = ((bf16[4,128,512]{2,1,0:T(8,128)(2,1)}), bf16[4,128,512]{2,1,0:T(8,128)(2,1)S(1)}, u32[]{:S(2)}, u32[]{:S(2)}) async-start(bf16[4,128,512]{2,1,0:T(8,128)(2,1)} %broadcast_in_dim.2), calls=%async_computation.3 | async-start | bytes 1048576 | tf_op jit(solution)/shard_map/all_to_all | solution.py:78
  85.0 10.9 %all-to-all-start.1 = ((bf16[4,256,256]{2,1,0:T(8,128)(2,1)}), bf16[4,256,256]{2,1,0:T(8,128)(2,1)S(1)}, u32[]{:S(2)}, u32[]{:S(2)}) async-start(bf16[4,256,256]{2,1,0:T(8,128)(2,1)} %add_convert_fusion.1), calls=%async_computation.1 | async-start | bytes 1048576 | tf_op jit(solution)/shard_map/all_to_all | solution.py:73
  95.9 20.4 %all-to-all-start = ((bf16[4,768,256]{2,1,0:T(8,128)(2,1)}), bf16[4,768,256]{2,1,0:T(8,128)(2,1)}, u32[]{:S(2)}, u32[]{:S(2)}) async-start(bf16[4,768,256]{2,1,0:T(8,128)(2,1)} %add_convert_fusion), calls=%async_computation | async-start | bytes 3145728 | tf_op jit(solution)/shard_map/all_to_all | solution.py:73
  100.3 10.5 %collective-permute-start.14 = (bf16[512,512]{1,0:T(8,128)(2,1)S(1)}, bf16[512,512]{1,0:T(8,128)(2,1)S(1)}, u32[]{:S(2)}, u32[]{:S(2)}) collective-permute-start(bf16[512,512]{1,0:T(8,128)(2,1)S(1)} %bitcast.17), channel_id=1, source_target_pairs={{0,1},{8,9},{1,0},{9,8},{64,65},{72,73},{65,64},{73,72},{2,3},{10,... | collective-permute-start | bytes 1572872 | tf_op jit(solution)/shard_map/ppermute | solution.py:44
  112.9 26.0 %copy-start.8 = (f32[2,4,32,256]{3,2,1,0:T(8,128)S(1)}, f32[2,4,32,256]{3,2,1,0:T(8,128)}, u32[]{:S(2)}) copy-start(f32[2,4,32,256]{3,2,1,0:T(8,128)} %param.23) | copy-start | bytes 786436
  112.9 26.0 %copy-start.9 = (f32[2,4,32,256]{3,2,1,0:T(8,128)S(1)}, f32[2,4,32,256]{3,2,1,0:T(8,128)}, u32[]{:S(2)}) copy-start(f32[2,4,32,256]{3,2,1,0:T(8,128)} %moment.1) | copy-start | bytes 786436
  112.9 26.0 %copy-start.10 = (f32[2,4,32,256]{3,2,1,0:T(8,128)S(1)}, f32[2,4,32,256]{3,2,1,0:T(8,128)}, u32[]{:S(2)}) copy-start(f32[2,4,32,256]{3,2,1,0:T(8,128)} %second.1) | copy-start | bytes 786436
  116.3 22.6 %all-to-all-start.4 = ((bf16[16,2,32,256]{3,2,1,0:T(8,128)(2,1)}), bf16[16,2,32,256]{3,2,1,0:T(8,128)(2,1)S(1)}, u32[]{:S(2)}, u32[]{:S(2)}) async-start(bf16[16,2,32,256]{3,2,1,0:T(8,128)(2,1)} %shard_map.174), calls=%async_computation.4 | async-start | bytes 1048576 | tf_op jit(solution)/shard_map/all_to_all | solution.py:423
  125.3 17.6 %copy-start.5 = (f32[256,512]{1,0:T(8,128)S(1)}, f32[256,512]{1,0:T(8,128)}, u32[]{:S(2)}) copy-start(f32[256,512]{1,0:T(8,128)} %refs_4_.1) | copy-start | bytes 1572868
  125.3 17.6 %copy-start.6 = (f32[256,512]{1,0:T(8,128)S(1)}, f32[256,512]{1,0:T(8,128)}, u32[]{:S(2)}) copy-start(f32[256,512]{1,0:T(8,128)} %refs_5_.3) | copy-start | bytes 1572868
  125.4 17.6 %copy-start.7 = (f32[256,512]{1,0:T(8,128)S(1)}, f32[256,512]{1,0:T(8,128)}, u32[]{:S(2)}) copy-start(f32[256,512]{1,0:T(8,128)} %refs_6_.1) | copy-start | bytes 1572868
  128.2 12.7 %collective-permute-start.10 = (bf16[256,256]{1,0:T(8,128)(2,1)}, bf16[256,256]{1,0:T(8,128)(2,1)S(1)}, u32[]{:S(2)}, u32[]{:S(2)}) collective-permute-start(bf16[256,256]{1,0:T(8,128)(2,1)} %get-tuple-element.53), channel_id=1, source_target_pairs={{0,0},{8,8},{1,16},{9,24},{64,64},{72,72},{65,80},{73,88},{2,2},{1... | collective-permute-start | bytes 393224 | tf_op jit(solution)/shard_map/ppermute | solution.py:44
  129.7 11.1 %collective-permute-start.11 = (bf16[256,256]{1,0:T(8,128)(2,1)}, bf16[256,256]{1,0:T(8,128)(2,1)S(1)}, u32[]{:S(2)}, u32[]{:S(2)}) collective-permute-start(bf16[256,256]{1,0:T(8,128)(2,1)} %get-tuple-element.54), channel_id=1, source_target_pairs={{0,64},{8,72},{1,80},{9,88},{64,0},{72,8},{65,16},{73,24},{2,66},{... | collective-permute-start | bytes 393224 | tf_op jit(solution)/shard_map/ppermute | solution.py:44
  131.1 9.7 %collective-permute-start.12 = (bf16[256,256]{1,0:T(8,128)(2,1)}, bf16[256,256]{1,0:T(8,128)(2,1)S(1)}, u32[]{:S(2)}, u32[]{:S(2)}) collective-permute-start(bf16[256,256]{1,0:T(8,128)(2,1)} %get-tuple-element.55), channel_id=1, source_target_pairs={{0,32},{8,40},{1,48},{9,56},{64,96},{72,104},{65,112},{73,120},{2,... | collective-permute-start | bytes 393224 | tf_op jit(solution)/shard_map/ppermute | solution.py:44
  137.6 5.4 %collective-permute-start.13 = (bf16[256,256]{1,0:T(8,128)(2,1)S(1)}, bf16[256,256]{1,0:T(8,128)(2,1)S(1)}, u32[]{:S(2)}, u32[]{:S(2)}) collective-permute-start(bf16[256,256]{1,0:T(8,128)(2,1)S(1)} %get-tuple-element.56), channel_id=1, source_target_pairs={{0,96},{8,104},{1,112},{9,120},{64,32},{72,40},{65,48},{73,56},{2,... | collective-permute-start | bytes 393224 | tf_op jit(solution)/shard_map/ppermute | solution.py:44
  145.2 9.4 %collective-permute-start.18 = (bf16[768,256]{1,0:T(8,128)(2,1)S(1)}, bf16[768,256]{1,0:T(8,128)(2,1)S(1)}, u32[]{:S(2)}, u32[]{:S(2)}) collective-permute-start(bf16[768,256]{1,0:T(8,128)(2,1)S(1)} %get-tuple-element.62), channel_id=1, source_target_pairs={{0,32},{8,40},{1,33},{9,41},{64,96},{72,104},{65,97},{73,105},{2,3... | collective-permute-start | bytes 1179656 | tf_op jit(solution)/shard_map/ppermute | solution.py:44
  148.3 11.7 %collective-permute-start.15 = (bf16[768,256]{1,0:T(8,128)(2,1)S(1)}, bf16[768,256]{1,0:T(8,128)(2,1)S(1)}, u32[]{:S(2)}, u32[]{:S(2)}) collective-permute-start(bf16[768,256]{1,0:T(8,128)(2,1)S(1)} %get-tuple-element.62), channel_id=1, source_target_pairs={{0,64},{8,72},{1,65},{9,73},{64,0},{72,8},{65,1},{73,9},{2,66},{10... | collective-permute-start | bytes 1179656 | tf_op jit(solution)/shard_map/ppermute | solution.py:44
  150.8 20.7 %collective-permute-start.17 = (bf16[768,256]{1,0:T(8,128)(2,1)S(1)}, bf16[768,256]{1,0:T(8,128)(2,1)S(1)}, u32[]{:S(2)}, u32[]{:S(2)}) collective-permute-start(bf16[768,256]{1,0:T(8,128)(2,1)S(1)} %get-tuple-element.62), channel_id=1, source_target_pairs={{0,48},{8,56},{1,49},{9,57},{64,112},{72,120},{65,113},{73,121},{2... | collective-permute-start | bytes 1179656 | tf_op jit(solution)/shard_map/ppermute | solution.py:44
  154.0 17.5 %collective-permute-start.16 = (bf16[768,256]{1,0:T(8,128)(2,1)S(1)}, bf16[768,256]{1,0:T(8,128)(2,1)S(1)}, u32[]{:S(2)}, u32[]{:S(2)}) collective-permute-start(bf16[768,256]{1,0:T(8,128)(2,1)S(1)} %get-tuple-element.62), channel_id=1, source_target_pairs={{0,16},{8,24},{1,17},{9,25},{64,80},{72,88},{65,81},{73,89},{2,18}... | collective-permute-start | bytes 1179656 | tf_op jit(solution)/shard_map/ppermute | solution.py:44
  154.5 19.9 %collective-permute-start.21 = (bf16[768,256]{1,0:T(8,128)(2,1)S(1)}, bf16[768,256]{1,0:T(8,128)(2,1)S(1)}, u32[]{:S(2)}, u32[]{:S(2)}) collective-permute-start(bf16[768,256]{1,0:T(8,128)(2,1)S(1)} %collective-permute-done.18), channel_id=1, source_target_pairs={{0,64},{8,72},{1,65},{9,73},{64,0},{72,8},{65,1},{73,9},{2,66},{10... | collective-permute-start | bytes 1179656 | tf_op jit(solution)/shard_map/ppermute | solution.py:44
  160.0 20.0 %collective-permute-start.20 = (bf16[768,256]{1,0:T(8,128)(2,1)S(1)}, bf16[768,256]{1,0:T(8,128)(2,1)S(1)}, u32[]{:S(2)}, u32[]{:S(2)}) collective-permute-start(bf16[768,256]{1,0:T(8,128)(2,1)S(1)} %collective-permute-done.15), channel_id=1, source_target_pairs={{0,48},{8,56},{1,49},{9,57},{64,112},{72,120},{65,113},{73,121},{2... | collective-permute-start | bytes 1179656 | tf_op jit(solution)/shard_map/ppermute | solution.py:44
  165.5 14.5 %collective-permute-start.19 = (bf16[768,256]{1,0:T(8,128)(2,1)S(1)}, bf16[768,256]{1,0:T(8,128)(2,1)S(1)}, u32[]{:S(2)}, u32[]{:S(2)}) collective-permute-start(bf16[768,256]{1,0:T(8,128)(2,1)S(1)} %collective-permute-done.15), channel_id=1, source_target_pairs={{0,16},{8,24},{1,17},{9,25},{64,80},{72,88},{65,81},{73,89},{2,18}... | collective-permute-start | bytes 1179656 | tf_op jit(solution)/shard_map/ppermute | solution.py:44
  171.8 10.0 %collective-permute-start.22 = (bf16[4,768,256]{2,1,0:T(8,128)(2,1)S(1)}, bf16[4,768,256]{2,1,0:T(8,128)(2,1)S(1)}, u32[]{:S(2)}, u32[]{:S(2)}) collective-permute-start(bf16[4,768,256]{2,1,0:T(8,128)(2,1)S(1)} %pad_maximum_fusion.first), channel_id=1, source_target_pairs={{0,8},{8,0},{1,9},{9,1},{64,72},{72,64},{65,73},{73,65},{2,10},{10... | collective-permute-start | bytes 4718600 | tf_op jit(solution)/shard_map/ppermute | solution.py:44
  180.2 4.6 %collective-permute-start.23 = (bf16[4,768,256]{2,1,0:T(8,128)(2,1)S(1)}, bf16[4,768,256]{2,1,0:T(8,128)(2,1)S(1)}, u32[]{:S(2)}, u32[]{:S(2)}) collective-permute-start(bf16[4,768,256]{2,1,0:T(8,128)(2,1)S(1)} %pad_maximum_fusion.1.second), channel_id=1, source_target_pairs={{0,8},{8,0},{1,9},{9,1},{64,72},{72,64},{65,73},{73,65},{2,10},{10... | collective-permute-start | bytes 4718600 | tf_op jit(solution)/shard_map/ppermute | solution.py:44

commit v3 on v2

--- a/solution.py
+++ b/solution.py
@@ -44,6 +44,15 @@
     return lax.ppermute(array, AXES, pairs)
 
 
+def swap_among(array, axis, groups):
+    return lax.all_to_all(array, axis, 0, 0, axis_index_groups=groups)
+
+
+X_GROUPS = [[z * 8 + x * 2 + c for x in range(4)] for z in range(2) for c in range(2)]
+ZL_X_GROUPS = [[z * 8 + x * 2 + c for z in range(2) for x in range(4)] for c in range(2)]
+Y_GROUPS = [[y * 2 + z for y in range(4)] for z in range(2)]
+
+
 def along_x(k):
     return lambda x, y, zl, zh, c: (x + k, y, zl, zh, c)
 
@@ -68,89 +77,80 @@
     return lambda x, y, zl, zh, c: (2 * ((x & 1) ^ ka) + zh, y, zl ^ kb, x >> 1, c)
 
 
-def all_x(array):
-    groups = [[z * 8 + x * 2 + c for x in range(4)] for z in range(2) for c in range(2)]
-    return lax.all_to_all(array, "fsdp", 0, 0, axis_index_groups=groups)
-
-
-def all_y(array):
-    groups = [[y * 2 + z for y in range(4)] for z in range(2)]
-    return lax.all_to_all(array, "tp", 0, 0, axis_index_groups=groups)
-
-
-def partials_kernel(counts, scale, where, *refs):
-    acts, cots, (keep, give) = refs[: sum(counts)], refs[-4:-2], refs[-2:]
-    zh, c = where[ZH], where[CORE]
-    wide = keep.shape[2]
-    for side in range(2):
-        place = 2 * (side ^ zh)
+def partials_kernel(counts, where, *refs):
+    acts, (cot, keep, give) = refs[: sum(counts)], refs[-3:]
+    c, wide = where[CORE], keep.shape[2]
+    for out, h in ((keep, c), (give, 1 - c)):
+        half = pl.ds(pl.multiple_of(h * wide, wide), wide)
         first = 0
         for d, count in enumerate(counts):
-            total, row = None, 0
-            for ref in acts[first : first + count]:
-                term = contract_rows(ref[...], cots[side][pl.ds(row, ref.shape[0]), :])
-                total = term if total is None else total + term
-                row += ref.shape[0]
+            for j in range(2):
+                total, row = None, 0
+                for ref in acts[first : first + count]:
+                    block = cot[pl.ds(row, ref.shape[0]), pl.ds(j * wide, wide)]
+                    term = contract_rows(ref[:, half], block)
+                    total = term if total is None else total + term
+                    row += ref.shape[0]
+                out[j, pl.ds(d * wide, wide), :] = total.astype(BF16)
             first += count
-            total = total * scale
-            rows = pl.ds(d * wide, wide)
-            for h in range(2):
-                part = total[h * wide : (h + 1) * wide]
-
-                @pl.when(c == h)
-                def _():
-                    keep[place, rows, :] = part[:, :wide].astype(BF16)
-                    keep[place + 1, rows, :] = part[:, wide:].astype(BF16)
-
-                @pl.when(c != h)
-                def _():
-                    give[place, rows, :] = part[:, :wide].astype(BF16)
-                    give[place + 1, rows, :] = part[:, wide:].astype(BF16)
-
-
-def partials(here, acts, cots, scale):
+
+
+def partials(here, acts, cot):
     counts = [len(parts) for parts in acts]
     flat = [part for parts in acts for part in parts]
     wide = flat[0].shape[1] // 2
-    shape = (4, len(counts) * wide, wide)
-    return pl.pallas_call(
-        functools.partial(partials_kernel, counts, scale),
+    shape = (2, len(counts) * wide, wide)
+    return pl.pallas_call(
+        functools.partial(partials_kernel, counts),
         out_shape=(jax.ShapeDtypeStruct(shape, BF16),) * 2,
         in_specs=[pl.BlockSpec(memory_space=pltpu.SMEM)]
-        + [pl.BlockSpec(memory_space=pltpu.VMEM)] * (len(flat) + 2),
+        + [pl.BlockSpec(memory_space=pltpu.VMEM)] * (len(flat) + 1),
         out_specs=(pl.BlockSpec(memory_space=pltpu.VMEM), pl.BlockSpec(memory_space=pltpu.VMEM)),
         compiler_params=pltpu.CompilerParams(vmem_limit_bytes=48 * 1024 * 1024),
-    )(here, *flat, *cots)
-
-
-def low_kernel(scales, where, act, cot, adapters, keep, give):
-    rows, rank = keep.shape[0], adapters.shape[3]
-    for h in range(2):
-        part = pl.ds(h * rows, rows)
-        down = jnp.dot(act[part, :], adapters[0, 0], preferred_element_type=F32) * scales[0]
-        up = jnp.dot(cot[part, :], adapters[1, 0], preferred_element_type=F32) * scales[1]
-
-        @pl.when(where[ZH] == h)
-        def _():
-            keep[:, :rank] = down
-            keep[:, rank:] = up
-
-        @pl.when(where[ZH] != h)
-        def _():
-            give[:, :rank] = down.astype(BF16)
-            give[:, rank:] = up.astype(BF16)
+    )(here, *flat, cot)
+
+
+def add_kernel(where, *refs):
+    parts, outs = refs[:8], refs[8:]
+    rows = parts[0].shape[1]
+    for k, out in enumerate(outs):
+        quarter = (where[X] + k) & 3
+        side, j = (quarter >> 1) ^ where[ZH], quarter & 1
+        for number in range(2):
+
+            @pl.when(side == number)
+            def _():
+                keep, got, keep_far, got_far = parts[4 * number : 4 * number + 4]
+                out[:rows] = (keep[j].astype(F32) + got[j].astype(F32)).astype(BF16)
+                out[rows:] = (keep_far[j].astype(F32) + got_far[j].astype(F32)).astype(BF16)
+
+
+def add_blocks(here, parts):
+    vmem = pl.BlockSpec(memory_space=pltpu.VMEM)
+    _, rows, wide = parts[0].shape
+    return pl.pallas_call(
+        add_kernel,
+        out_shape=(jax.ShapeDtypeStruct((rows + parts[2].shape[1], wide), BF16),) * 4,
+        in_specs=[pl.BlockSpec(memory_space=pltpu.SMEM)] + [vmem] * 8,
+        out_specs=(vmem,) * 4,
+        compiler_params=pltpu.CompilerParams(vmem_limit_bytes=32 * 1024 * 1024),
+    )(here, *parts)
+
+
+def low_kernel(scales, where, act, cot, adapters, out):
+    rank = adapters.shape[3]
+    down = jnp.dot(act[...], adapters[0, 0], preferred_element_type=F32) * scales[0]
+    up = jnp.dot(cot[...], adapters[1, 0], preferred_element_type=F32) * scales[1]
+    out[:, :rank] = down.astype(BF16)
+    out[:, rank:] = up.astype(BF16)
 
 
 def low_parts(here, act, cot, adapters, scales):
-    rows, rank = act.shape[0] // 2, adapters.shape[3]
+    rank = adapters.shape[3]
     whole = pl.BlockSpec(act.shape, lambda i, where: (0, 0))
-    out = pl.BlockSpec((rows, 2 * rank), lambda i, where: (0, 0))
     return pl.pallas_call(
         functools.partial(low_kernel, scales),
-        out_shape=(
-            jax.ShapeDtypeStruct((rows, 2 * rank), F32),
-            jax.ShapeDtypeStruct((rows, 2 * rank), BF16),
-        ),
+        out_shape=jax.ShapeDtypeStruct((act.shape[0], 2 * rank), BF16),
         grid_spec=pltpu.PrefetchScalarGridSpec(
             num_scalar_prefetch=1,
             grid=(1,),
@@ -161,36 +161,31 @@
                     (2, 1) + adapters.shape[2:], lambda i, where: (0, where[REGION], 0, 0)
                 ),
             ],
-            out_specs=(out, out),
+            out_specs=pl.BlockSpec((act.shape[0], 2 * rank), lambda i, where: (0, 0)),
         ),
         compiler_params=pltpu.CompilerParams(vmem_limit_bytes=32 * 1024 * 1024),
     )(here, act, cot, adapters)
 
 
-def grads_kernel(scales, where, low_half, low_other, act, cot, out):
-    rows, rank = low_half.shape[0], out.shape[3]
-    zh = where[ZH]
-    mine = pl.ds(pl.multiple_of(zh * rows, rows), rows)
-    theirs = pl.ds(pl.multiple_of((1 - zh) * rows, rows), rows)
+def grads_kernel(scales, low, act, cot, out):
+    rank = out.shape[3]
     for side, source, start in ((0, act, rank), (1, cot, 0)):
-        columns = pl.ds(start, rank)
-        total = contract_rows(source[mine, :], low_half[:, columns])
-        total = total + contract_rows(source[theirs, :], low_other[:, columns])
+        total = contract_rows(source[...], low[:, pl.ds(start, rank)])
         total = (total * scales[side]).astype(BF16)
         for f in range(out.shape[0]):
             out[f, side] = total[f * out.shape[2] : (f + 1) * out.shape[2]]
 
 
-def adapter_grads(here, low_half, low_other, act, cot, scales, count):
-    rank = low_half.shape[1] // 2
+def adapter_grads(low, act, cot, scales, count):
+    rank = low.shape[1] // 2
     vmem = pl.BlockSpec(memory_space=pltpu.VMEM)
     return pl.pallas_call(
         functools.partial(grads_kernel, scales),
         out_shape=jax.ShapeDtypeStruct((count, 2, act.shape[1] // count, rank), BF16),
-        in_specs=[pl.BlockSpec(memory_space=pltpu.SMEM)] + [vmem] * 4,
+        in_specs=[vmem] * 3,
         out_specs=vmem,
         compiler_params=pltpu.CompilerParams(vmem_limit_bytes=32 * 1024 * 1024),
-    )(here, low_half, low_other, act, cot)
+    )(low, act, cot)
 
 
 def adamw_values(param, moment, second, grad, first_fix, second_fix):
@@ -235,47 +230,39 @@
     )(regions, fixes, got, param, moment, second)
 
 
-def pick_kernel(where, near, far, *outs):
-    wide = far.shape[1]
+def pick_kernel(where, *refs):
+    arrays, outs = refs[:4], refs[4:]
+    wide = outs[0].shape[0]
     for k, out in enumerate(outs):
         row_y = 2 * (where[ZL] ^ (k % 2)) + ((where[X] & 1) ^ (k // 2))
         away = (row_y - where[Y] + 4) & 3
         place = away ^ (away >> 1)
-
-        @pl.when(place < 3)
-        def _():
-            rows = pl.ds(pl.multiple_of(jnp.minimum(place, 2) * wide, wide), wide)
-            total = near[0, rows, :].astype(F32)
-            for q in range(1, 4):
-                total = total + near[q, rows, :].astype(F32)
-            out[...] = total.astype(BF16)
-
-        @pl.when(place == 3)
-        def _():
-            total = far[0].astype(F32)
-            for q in range(1, 4):
-                total = total + far[q].astype(F32)
-            out[...] = total.astype(BF16)
-
-
-def pick_blocks(here, near, far):
+        rows = pl.ds(pl.multiple_of(place * wide, wide), wide)
+        total = arrays[0][rows, :].astype(F32)
+        for array in arrays[1:]:
+            total = total + array[rows, :].astype(F32)
+        out[...] = total.astype(BF16)
+
+
+def pick_blocks(here, arrays):
     vmem = pl.BlockSpec(memory_space=pltpu.VMEM)
-    count = 4
+    rows, columns = arrays[0].shape
     return pl.pallas_call(
         pick_kernel,
-        out_shape=(jax.ShapeDtypeStruct(far.shape[1:], BF16),) * count,
-        in_specs=[pl.BlockSpec(memory_space=pltpu.SMEM), vmem, vmem],
-        out_specs=(vmem,) * count,
-        compiler_params=pltpu.CompilerParams(vmem_limit_bytes=32 * 1024 * 1024),
-    )(here, near, far)
-
-
-def weight_kernel(where, fixes, *refs):
+        out_shape=(jax.ShapeDtypeStruct((rows // 4, columns), BF16),) * 4,
+        in_specs=[pl.BlockSpec(memory_space=pltpu.SMEM)] + [vmem] * 4,
+        out_specs=(vmem,) * 4,
+        compiler_params=pltpu.CompilerParams(vmem_limit_bytes=32 * 1024 * 1024),
+    )(here, *arrays)
+
+
+def weight_kernel(scale, where, fixes, *refs):
     terms, (param, moment, second, extra), outs = refs[:4], refs[4:8], refs[8:]
     new_param, new_moment, new_second, rounded = outs
     rows, wide = terms[0].shape
     for ka in range(2):
         grad = terms[2 * ka][...].astype(F32) + terms[2 * ka + 1][...].astype(F32)
+        grad = grad * scale
         for h in range(2):
 
             @pl.when(((where[X] >> 1) ^ ka) == h)
@@ -293,13 +280,13 @@
     rounded[pl.ds(2 * rows, extra.shape[0]), :] = extra[...]
 
 
-def weight_update(here, fixes, terms, param, moment, second, extra):
+def weight_update(here, scale, fixes, terms, param, moment, second, extra):
     vmem = pl.BlockSpec(memory_space=pltpu.VMEM)
     smem = pl.BlockSpec(memory_space=pltpu.SMEM)
     like = jax.ShapeDtypeStruct(param.shape, F32)
     rounded = jax.ShapeDtypeStruct((2 * param.shape[0] + extra.shape[0], extra.shape[1]), BF16)
     return pl.pallas_call(
-        weight_kernel,
+        functools.partial(weight_kernel, scale),
         out_shape=(like, like, like, rounded),
         in_specs=[smem, smem] + [vmem] * 8,
         out_specs=(vmem,) * 4,
@@ -391,60 +378,45 @@
     ])
 
     middle = tok_dev // 2
-    half = activations.shape[1] // 2
-    act_first, act_second = activations[:middle], activations[middle:]
-    back_first = move(act_first, along_y(1))
-    ahead_first = move(act_first, along_y(-1))
+    back = move(activations, along_y(1))
+    ahead = move(activations, along_y(-1))
     cot_zh = move(cotangent, other_zh)
-    back_second = move(act_second, along_y(1))
-    ahead_second = move(act_second, along_y(-1))
-    far_first = move(back_first, along_y(1))
-    far_second = move(ahead_second, along_y(-1))
-
-    low_keep, low_give = low_parts(
-        here, activations, cotangent, adapter_copy, (inv_width, inv_rank)
-    )
-    low_give, back_first, ahead_first, cot_zh = lax.optimization_barrier(
-        (low_give, back_first, ahead_first, cot_zh)
-    )
-    low_half = (low_keep + move(low_give, other_zh).astype(F32)).astype(BF16)
-    low_half = low_half.reshape(4, tok_dev // 8, 2 * rank)
-    low_half, back_second, ahead_second = lax.optimization_barrier(
-        (low_half, back_second, ahead_second)
-    )
-    low_own = jnp.sum(all_y(low_half).astype(F32), axis=0).astype(BF16)
-    low_half = all_y(jnp.broadcast_to(low_own[None], low_half.shape))
-    low_half = low_half.reshape(tok_dev // 2, 2 * rank)
-    low_other = move(low_half, other_zh)
+    far_first = move(back[:middle], along_y(1))
+    far_second = move(ahead[middle:], along_y(-1))
+
+    low = low_parts(here, activations, cotangent, adapter_copy, (inv_width, inv_rank))
+    low = swap_among(low.reshape(tp_count, tok_dev // tp_count, 2 * rank), "tp", None)
+    low_sum = jnp.sum(low.astype(F32), axis=0).astype(BF16)
+
+    def swapped(acts, cot):
+        keep, give = partials(here, acts, cot)
+        return [keep, move(give, other_core)]
+
+    low_sum, back, ahead = lax.optimization_barrier((low_sum, back, ahead))
+    near_acts = [[activations], [ahead], [back]]
+    parts = swapped(near_acts, cotangent)
+    far_acts = [[far_first, far_second]]
+    far_first, far_second, cot_zh = lax.optimization_barrier((far_first, far_second, cot_zh))
+    parts += swapped(far_acts, cotangent)
+    parts += swapped(near_acts, cot_zh) + swapped(far_acts, cot_zh)
+    blocks = add_blocks(here, parts)
+    low_sum, *blocks = lax.optimization_barrier((low_sum, *blocks))
+    low_all = swap_among(jnp.broadcast_to(low_sum[None], low.shape), "tp", None)
+    blocks = [blocks[0]] + [move(blocks[k], along_x(k)) for k in (1, 3, 2)]
+    blocks = pick_blocks(here, blocks)
+    low_all = low_all.reshape(tok_dev, 2 * rank)
+
     parts = adapter_grads(
-        here, low_half, low_other, activations, cotangent,
+        low_all, activations, cotangent,
         (inv_width * grad_scale, inv_rank * grad_scale), fsdp_count,
     )
     got = lax.all_to_all(parts, "fsdp", 0, 0)
     new_adapter, new_adapter_moment, new_adapter_second, adapter_rows = adapter_update(
         region_of, fixes, got, adapter_master, adapter_moment, adapter_second
     )
-
-    scale = inv_width * grad_scale
-    cots = [cotangent, cot_zh]
-    near_keep, near_give = partials(
-        here, [[activations], [ahead_first, ahead_second], [back_first, back_second]], cots, scale
-    )
-    far_first, far_second, near_give = lax.optimization_barrier(
-        (far_first, far_second, near_give)
-    )
-    far_keep, far_give = partials(here, [[far_first, far_second]], cots, scale)
-
-    def reduce_x(keep, give):
-        both = (keep.astype(F32) + move(give, other_core).astype(F32)).astype(BF16)
-        return all_x(both)
-
-    near = reduce_x(near_keep, near_give)
-    far = reduce_x(far_keep, far_give)
-    blocks = pick_blocks(here, near, far)
     terms = [move(block, to_owner(k // 2, k % 2)) for k, block in enumerate(blocks)]
     new_weight, new_weight_moment, new_weight_second, piece = weight_update(
-        here, fixes, terms, weight_master, weight_moment, weight_second, adapter_rows
+        here, inv_width * grad_scale, fixes, terms, weight_master, weight_moment, weight_second, adapter_rows
     )
 
     from_zl = move(piece, other_zl)

time: 190 us -> 163 us (0.86)
  starting transfers between devices: 75.3 us -> 63.3 us
  blocking collectives: 11.4 us -> 0 us
  local copies, waits for them, and re-layouts: 6.8 us -> 16.7 us
  waiting for transfers between devices: 62.3 us -> 53.3 us
  other arithmetic: 6.06 us -> 1.84 us
    ppermute x24 -> x25, waiting for transfers between devices: 50 us -> 32.3 us  [move(): return lax.ppermute(array, AXES, pairs)]
    all_to_all x1 -> x0, blocking collectives: 11.4 us -> none  [all_y(): return lax.all_to_all(array, 'tp', 0, 0, axis_index_groups=groups)]
    all_to_all x3 -> x2, waiting for transfers between devices: 12.3 us -> 21 us  [swap_among(): return lax.all_to_all(array, axis, 0, 0, axis_index_groups=groups)]
    unnamed x24 -> x36, local copies, waits for them, and re-layouts: 2.42 us -> 11 us
    ppermute x24 -> x25, starting transfers between devices: 54.5 us -> 47.9 us  [move(): return lax.ppermute(array, AXES, pairs)]
    convert_element_type x3 -> x0, other arithmetic: 5.51 us -> none  [the longest x2 5.35 us: reduce_x(): both = (keep.astype(F32) + move(give, other_core).astype(F32)).astype(BF16)]
    all_to_all x1, starting transfers between devices: 9.03 us -> 6.32 us  [shards(): got = lax.all_to_all(parts, 'fsdp', 0, 0)]
    all_to_all x3 -> x2, starting transfers between devices: 11.8 us -> 9.12 us  [swap_among(): return lax.all_to_all(array, axis, 0, 0, axis_index_groups=groups)]
  transfers between devices with their start and end apart: 28 -> 28, of which waited for: 14 -> 12; matrix products, arithmetic and copies ran while one was open for 6% -> 4% of each run, Pallas kernels for 10% -> 11%
where the time goes in v3:
time: 163 us
  starting transfers between devices  63.3 us (39%)
  waiting for transfers between devices  53.3 us (33%)
  Pallas kernels  25.9 us (16%)
  local copies, waits for them, and re-layouts  16.7 us (10%)
  other arithmetic  1.84 us (1%)
    ppermute x25, starting transfers between devices, move(): return lax.ppermute(array, AXES, pairs)  47.9 us
    ppermute x25, waiting for transfers between devices, move(): return lax.ppermute(array, AXES, pairs)  32.3 us
    all_to_all x2, waiting for transfers between devices, swap_among(): return lax.all_to_all(array, axis, 0, 0, axis_index_groups=groups)  21 us
    unnamed x36, local copies, waits for them, and re-layouts  11 us
    pallas_call x4, Pallas kernels, partials(): pl.pallas_call(functools.partial(partials_kernel, counts), out_shape=(jax...  10.8 us
    all_to_all x2, starting transfers between devices, swap_among(): return lax.all_to_all(array, axis, 0, 0, axis_index_groups=groups)  9.12 us
    all_to_all x1, starting transfers between devices, shards(): got = lax.all_to_all(parts, 'fsdp', 0, 0)  6.32 us
    pallas_call x1, Pallas kernels, place_blocks(): pl.pallas_call(place_kernel, out_shape=(jax.ShapeDtypeStruct((16, rows, 2...  4.56 us
  transfers between devices with their start and end apart: 28, of which 12 were waited for; matrix products, arithmetic and copies ran while one was open for 4% of the time, Pallas kernels for 11%

profile of v3, /device:TPU:1, one launch (start us, length us, event | category | flops | bytes accessed | tf_op | source)
XLA Modules:
  0.0 162.6 jit_solution(6685043540499592049)
XLA Ops:
  0.6 3.6 %collective-permute-start.1 = (bf16[1024,512]{1,0:T(8,128)(2,1)}, bf16[1024,512]{1,0:T(8,128)(2,1)S(1)}, u32[]{:S(2)}, u32[]{:S(2)}) collective-permute-start(bf16[1024,512]{1,0:T(8,128)(2,1)} %act.3), channel_id=1, source_target_pairs={{0,6},{8,14},{1,7},{9,15},{64,70},{72,78},{65,71},{73,79},{2,0},{1... | collective-permute-start | bytes 3145736 | tf_op jit(solution)/shard_map/ppermute | solution.py:44
  4.3 3.6 %collective-permute-start.6 = (bf16[1024,512]{1,0:T(8,128)(2,1)}, bf16[1024,512]{1,0:T(8,128)(2,1)}, u32[]{:S(2)}, u32[]{:S(2)}) collective-permute-start(bf16[1024,512]{1,0:T(8,128)(2,1)} %cot.3), channel_id=1, source_target_pairs={{0,1},{8,9},{1,0},{9,8},{64,65},{72,73},{65,64},{73,72},{2,3},{10,... | collective-permute-start | bytes 3145736 | tf_op jit(solution)/shard_map/ppermute | solution.py:44
  7.9 1.2 dynamic_slice.4
  9.1 0.7 stack.59.where
  9.8 1.2 copy-done
  11.1 1.2 copy-done.2
  12.3 1.6 copy-done.5
  13.9 2.2 %shard_map.170 = bf16[1024,512]{1,0:T(8,128)(2,1)} custom-call(s32[6]{0:T(128)S(1)} %stack.59.where, bf16[1024,512]{1,0:T(8,128)(2,1)S(1)} %copy-done, bf16[1024,512]{1,0:T(8,128)(2,1)S(1)} %copy-done.2, bf16[2,4,512,256]{3,2,1,0:T(8,128)(2,1)S(1)} %copy-done.5), custom_call_target="tpu_custom_call" | custom-call | tf_op jit(solution)/shard_map/pallas_call | solution.py:151
  16.1 4.2 %all-to-all-start = ((bf16[8,128,512]{2,1,0:T(8,128)(2,1)}), bf16[8,128,512]{2,1,0:T(8,128)(2,1)}, u32[]{:S(2)}, u32[]{:S(2)}) async-start(bf16[8,128,512]{2,1,0:T(8,128)(2,1)} %bitcast.5), calls=%async_computation | async-start | bytes 2097152 | tf_op jit(solution)/shard_map/all_to_all | solution.py:48
  20.4 6.0 %collective-permute-done.1.refs_1_ = bf16[1024,512]{1,0:T(8,128)(2,1)S(1)} collective-permute-done((bf16[1024,512]{1,0:T(8,128)(2,1)}, bf16[1024,512]{1,0:T(8,128)(2,1)S(1)}, u32[]{:S(2)}, u32[]{:S(2)}) %collective-permute-start.1) | collective-permute-done | bytes 1048608 | tf_op jit(solution)/shard_map/ppermute | solution.py:44
  26.4 0.8 slice.9
  27.2 3.4 %collective-permute-start.4 = (bf16[512,512]{1,0:T(8,128)(2,1)}, bf16[512,512]{1,0:T(8,128)(2,1)}, u32[]{:S(2)}, u32[]{:S(2)}) collective-permute-start(bf16[512,512]{1,0:T(8,128)(2,1)} %slice.9), channel_id=1, source_target_pairs={{0,6},{8,14},{1,7},{9,15},{64,70},{72,78},{65,71},{73,79},{2,0},{1... | collective-permute-start | bytes 1572872 | tf_op jit(solution)/shard_map/ppermute | solution.py:44
  30.6 1.9 %slice.8 = bf16[512,512]{1,0:T(8,128)(2,1)} slice(bf16[1024,512]{1,0:T(8,128)(2,1)} %collective-permute-done.refs_2_), slice={[0:512], [0:512]} | slice | bytes 1048576 | tf_op jit(solution)/shard_map/slice | solution.py:384
  32.5 9.4 %all-to-all-done = bf16[8,128,512]{2,1,0:T(8,128)(2,1)} async-done(((bf16[8,128,512]{2,1,0:T(8,128)(2,1)}), bf16[8,128,512]{2,1,0:T(8,128)(2,1)}, u32[]{:S(2)}, u32[]{:S(2)}) %all-to-all-start) | async-done | bytes 1048608 | tf_op jit(solution)/shard_map/all_to_all | solution.py:48
  42.0 1.4 reduce_sum.12
  43.4 3.1 %shard_map.171 = (bf16[2,768,256]{2,1,0:T(8,128)(2,1)S(1)}, bf16[2,768,256]{2,1,0:T(8,128)(2,1)S(1)}) custom-call(s32[6]{0:T(128)S(1)} %stack.59.where, bf16[1024,512]{1,0:T(8,128)(2,1)S(1)} %copy-done.1, bf16[1024,512]{1,0:T(8,128)(2,1)S(1)} %collective-permute-done.1.refs_1_, bf16[1024,512]{1,0:T(8,128)(2,1)} %collective-permute-done.refs_2_, ...), custom_call_target="tpu_custom_call" | custom-call | tf_op jit(solution)/shard_map/pallas_call | solution.py:103
  46.5 5.5 %collective-permute-start.2 = (bf16[2,768,256]{2,1,0:T(8,128)(2,1)S(1)}, bf16[2,768,256]{2,1,0:T(8,128)(2,1)S(1)}, u32[]{:S(2)}, u32[]{:S(2)}) collective-permute-start(bf16[2,768,256]{2,1,0:T(8,128)(2,1)S(1)} %get-tuple-element.47), channel_id=1, source_target_pairs={{0,8},{8,0},{1,9},{9,1},{64,72},{72,64},{65,73},{73,65},{2,10},{10... | collective-permute-start | bytes 2359304 | tf_op jit(solution)/shard_map/ppermute | solution.py:44
  52.0 0.4 collective-permute-done.3.refs_0_
  52.3 3.4 %shard_map.173 = (bf16[2,768,256]{2,1,0:T(8,128)(2,1)S(1)}, bf16[2,768,256]{2,1,0:T(8,128)(2,1)S(1)}) custom-call(s32[6]{0:T(128)S(1)} %stack.59.where, bf16[1024,512]{1,0:T(8,128)(2,1)S(1)} %copy-done.1, bf16[1024,512]{1,0:T(8,128)(2,1)S(1)} %collective-permute-done.1.refs_1_, bf16[1024,512]{1,0:T(8,128)(2,1)} %collective-permute-done.refs_2_, ...), custom_call_target="tpu_custom_call" | custom-call | tf_op jit(solution)/shard_map/pallas_call | solution.py:103
  55.8 1.6 collective-permute-start.7
  57.3 2.3 %shard_map.174 = (bf16[2,256,256]{2,1,0:T(8,128)(2,1)S(1)}, bf16[2,256,256]{2,1,0:T(8,128)(2,1)S(1)}) custom-call(s32[6]{0:T(128)S(1)} %stack.59.where, bf16[512,512]{1,0:T(8,128)(2,1)} %collective-permute-done.3.refs_0_, bf16[512,512]{1,0:T(8,128)(2,1)} %collective-permute-done.4.refs_1_, bf16[1024,512]{1,0:T(8,128)(2,1)} %collective-permute-done.6.refs_3_.refs_2_), custom_call_target="tpu_custom_call" | custom-call | tf_op jit(solution)/shard_map/pallas_call | solution.py:103
  59.7 0.1 collective-permute-start.8
  59.8 2.0 %shard_map.172 = (bf16[2,256,256]{2,1,0:T(8,128)(2,1)S(1)}, bf16[2,256,256]{2,1,0:T(8,128)(2,1)S(1)}) custom-call(s32[6]{0:T(128)S(1)} %stack.59.where, bf16[512,512]{1,0:T(8,128)(2,1)} %collective-permute-done.3.refs_0_, bf16[512,512]{1,0:T(8,128)(2,1)} %collective-permute-done.4.refs_1_, bf16[1024,512]{1,0:T(8,128)(2,1)S(1)} %copy-done.3), custom_call_target="tpu_custom_call" | custom-call | tf_op jit(solution)/shard_map/pallas_call | solution.py:103
  61.8 0.6 collective-permute-start.5
  62.3 1.2 collective-permute-done.5.refs_3_
  63.5 1.1 shard_map.175
  64.6 0.8 copy-done.6
  65.4 0.8 copy-done.15
  66.2 0.8 copy-done.16
  67.0 0.8 copy-done.17
  67.8 1.1 broadcast_in_dim.2
  68.8 4.9 %all-to-all-start.1 = ((bf16[8,128,512]{2,1,0:T(8,128)(2,1)}), bf16[8,128,512]{2,1,0:T(8,128)(2,1)S(1)}, u32[]{:S(2)}, u32[]{:S(2)}) async-start(bf16[8,128,512]{2,1,0:T(8,128)(2,1)} %broadcast_in_dim.2), calls=%async_computation.1 | async-start | bytes 2097152 | tf_op jit(solution)/shard_map/all_to_all | solution.py:48
  73.7 1.2 collective-permute-start.9
  74.9 1.5 collective-permute-start.10
  76.4 1.5 collective-permute-start.11
  77.9 11.5 %all-to-all-done.1 = bf16[8,128,512]{2,1,0:T(8,128)(2,1)S(1)} async-done(((bf16[8,128,512]{2,1,0:T(8,128)(2,1)}), bf16[8,128,512]{2,1,0:T(8,128)(2,1)S(1)}, u32[]{:S(2)}, u32[]{:S(2)}) %all-to-all-start.1) | async-done | bytes 1048608 | tf_op jit(solution)/shard_map/all_to_all | solution.py:48
  89.4 0.8 shard_map.177
  90.2 0.8 copy-done.4
  91.0 6.3 %all-to-all-start.2 = ((bf16[16,2,32,256]{3,2,1,0:T(8,128)(2,1)}), bf16[16,2,32,256]{3,2,1,0:T(8,128)(2,1)S(1)}, u32[]{:S(2)}, u32[]{:S(2)}) async-start(bf16[16,2,32,256]{3,2,1,0:T(8,128)(2,1)} %copy-done.4), calls=%async_computation.2 | async-start | bytes 1048576 | tf_op jit(solution)/shard_map/all_to_all | solution.py:413
  97.3 2.9 %collective-permute-done.11.refs_3_ = bf16[1024,256]{1,0:T(8,128)(2,1)} collective-permute-done((bf16[1024,256]{1,0:T(8,128)(2,1)}, bf16[1024,256]{1,0:T(8,128)(2,1)}, u32[]{:S(2)}, u32[]{:S(2)}) %collective-permute-start.11) | collective-permute-done | bytes 524320 | tf_op jit(solution)/shard_map/ppermute | solution.py:44
  100.3 1.0 copy-done.7
  101.3 2.3 %shard_map.176 = (bf16[256,256]{1,0:T(8,128)(2,1)}, bf16[256,256]{1,0:T(8,128)(2,1)}, bf16[256,256]{1,0:T(8,128)(2,1)}, bf16[256,256]{1,0:T(8,128)(2,1)S(1)}) custom-call(s32[6]{0:T(128)S(1)} %stack.59.where, bf16[1024,256]{1,0:T(8,128)(2,1)S(1)} %copy-done.7, bf16[1024,256]{1,0:T(8,128)(2,1)} %collective-permute-done.9.refs_1_, ...), custom_call_target="tpu_custom_call" | custom-call | tf_op jit(solution)/shard_map/pallas_call | solution.py:250
  103.6 1.6 collective-permute-start.12
  105.2 0.7 collective-permute-start.13
  105.9 5.8 %collective-permute-start.14 = (bf16[256,256]{1,0:T(8,128)(2,1)}, bf16[256,256]{1,0:T(8,128)(2,1)S(1)}, u32[]{:S(2)}, u32[]{:S(2)}) collective-permute-start(bf16[256,256]{1,0:T(8,128)(2,1)} %get-tuple-element.65), channel_id=1, source_target_pairs={{0,32},{8,40},{1,48},{9,56},{64,96},{72,104},{65,112},{73,120},{2,... | collective-permute-start | bytes 393224 | tf_op jit(solution)/shard_map/ppermute | solution.py:44
  111.7 0.4 collective-permute-start.15
  112.9 0.9 copy-done.12
  113.8 0.9 copy-done.13
  114.8 1.9 %shard_map.178 = (f32[2,4,32,256]{3,2,1,0:T(8,128)}, f32[2,4,32,256]{3,2,1,0:T(8,128)}, f32[2,4,32,256]{3,2,1,0:T(8,128)}, bf16[256,256]{1,0:T(8,128)(2,1)S(1)}) custom-call(s32[16]{0:T(128)S(1)} %copy-done.14, f32[2]{0:T(128)S(1)} %pad_maximum_fusion.2.fixes, bf16[16,2,32,256]{3,2,1,0:T(8,128)(2,1)S(1)} %all-to-all-done.2.got, ...), custom_call_target="tpu_custom_call" | custom-call | tf_op jit(solution)/shard_map/pallas_call | solution.py:224
  116.7 1.1 collective-permute-done.15.refs_3_
  117.8 2.2 %shard_map.179 = (f32[256,512]{1,0:T(8,128)}, f32[256,512]{1,0:T(8,128)}, f32[256,512]{1,0:T(8,128)}, bf16[768,256]{1,0:T(8,128)(2,1)S(1)}) custom-call(s32[6]{0:T(128)S(1)} %stack.59.where, f32[2]{0:T(128)S(1)} %pad_maximum_fusion.2.fixes, bf16[256,256]{1,0:T(8,128)(2,1)S(1)} %collective-permute-done.12.refs_0_, ...), custom_call_target="tpu_custom_call" | custom-call | tf_op jit(solution)/shard_map/pallas_call | solution.py:288
  120.0 4.9 %collective-permute-start.19 = (bf16[768,256]{1,0:T(8,128)(2,1)S(1)}, bf16[768,256]{1,0:T(8,128)(2,1)S(1)}, u32[]{:S(2)}, u32[]{:S(2)}) collective-permute-start(bf16[768,256]{1,0:T(8,128)(2,1)S(1)} %get-tuple-element.72), channel_id=1, source_target_pairs={{0,32},{8,40},{1,33},{9,41},{64,96},{72,104},{65,97},{73,105},{2,3... | collective-permute-start | bytes 1179656 | tf_op jit(solution)/shard_map/ppermute | solution.py:44
  124.9 2.9 %collective-permute-start.18 = (bf16[768,256]{1,0:T(8,128)(2,1)S(1)}, bf16[768,256]{1,0:T(8,128)(2,1)S(1)}, u32[]{:S(2)}, u32[]{:S(2)}) collective-permute-start(bf16[768,256]{1,0:T(8,128)(2,1)S(1)} %get-tuple-element.72), channel_id=1, source_target_pairs={{0,48},{8,56},{1,49},{9,57},{64,112},{72,120},{65,113},{73,121},{2... | collective-permute-start | bytes 1179656 | tf_op jit(solution)/shard_map/ppermute | solution.py:44
  127.8 4.4 %collective-permute-done.19 = bf16[768,256]{1,0:T(8,128)(2,1)S(1)} collective-permute-done((bf16[768,256]{1,0:T(8,128)(2,1)S(1)}, bf16[768,256]{1,0:T(8,128)(2,1)S(1)}, u32[]{:S(2)}, u32[]{:S(2)}) %collective-permute-start.19) | collective-permute-done | bytes 393248 | tf_op jit(solution)/shard_map/ppermute | solution.py:44
  132.2 1.9 %collective-permute-done.16 = bf16[768,256]{1,0:T(8,128)(2,1)S(1)} collective-permute-done((bf16[768,256]{1,0:T(8,128)(2,1)S(1)}, bf16[768,256]{1,0:T(8,128)(2,1)S(1)}, u32[]{:S(2)}, u32[]{:S(2)}) %collective-permute-start.16) | collective-permute-done | bytes 393248 | tf_op jit(solution)/shard_map/ppermute | solution.py:44
  134.1 3.7 %collective-permute-start.21 = (bf16[768,256]{1,0:T(8,128)(2,1)S(1)}, bf16[768,256]{1,0:T(8,128)(2,1)S(1)}, u32[]{:S(2)}, u32[]{:S(2)}) collective-permute-start(bf16[768,256]{1,0:T(8,128)(2,1)S(1)} %collective-permute-done.16), channel_id=1, source_target_pairs={{0,48},{8,56},{1,49},{9,57},{64,112},{72,120},{65,113},{73,121},{2... | collective-permute-start | bytes 1179656 | tf_op jit(solution)/shard_map/ppermute | solution.py:44
  137.8 6.9 %collective-permute-done.18 = bf16[768,256]{1,0:T(8,128)(2,1)S(1)} collective-permute-done((bf16[768,256]{1,0:T(8,128)(2,1)S(1)}, bf16[768,256]{1,0:T(8,128)(2,1)S(1)}, u32[]{:S(2)}, u32[]{:S(2)}) %collective-permute-start.18) | collective-permute-done | bytes 393248 | tf_op jit(solution)/shard_map/ppermute | solution.py:44
  144.7 0.2 pad_maximum_fusion.first
  144.9 3.7 %collective-permute-start.23 = (bf16[4,768,256]{2,1,0:T(8,128)(2,1)S(1)}, bf16[4,768,256]{2,1,0:T(8,128)(2,1)S(1)}, u32[]{:S(2)}, u32[]{:S(2)}) collective-permute-start(bf16[4,768,256]{2,1,0:T(8,128)(2,1)S(1)} %pad_maximum_fusion.first), channel_id=1, source_target_pairs={{0,8},{8,0},{1,9},{9,1},{64,72},{72,64},{65,73},{73,65},{2,10},{10... | collective-permute-start | bytes 4718600 | tf_op jit(solution)/shard_map/ppermute | solution.py:44
  148.6 4.6 %collective-permute-done.21 = bf16[768,256]{1,0:T(8,128)(2,1)S(1)} collective-permute-done((bf16[768,256]{1,0:T(8,128)(2,1)S(1)}, bf16[768,256]{1,0:T(8,128)(2,1)S(1)}, u32[]{:S(2)}, u32[]{:S(2)}) %collective-permute-start.21) | collective-permute-done | bytes 393248 | tf_op jit(solution)/shard_map/ppermute | solution.py:44
  153.1 0.2 pad_maximum_fusion.1.second
  153.3 1.6 %collective-permute-start.24 = (bf16[4,768,256]{2,1,0:T(8,128)(2,1)S(1)}, bf16[4,768,256]{2,1,0:T(8,128)(2,1)S(1)}, u32[]{:S(2)}, u32[]{:S(2)}) collective-permute-start(bf16[4,768,256]{2,1,0:T(8,128)(2,1)S(1)} %pad_maximum_fusion.1.second), channel_id=1, source_target_pairs={{0,8},{8,0},{1,9},{9,1},{64,72},{72,64},{65,73},{73,65},{2,10},{10... | collective-permute-start | bytes 4718600 | tf_op jit(solution)/shard_map/ppermute | solution.py:44
  155.0 3.0 %collective-permute-done.24.second_peer = bf16[4,768,256]{2,1,0:T(8,128)(2,1)S(1)} collective-permute-done((bf16[4,768,256]{2,1,0:T(8,128)(2,1)S(1)}, bf16[4,768,256]{2,1,0:T(8,128)(2,1)S(1)}, u32[]{:S(2)}, u32[]{:S(2)}) %collective-permute-start.24) | collective-permute-done | bytes 1572896 | tf_op jit(solution)/shard_map/ppermute | solution.py:44
  158.0 4.6 %shard_map.180 = (bf16[16,256,512]{2,1,0:T(8,128)(2,1)}, bf16[8,16,32,256]{3,2,1,0:T(8,128)(2,1)}) custom-call(s32[6]{0:T(128)S(1)} %stack.59.where, bf16[4,768,256]{2,1,0:T(8,128)(2,1)S(1)} %pad_maximum_fusion.first, bf16[4,768,256]{2,1,0:T(8,128)(2,1)S(1)} %pad_maximum_fusion.1.second, bf16[4,768,256]{2,1,0:T(8,128)(2,1)S(1)} %collective-permute-done.23.first_peer, ...), custom_call_target="tpu_custom_call" | custom-call | tf_op jit(solution)/shard_map/pallas_call | solution.py:326
  (48 shorter events, 0.2 us)
Async XLA Ops:
  0.6 25.8 %collective-permute-start.1 = (bf16[1024,512]{1,0:T(8,128)(2,1)}, bf16[1024,512]{1,0:T(8,128)(2,1)S(1)}, u32[]{:S(2)}, u32[]{:S(2)}) collective-permute-start(bf16[1024,512]{1,0:T(8,128)(2,1)} %act.3), channel_id=1, source_target_pairs={{0,6},{8,14},{1,7},{9,15},{64,70},{72,78},{65,71},{73,79},{2,0},{1... | collective-permute-start | bytes 3145736 | tf_op jit(solution)/shard_map/ppermute | solution.py:44
  4.3 26.4 %collective-permute-start = (bf16[1024,512]{1,0:T(8,128)(2,1)}, bf16[1024,512]{1,0:T(8,128)(2,1)}, u32[]{:S(2)}, u32[]{:S(2)}) collective-permute-start(bf16[1024,512]{1,0:T(8,128)(2,1)} %act.3), channel_id=1, source_target_pairs={{0,2},{8,10},{1,3},{9,11},{64,66},{72,74},{65,67},{73,75},{2,4},{1... | collective-permute-start | bytes 3145736 | tf_op jit(solution)/shard_map/ppermute | solution.py:44
  4.3 47.7 %collective-permute-start.6 = (bf16[1024,512]{1,0:T(8,128)(2,1)}, bf16[1024,512]{1,0:T(8,128)(2,1)}, u32[]{:S(2)}, u32[]{:S(2)}) collective-permute-start(bf16[1024,512]{1,0:T(8,128)(2,1)} %cot.3), channel_id=1, source_target_pairs={{0,1},{8,9},{1,0},{9,8},{64,65},{72,73},{65,64},{73,72},{2,3},{10,... | collective-permute-start | bytes 3145736 | tf_op jit(solution)/shard_map/ppermute | solution.py:44
  9.8 1.2 copy-start
  11.1 1.2 copy-start.2
  12.3 1.6 copy-start.5
  16.1 25.9 %all-to-all-start = ((bf16[8,128,512]{2,1,0:T(8,128)(2,1)}), bf16[8,128,512]{2,1,0:T(8,128)(2,1)}, u32[]{:S(2)}, u32[]{:S(2)}) async-start(bf16[8,128,512]{2,1,0:T(8,128)(2,1)} %bitcast.5), calls=%async_computation | async-start | bytes 2097152 | tf_op jit(solution)/shard_map/all_to_all | solution.py:48
  20.4 23.0 %copy-start.1 = (bf16[1024,512]{1,0:T(8,128)(2,1)S(1)}, bf16[1024,512]{1,0:T(8,128)(2,1)}, u32[]{:S(2)}) copy-start(bf16[1024,512]{1,0:T(8,128)(2,1)} %act.3) | copy-start | bytes 3145732
  20.4 23.0 %copy-start.3 = (bf16[1024,512]{1,0:T(8,128)(2,1)S(1)}, bf16[1024,512]{1,0:T(8,128)(2,1)}, u32[]{:S(2)}) copy-start(bf16[1024,512]{1,0:T(8,128)(2,1)} %cot.3) | copy-start | bytes 3145732
  27.2 24.7 %collective-permute-start.4 = (bf16[512,512]{1,0:T(8,128)(2,1)}, bf16[512,512]{1,0:T(8,128)(2,1)}, u32[]{:S(2)}, u32[]{:S(2)}) collective-permute-start(bf16[512,512]{1,0:T(8,128)(2,1)} %slice.9), channel_id=1, source_target_pairs={{0,6},{8,14},{1,7},{9,15},{64,70},{72,78},{65,71},{73,79},{2,0},{1... | collective-permute-start | bytes 1572872 | tf_op jit(solution)/shard_map/ppermute | solution.py:44
  32.5 19.8 %collective-permute-start.3 = (bf16[512,512]{1,0:T(8,128)(2,1)}, bf16[512,512]{1,0:T(8,128)(2,1)}, u32[]{:S(2)}, u32[]{:S(2)}) collective-permute-start(bf16[512,512]{1,0:T(8,128)(2,1)} %slice.8), channel_id=1, source_target_pairs={{0,2},{8,10},{1,3},{9,11},{64,66},{72,74},{65,67},{73,75},{2,4},{1... | collective-permute-start | bytes 1572872 | tf_op jit(solution)/shard_map/ppermute | solution.py:44
  46.5 17.0 %collective-permute-start.2 = (bf16[2,768,256]{2,1,0:T(8,128)(2,1)S(1)}, bf16[2,768,256]{2,1,0:T(8,128)(2,1)S(1)}, u32[]{:S(2)}, u32[]{:S(2)}) collective-permute-start(bf16[2,768,256]{2,1,0:T(8,128)(2,1)S(1)} %get-tuple-element.47), channel_id=1, source_target_pairs={{0,8},{8,0},{1,9},{9,1},{64,72},{72,64},{65,73},{73,65},{2,10},{10... | collective-permute-start | bytes 2359304 | tf_op jit(solution)/shard_map/ppermute | solution.py:44
  55.8 7.7 %collective-permute-start.7 = (bf16[2,768,256]{2,1,0:T(8,128)(2,1)S(1)}, bf16[2,768,256]{2,1,0:T(8,128)(2,1)S(1)}, u32[]{:S(2)}, u32[]{:S(2)}) collective-permute-start(bf16[2,768,256]{2,1,0:T(8,128)(2,1)S(1)} %get-tuple-element.52), channel_id=1, source_target_pairs={{0,8},{8,0},{1,9},{9,1},{64,72},{72,64},{65,73},{73,65},{2,10},{10... | collective-permute-start | bytes 2359304 | tf_op jit(solution)/shard_map/ppermute | solution.py:44
  59.7 2.7 %collective-permute-start.8 = (bf16[2,256,256]{2,1,0:T(8,128)(2,1)S(1)}, bf16[2,256,256]{2,1,0:T(8,128)(2,1)S(1)}, u32[]{:S(2)}, u32[]{:S(2)}) collective-permute-start(bf16[2,256,256]{2,1,0:T(8,128)(2,1)S(1)} %get-tuple-element.54), channel_id=1, source_target_pairs={{0,8},{8,0},{1,9},{9,1},{64,72},{72,64},{65,73},{73,65},{2,10},{10... | collective-permute-start | bytes 786440 | tf_op jit(solution)/shard_map/ppermute | solution.py:44
  61.8 1.7 %collective-permute-start.5 = (bf16[2,256,256]{2,1,0:T(8,128)(2,1)S(1)}, bf16[2,256,256]{2,1,0:T(8,128)(2,1)S(1)}, u32[]{:S(2)}, u32[]{:S(2)}) collective-permute-start(bf16[2,256,256]{2,1,0:T(8,128)(2,1)S(1)} %get-tuple-element.49), channel_id=1, source_target_pairs={{0,8},{8,0},{1,9},{9,1},{64,72},{72,64},{65,73},{73,65},{2,10},{10... | collective-permute-start | bytes 786440 | tf_op jit(solution)/shard_map/ppermute | solution.py:44
  64.6 0.8 copy-start.6
  65.4 0.8 copy-start.15
  66.2 0.8 copy-start.16
  67.0 0.8 copy-start.17
  68.8 20.6 %all-to-all-start.1 = ((bf16[8,128,512]{2,1,0:T(8,128)(2,1)}), bf16[8,128,512]{2,1,0:T(8,128)(2,1)S(1)}, u32[]{:S(2)}, u32[]{:S(2)}) async-start(bf16[8,128,512]{2,1,0:T(8,128)(2,1)} %broadcast_in_dim.2), calls=%async_computation.1 | async-start | bytes 2097152 | tf_op jit(solution)/shard_map/all_to_all | solution.py:48
  73.7 23.6 %collective-permute-start.9 = (bf16[1024,256]{1,0:T(8,128)(2,1)}, bf16[1024,256]{1,0:T(8,128)(2,1)}, u32[]{:S(2)}, u32[]{:S(2)}) collective-permute-start(bf16[1024,256]{1,0:T(8,128)(2,1)} %copy-done.17), channel_id=1, source_target_pairs={{0,16},{8,24},{1,17},{9,25},{64,80},{72,88},{65,81},{73,89},{2,18}... | collective-permute-start | bytes 1572872 | tf_op jit(solution)/shard_map/ppermute | solution.py:44
  74.9 22.4 %collective-permute-start.10 = (bf16[1024,256]{1,0:T(8,128)(2,1)}, bf16[1024,256]{1,0:T(8,128)(2,1)}, u32[]{:S(2)}, u32[]{:S(2)}) collective-permute-start(bf16[1024,256]{1,0:T(8,128)(2,1)} %copy-done.16), channel_id=1, source_target_pairs={{0,48},{8,56},{1,49},{9,57},{64,112},{72,120},{65,113},{73,121},{2... | collective-permute-start | bytes 1572872 | tf_op jit(solution)/shard_map/ppermute | solution.py:44
  76.4 23.9 %collective-permute-start.11 = (bf16[1024,256]{1,0:T(8,128)(2,1)}, bf16[1024,256]{1,0:T(8,128)(2,1)}, u32[]{:S(2)}, u32[]{:S(2)}) collective-permute-start(bf16[1024,256]{1,0:T(8,128)(2,1)} %copy-done.15), channel_id=1, source_target_pairs={{0,32},{8,40},{1,33},{9,41},{64,96},{72,104},{65,97},{73,105},{2,3... | collective-permute-start | bytes 1572872 | tf_op jit(solution)/shard_map/ppermute | solution.py:44
  89.4 23.4 %copy-start.11 = (f32[2,4,32,256]{3,2,1,0:T(8,128)S(1)}, f32[2,4,32,256]{3,2,1,0:T(8,128)}, u32[]{:S(2)}) copy-start(f32[2,4,32,256]{3,2,1,0:T(8,128)} %param.23) | copy-start | bytes 786436
  89.4 23.4 %copy-start.14 = (s32[16]{0:T(128)S(1)}, s32[16]{0:T(128)}, u32[]{:S(2)}) copy-start(s32[16]{0:T(128)} %regions.1) | copy-start | bytes 196
  90.2 0.8 copy-start.4
  91.0 26.8 %copy-start.8 = (f32[256,512]{1,0:T(8,128)S(1)}, f32[256,512]{1,0:T(8,128)}, u32[]{:S(2)}) copy-start(f32[256,512]{1,0:T(8,128)} %refs_4_.1) | copy-start | bytes 1572868
  91.0 26.8 %copy-start.9 = (f32[256,512]{1,0:T(8,128)S(1)}, f32[256,512]{1,0:T(8,128)}, u32[]{:S(2)}) copy-start(f32[256,512]{1,0:T(8,128)} %refs_5_.1) | copy-start | bytes 1572868
  91.0 21.9 %all-to-all-start.2 = ((bf16[16,2,32,256]{3,2,1,0:T(8,128)(2,1)}), bf16[16,2,32,256]{3,2,1,0:T(8,128)(2,1)S(1)}, u32[]{:S(2)}, u32[]{:S(2)}) async-start(bf16[16,2,32,256]{3,2,1,0:T(8,128)(2,1)} %copy-done.4), calls=%async_computation.2 | async-start | bytes 1048576 | tf_op jit(solution)/shard_map/all_to_all | solution.py:413
  100.3 1.0 copy-start.7
  101.3 16.5 %copy-start.10 = (f32[256,512]{1,0:T(8,128)S(1)}, f32[256,512]{1,0:T(8,128)}, u32[]{:S(2)}) copy-start(f32[256,512]{1,0:T(8,128)} %refs_6_.1) | copy-start | bytes 1572868
  103.6 13.1 %collective-permute-start.12 = (bf16[256,256]{1,0:T(8,128)(2,1)}, bf16[256,256]{1,0:T(8,128)(2,1)S(1)}, u32[]{:S(2)}, u32[]{:S(2)}) collective-permute-start(bf16[256,256]{1,0:T(8,128)(2,1)} %get-tuple-element.63), channel_id=1, source_target_pairs={{0,0},{8,8},{1,16},{9,24},{64,64},{72,72},{65,80},{73,88},{2,2},{1... | collective-permute-start | bytes 393224 | tf_op jit(solution)/shard_map/ppermute | solution.py:44
  105.2 11.5 %collective-permute-start.13 = (bf16[256,256]{1,0:T(8,128)(2,1)}, bf16[256,256]{1,0:T(8,128)(2,1)S(1)}, u32[]{:S(2)}, u32[]{:S(2)}) collective-permute-start(bf16[256,256]{1,0:T(8,128)(2,1)} %get-tuple-element.64), channel_id=1, source_target_pairs={{0,64},{8,72},{1,80},{9,88},{64,0},{72,8},{65,16},{73,24},{2,66},{... | collective-permute-start | bytes 393224 | tf_op jit(solution)/shard_map/ppermute | solution.py:44
  105.9 10.8 %collective-permute-start.14 = (bf16[256,256]{1,0:T(8,128)(2,1)}, bf16[256,256]{1,0:T(8,128)(2,1)S(1)}, u32[]{:S(2)}, u32[]{:S(2)}) collective-permute-start(bf16[256,256]{1,0:T(8,128)(2,1)} %get-tuple-element.65), channel_id=1, source_target_pairs={{0,32},{8,40},{1,48},{9,56},{64,96},{72,104},{65,112},{73,120},{2,... | collective-permute-start | bytes 393224 | tf_op jit(solution)/shard_map/ppermute | solution.py:44
  111.7 6.1 %collective-permute-start.15 = (bf16[256,256]{1,0:T(8,128)(2,1)S(1)}, bf16[256,256]{1,0:T(8,128)(2,1)S(1)}, u32[]{:S(2)}, u32[]{:S(2)}) collective-permute-start(bf16[256,256]{1,0:T(8,128)(2,1)S(1)} %get-tuple-element.66), channel_id=1, source_target_pairs={{0,96},{8,104},{1,112},{9,120},{64,32},{72,40},{65,48},{73,56},{2,... | collective-permute-start | bytes 393224 | tf_op jit(solution)/shard_map/ppermute | solution.py:44
  112.9 1.0 copy-start.12
  113.8 0.9 copy-start.13
  120.0 12.1 %collective-permute-start.19 = (bf16[768,256]{1,0:T(8,128)(2,1)S(1)}, bf16[768,256]{1,0:T(8,128)(2,1)S(1)}, u32[]{:S(2)}, u32[]{:S(2)}) collective-permute-start(bf16[768,256]{1,0:T(8,128)(2,1)S(1)} %get-tuple-element.72), channel_id=1, source_target_pairs={{0,32},{8,40},{1,33},{9,41},{64,96},{72,104},{65,97},{73,105},{2,3... | collective-permute-start | bytes 1179656 | tf_op jit(solution)/shard_map/ppermute | solution.py:44
  124.9 9.1 %collective-permute-start.16 = (bf16[768,256]{1,0:T(8,128)(2,1)S(1)}, bf16[768,256]{1,0:T(8,128)(2,1)S(1)}, u32[]{:S(2)}, u32[]{:S(2)}) collective-permute-start(bf16[768,256]{1,0:T(8,128)(2,1)S(1)} %get-tuple-element.72), channel_id=1, source_target_pairs={{0,64},{8,72},{1,65},{9,73},{64,0},{72,8},{65,1},{73,9},{2,66},{10... | collective-permute-start | bytes 1179656 | tf_op jit(solution)/shard_map/ppermute | solution.py:44
  124.9 19.8 %collective-permute-start.18 = (bf16[768,256]{1,0:T(8,128)(2,1)S(1)}, bf16[768,256]{1,0:T(8,128)(2,1)S(1)}, u32[]{:S(2)}, u32[]{:S(2)}) collective-permute-start(bf16[768,256]{1,0:T(8,128)(2,1)S(1)} %get-tuple-element.72), channel_id=1, source_target_pairs={{0,48},{8,56},{1,49},{9,57},{64,112},{72,120},{65,113},{73,121},{2... | collective-permute-start | bytes 1179656 | tf_op jit(solution)/shard_map/ppermute | solution.py:44
  127.8 16.9 %collective-permute-start.17 = (bf16[768,256]{1,0:T(8,128)(2,1)S(1)}, bf16[768,256]{1,0:T(8,128)(2,1)S(1)}, u32[]{:S(2)}, u32[]{:S(2)}) collective-permute-start(bf16[768,256]{1,0:T(8,128)(2,1)S(1)} %get-tuple-element.72), channel_id=1, source_target_pairs={{0,16},{8,24},{1,17},{9,25},{64,80},{72,88},{65,81},{73,89},{2,18}... | collective-permute-start | bytes 1179656 | tf_op jit(solution)/shard_map/ppermute | solution.py:44
  132.2 16.4 %collective-permute-start.22 = (bf16[768,256]{1,0:T(8,128)(2,1)S(1)}, bf16[768,256]{1,0:T(8,128)(2,1)S(1)}, u32[]{:S(2)}, u32[]{:S(2)}) collective-permute-start(bf16[768,256]{1,0:T(8,128)(2,1)S(1)} %collective-permute-done.19), channel_id=1, source_target_pairs={{0,64},{8,72},{1,65},{9,73},{64,0},{72,8},{65,1},{73,9},{2,66},{10... | collective-permute-start | bytes 1179656 | tf_op jit(solution)/shard_map/ppermute | solution.py:44
  134.1 19.1 %collective-permute-start.21 = (bf16[768,256]{1,0:T(8,128)(2,1)S(1)}, bf16[768,256]{1,0:T(8,128)(2,1)S(1)}, u32[]{:S(2)}, u32[]{:S(2)}) collective-permute-start(bf16[768,256]{1,0:T(8,128)(2,1)S(1)} %collective-permute-done.16), channel_id=1, source_target_pairs={{0,48},{8,56},{1,49},{9,57},{64,112},{72,120},{65,113},{73,121},{2... | collective-permute-start | bytes 1179656 | tf_op jit(solution)/shard_map/ppermute | solution.py:44
  137.8 15.3 %collective-permute-start.20 = (bf16[768,256]{1,0:T(8,128)(2,1)S(1)}, bf16[768,256]{1,0:T(8,128)(2,1)S(1)}, u32[]{:S(2)}, u32[]{:S(2)}) collective-permute-start(bf16[768,256]{1,0:T(8,128)(2,1)S(1)} %collective-permute-done.16), channel_id=1, source_target_pairs={{0,16},{8,24},{1,17},{9,25},{64,80},{72,88},{65,81},{73,89},{2,18}... | collective-permute-start | bytes 1179656 | tf_op jit(solution)/shard_map/ppermute | solution.py:44
  144.9 10.1 %collective-permute-start.23 = (bf16[4,768,256]{2,1,0:T(8,128)(2,1)S(1)}, bf16[4,768,256]{2,1,0:T(8,128)(2,1)S(1)}, u32[]{:S(2)}, u32[]{:S(2)}) collective-permute-start(bf16[4,768,256]{2,1,0:T(8,128)(2,1)S(1)} %pad_maximum_fusion.first), channel_id=1, source_target_pairs={{0,8},{8,0},{1,9},{9,1},{64,72},{72,64},{65,73},{73,65},{2,10},{10... | collective-permute-start | bytes 4718600 | tf_op jit(solution)/shard_map/ppermute | solution.py:44
  153.3 4.7 %collective-permute-start.24 = (bf16[4,768,256]{2,1,0:T(8,128)(2,1)S(1)}, bf16[4,768,256]{2,1,0:T(8,128)(2,1)S(1)}, u32[]{:S(2)}, u32[]{:S(2)}) collective-permute-start(bf16[4,768,256]{2,1,0:T(8,128)(2,1)S(1)} %pad_maximum_fusion.1.second), channel_id=1, source_target_pairs={{0,8},{8,0},{1,9},{9,1},{64,72},{72,64},{65,73},{73,65},{2,10},{10... | collective-permute-start | bytes 4718600 | tf_op jit(solution)/shard_map/ppermute | solution.py:44

commit v4 on v3

--- a/solution.py
+++ b/solution.py
@@ -137,20 +137,26 @@
     )(here, *parts)
 
 
-def low_kernel(scales, where, act, cot, adapters, out):
-    rank = adapters.shape[3]
-    down = jnp.dot(act[...], adapters[0, 0], preferred_element_type=F32) * scales[0]
-    up = jnp.dot(cot[...], adapters[1, 0], preferred_element_type=F32) * scales[1]
-    out[:, :rank] = down.astype(BF16)
-    out[:, rank:] = up.astype(BF16)
+def low_kernel(scales, where, act, cot, adapters, keep, give):
+    rows, rank = keep.shape[0], adapters.shape[3]
+    for out, h in ((keep, where[ZH]), (give, 1 - where[ZH])):
+        part = pl.ds(pl.multiple_of(h * rows, rows), rows)
+        down = jnp.dot(act[part, :], adapters[0, 0], preferred_element_type=F32) * scales[0]
+        up = jnp.dot(cot[part, :], adapters[1, 0], preferred_element_type=F32) * scales[1]
+        out[:, :rank] = down.astype(out.dtype)
+        out[:, rank:] = up.astype(out.dtype)
 
 
 def low_parts(here, act, cot, adapters, scales):
-    rank = adapters.shape[3]
+    rows, rank = act.shape[0] // 2, adapters.shape[3]
     whole = pl.BlockSpec(act.shape, lambda i, where: (0, 0))
+    out = pl.BlockSpec((rows, 2 * rank), lambda i, where: (0, 0))
     return pl.pallas_call(
         functools.partial(low_kernel, scales),
-        out_shape=jax.ShapeDtypeStruct((act.shape[0], 2 * rank), BF16),
+        out_shape=(
+            jax.ShapeDtypeStruct((rows, 2 * rank), F32),
+            jax.ShapeDtypeStruct((rows, 2 * rank), BF16),
+        ),
         grid_spec=pltpu.PrefetchScalarGridSpec(
             num_scalar_prefetch=1,
             grid=(1,),
@@ -161,14 +167,52 @@
                     (2, 1) + adapters.shape[2:], lambda i, where: (0, where[REGION], 0, 0)
                 ),
             ],
-            out_specs=pl.BlockSpec((act.shape[0], 2 * rank), lambda i, where: (0, 0)),
+            out_specs=(out, out),
         ),
         compiler_params=pltpu.CompilerParams(vmem_limit_bytes=32 * 1024 * 1024),
     )(here, act, cot, adapters)
 
 
-def grads_kernel(scales, low, act, cot, out):
-    rank = out.shape[3]
+def low_add_kernel(keep, got, out):
+    out[...] = (keep[...] + got[...].astype(F32)).astype(BF16)
+
+
+def low_add(keep, got):
+    vmem = pl.BlockSpec(memory_space=pltpu.VMEM)
+    return pl.pallas_call(
+        low_add_kernel,
+        out_shape=jax.ShapeDtypeStruct(keep.shape, BF16),
+        in_specs=[vmem, vmem],
+        out_specs=vmem,
+        compiler_params=pltpu.CompilerParams(vmem_limit_bytes=16 * 1024 * 1024),
+    )(keep, got)
+
+
+def sum_kernel(parts, out):
+    total = parts[0].astype(F32)
+    for i in range(1, parts.shape[0]):
+        total = total + parts[i].astype(F32)
+    out[...] = total.astype(BF16)
+
+
+def sum_parts(parts):
+    vmem = pl.BlockSpec(memory_space=pltpu.VMEM)
+    return pl.pallas_call(
+        sum_kernel,
+        out_shape=jax.ShapeDtypeStruct(parts.shape[1:], BF16),
+        in_specs=[vmem],
+        out_specs=vmem,
+        compiler_params=pltpu.CompilerParams(vmem_limit_bytes=16 * 1024 * 1024),
+    )(parts)
+
+
+def grads_kernel(scales, where, *refs):
+    pieces, (act, cot, out, low) = refs[:4], refs[4:]
+    rows, rank = pieces[0].shape[1], out.shape[3]
+    for k, piece in enumerate(pieces):
+        for other in range(2):
+            place = 4 * (where[ZH] ^ other) + ((where[Y] - k + 4) & 3)
+            low[pl.ds(pl.multiple_of(place * rows, rows), rows), :] = piece[other]
     for side, source, start in ((0, act, rank), (1, cot, 0)):
         total = contract_rows(source[...], low[:, pl.ds(start, rank)])
         total = (total * scales[side]).astype(BF16)
@@ -176,16 +220,17 @@
             out[f, side] = total[f * out.shape[2] : (f + 1) * out.shape[2]]
 
 
-def adapter_grads(low, act, cot, scales, count):
-    rank = low.shape[1] // 2
+def adapter_grads(here, pieces, act, cot, scales, count):
+    rank = pieces[0].shape[2] // 2
     vmem = pl.BlockSpec(memory_space=pltpu.VMEM)
     return pl.pallas_call(
         functools.partial(grads_kernel, scales),
         out_shape=jax.ShapeDtypeStruct((count, 2, act.shape[1] // count, rank), BF16),
-        in_specs=[vmem] * 3,
+        in_specs=[pl.BlockSpec(memory_space=pltpu.SMEM)] + [vmem] * 6,
         out_specs=vmem,
+        scratch_shapes=[pltpu.VMEM((act.shape[0], 2 * rank), BF16)],
         compiler_params=pltpu.CompilerParams(vmem_limit_bytes=32 * 1024 * 1024),
-    )(low, act, cot)
+    )(here, *pieces, act, cot)
 
 
 def adamw_values(param, moment, second, grad, first_fix, second_fix):
@@ -294,52 +339,47 @@
     )(here, fixes, *terms, param, moment, second, extra)
 
 
-def place_kernel(where, first, second, first_peer, second_peer, weight, adapter):
-    chip, c = pl.program_id(0), where[CORE]
-    dx, dz = (chip - where[X]) & 3, (chip >> 2) ^ where[ZL]
-    near_slot = jnp.where(dx == 0, dz, jnp.where(dx == 3, 2, 3))
-    far_slot = jnp.where(dx == 3, 5, jnp.where(dx == 1, 6, 7))
-    slot = jnp.where(
-        dz == 0, jnp.where(dx == 2, 4, near_slot), jnp.where(dx == 0, dz, far_slot)
-    )
+def place_kernel(slots, where, own, peer, *refs):
+    weight, adapter = refs[-2:]
     rows, wide = weight.shape[1], weight.shape[2] // 2
-
-    def put(core, block):
+    for core, source in ((where[CORE], own), (1 - where[CORE], peer)):
+        block = source[pl.program_id(0)]
         weight[core, :, :wide] = block[:rows]
         weight[core, :, wide:] = block[rows : 2 * rows]
         adapter[:, core] = block[2 * rows :].reshape(adapter.shape[0:1] + adapter.shape[2:])
 
-    for here, low, high in ((c, first, second), (1 - c, first_peer, second_peer)):
-
-        @pl.when(slot < 4)
-        def _():
-            put(here, low[jnp.minimum(slot, 3)])
-
-        @pl.when(slot >= 4)
-        def _():
-            put(here, high[jnp.maximum(slot - 4, 0)])
-
-
-def place_blocks(here, arrays, rows, groups):
-    wide = arrays[0].shape[2]
-    deep = (arrays[0].shape[1] - 2 * rows) // groups
-    return pl.pallas_call(
-        place_kernel,
-        out_shape=(
-            jax.ShapeDtypeStruct((16, rows, 2 * wide), BF16),
-            jax.ShapeDtypeStruct((groups, 16, deep, wide), BF16),
-        ),
+
+def place_blocks(here, slots, own, peer, rows, groups, outs):
+    wide = own.shape[2]
+    deep = (own.shape[1] - 2 * rows) // groups
+
+    def chip(i, where):
+        dx, dz = (functools.reduce(lambda rest, s: jnp.where(i == s[0], s[1], rest), enumerate(axis), 0) for axis in zip(*slots))
+        return ((where[ZL] ^ dz) << 2) + ((where[X] + dx) & 3)
+
+    def block(i, where):
+        return (0, 0, 0)
+
+    shapes = (
+        jax.ShapeDtypeStruct((16, rows, 2 * wide), BF16),
+        jax.ShapeDtypeStruct((groups, 16, deep, wide), BF16),
+    )
+    return pl.pallas_call(
+        functools.partial(place_kernel, slots),
+        out_shape=shapes,
         grid_spec=pltpu.PrefetchScalarGridSpec(
             num_scalar_prefetch=1,
-            grid=(8,),
-            in_specs=[pl.BlockSpec(array.shape, lambda i, where: (0, 0, 0)) for array in arrays],
+            grid=(len(slots),),
+            in_specs=[pl.BlockSpec(own.shape, block), pl.BlockSpec(own.shape, block)]
+            + [pl.BlockSpec(memory_space=pl.ANY)] * len(outs),
             out_specs=(
-                pl.BlockSpec((2, rows, 2 * wide), lambda i, where: (i, 0, 0)),
-                pl.BlockSpec((groups, 2, deep, wide), lambda i, where: (0, i, 0, 0)),
+                pl.BlockSpec((2, rows, 2 * wide), lambda i, where: (chip(i, where), 0, 0)),
+                pl.BlockSpec((groups, 2, deep, wide), lambda i, where: (0, chip(i, where), 0, 0)),
             ),
         ),
-        compiler_params=pltpu.CompilerParams(vmem_limit_bytes=40 * 1024 * 1024),
-    )(here, *arrays)
+        input_output_aliases={3: 0, 4: 1} if outs else {},
+        compiler_params=pltpu.CompilerParams(vmem_limit_bytes=24 * 1024 * 1024),
+    )(here, own, peer, *outs)
 
 
 def shards(
@@ -377,37 +417,42 @@
         1.0 - jnp.power(F32(beta_second), step_float),
     ])
 
+    low_keep, low_give = low_parts(
+        here, activations, cotangent, adapter_copy, (inv_width, inv_rank)
+    )
+    low_got = move(low_give, other_zh)
+
     middle = tok_dev // 2
     back = move(activations, along_y(1))
     ahead = move(activations, along_y(-1))
-    cot_zh = move(cotangent, other_zh)
-    far_first = move(back[:middle], along_y(1))
-    far_second = move(ahead[middle:], along_y(-1))
-
-    low = low_parts(here, activations, cotangent, adapter_copy, (inv_width, inv_rank))
-    low = swap_among(low.reshape(tp_count, tok_dev // tp_count, 2 * rank), "tp", None)
-    low_sum = jnp.sum(low.astype(F32), axis=0).astype(BF16)
+    low_got, cot_give, back_half, ahead_half = lax.optimization_barrier(
+        (low_got, cotangent, back[:middle], ahead[middle:])
+    )
+    cot_zh = move(cot_give, other_zh)
+    far_first = move(back_half, along_y(1))
+    far_second = move(ahead_half, along_y(-1))
+
+    low = low_add(low_keep, low_got).reshape(4, tok_dev // 8, 2 * rank)
+    low_sum = sum_parts(swap_among(low, "tp", Y_GROUPS))
 
     def swapped(acts, cot):
         keep, give = partials(here, acts, cot)
         return [keep, move(give, other_core)]
 
-    low_sum, back, ahead = lax.optimization_barrier((low_sum, back, ahead))
-    near_acts = [[activations], [ahead], [back]]
-    parts = swapped(near_acts, cotangent)
-    far_acts = [[far_first, far_second]]
-    far_first, far_second, cot_zh = lax.optimization_barrier((far_first, far_second, cot_zh))
-    parts += swapped(far_acts, cotangent)
+    low_sum, back, ahead, far_first, far_second = lax.optimization_barrier(
+        (low_sum, back, ahead, far_first, far_second)
+    )
+    low_both = jnp.stack([low_sum, move(low_sum, other_zh)])
+    near_acts, far_acts = [[activations], [ahead], [back]], [[far_first, far_second]]
+    parts = swapped(near_acts, cotangent) + swapped(far_acts, cotangent)
     parts += swapped(near_acts, cot_zh) + swapped(far_acts, cot_zh)
     blocks = add_blocks(here, parts)
-    low_sum, *blocks = lax.optimization_barrier((low_sum, *blocks))
-    low_all = swap_among(jnp.broadcast_to(low_sum[None], low.shape), "tp", None)
+    low_pieces = [low_both] + [move(low_both, along_y(k)) for k in (1, 2, 3)]
     blocks = [blocks[0]] + [move(blocks[k], along_x(k)) for k in (1, 3, 2)]
     blocks = pick_blocks(here, blocks)
-    low_all = low_all.reshape(tok_dev, 2 * rank)
 
     parts = adapter_grads(
-        low_all, activations, cotangent,
+        here, low_pieces, activations, cotangent,
         (inv_width * grad_scale, inv_rank * grad_scale), fsdp_count,
     )
     got = lax.all_to_all(parts, "fsdp", 0, 0)
@@ -431,14 +476,17 @@
         move(from_far, other_zl),
     ])
 
-    weight_next, adapter_next = place_blocks(
-        here,
-        [first, second, move(first, other_core), move(second, other_core)],
-        new_weight.shape[0],
-        2 * region_count,
-    )
-    weight_next = weight_next.reshape(width, -1)
-    adapter_next = adapter_next.reshape(adapter_copy.shape)
+    outs = ()
+    for slots, blocks in (
+        (((0, 0), (0, 1), (-1, 0), (1, 0)), first),
+        (((2, 0), (-1, 1), (1, 1), (2, 1)), second),
+    ):
+        outs = place_blocks(
+            here, slots, blocks, move(blocks, other_core), new_weight.shape[0],
+            2 * region_count, outs,
+        )
+    weight_next = outs[0].reshape(width, -1)
+    adapter_next = outs[1].reshape(adapter_copy.shape)
     return (
         new_weight,
         new_weight_moment,

time: 163 us -> 153 us (0.939)
  waiting for transfers between devices: 53.3 us -> 35.8 us
  blocking collectives: 0 us -> 14.5 us
  local copies, waits for them, and re-layouts: 16.7 us -> 6.77 us
  starting transfers between devices: 63.3 us -> 65.5 us
    all_to_all x2 -> x0, waiting for transfers between devices: 21 us -> none  [swap_among(): return lax.all_to_all(array, axis, 0, 0, axis_index_groups=groups)]
    all_to_all x0 -> x1, blocking collectives: none -> 14.5 us  [swap_among(): return lax.all_to_all(array, axis, 0, 0, axis_index_groups=groups)]
    ppermute x25 -> x30, starting transfers between devices: 47.9 us -> 59.9 us  [move(): return lax.ppermute(array, AXES, pairs)]
    all_to_all x2 -> x0, starting transfers between devices: 9.12 us -> none  [swap_among(): return lax.all_to_all(array, axis, 0, 0, axis_index_groups=groups)]
    unnamed x36 -> x20, local copies, waits for them, and re-layouts: 11 us -> 4.73 us
    ppermute x25 -> x30, waiting for transfers between devices: 32.3 us -> 35.8 us  [move(): return lax.ppermute(array, AXES, pairs)]
    slice x2, local copies, waits for them, and re-layouts: 2.7 us -> 0.07 us  [the longest x1 0.03 us: shards(): back[:middle]]
    pallas_call x1, Pallas kernels: 0.75 us -> 2.84 us  [adapter_grads(): pl.pallas_call(functools.partial(grads_kernel, scales), out_shape=jax.Sha...]
  transfers between devices with their start and end apart: 28 -> 31, of which waited for: 12 -> 10; matrix products, arithmetic and copies ran while one was open for 4% -> 2% of each run, Pallas kernels for 11% -> 15%
where the time goes in v4:
time: 153 us; the launch traced here: 152 us
  starting transfers between devices  65.5 us (43%)
  waiting for transfers between devices  35.8 us (23%)
  Pallas kernels  27.4 us (18%)
  blocking collectives  14.5 us (9%)
  local copies, waits for them, and re-layouts  6.77 us (4%)
  between operations  1.55 us (1%)
    ppermute x30, starting transfers between devices, move(): return lax.ppermute(array, AXES, pairs)  59.9 us
    ppermute x30, waiting for transfers between devices, move(): return lax.ppermute(array, AXES, pairs)  35.8 us
    all_to_all x1, blocking collectives, swap_among(): return lax.all_to_all(array, axis, 0, 0, axis_index_groups=groups)  14.5 us
    pallas_call x4, Pallas kernels, partials(): pl.pallas_call(functools.partial(partials_kernel, counts), out_shape=(jax...  8.84 us
    all_to_all x1, starting transfers between devices, shards(): got = lax.all_to_all(parts, 'fsdp', 0, 0)  5.61 us
    pallas_call x2, Pallas kernels, place_blocks(): pl.pallas_call(functools.partial(place_kernel, slots), out_shape=shapes,...  5.41 us
    unnamed x20, local copies, waits for them, and re-layouts  4.73 us
  transfers between devices with their start and end apart: 31, of which 10 were waited for; matrix products, arithmetic and copies ran while one was open for 2% of the time, Pallas kernels for 15%

profile of v4, /device:TPU:1, one launch (start us, length us, event | category | flops | bytes accessed | tf_op | source)
XLA Modules:
  0.0 152.0 jit_solution(3199000291035604072)
XLA Ops:
  0.6 3.6 %collective-permute-start.2 = (bf16[1024,512]{1,0:T(8,128)(2,1)}, bf16[1024,512]{1,0:T(8,128)(2,1)S(1)}, u32[]{:S(2)}, u32[]{:S(2)}) collective-permute-start(bf16[1024,512]{1,0:T(8,128)(2,1)} %refs_4_.2), channel_id=1, source_target_pairs={{0,6},{8,14},{1,7},{9,15},{64,70},{72,78},{65,71},{73,79},{2,0},{1... | collective-permute-start | bytes 3145736 | tf_op jit(solution)/shard_map/ppermute | solution.py:44
  4.3 1.2 dynamic_slice.4
  5.5 0.7 stack.68.where
  6.2 1.2 copy-done
  7.5 1.6 %copy-done.2 = bf16[2,4,512,256]{3,2,1,0:T(8,128)(2,1)S(1)} copy-done((bf16[2,4,512,256]{3,2,1,0:T(8,128)(2,1)S(1)}, bf16[2,4,512,256]{3,2,1,0:T(8,128)(2,1)}, u32[]{:S(2)}) %copy-start.2) | copy-done | bytes 2097176
  9.1 2.5 %shard_map.170 = (f32[512,512]{1,0:T(8,128)S(1)}, bf16[512,512]{1,0:T(8,128)(2,1)S(1)}) custom-call(s32[6]{0:T(128)S(1)} %stack.68.where, bf16[1024,512]{1,0:T(8,128)(2,1)S(1)} %copy-done, bf16[1024,512]{1,0:T(8,128)(2,1)} %refs_5_.2, bf16[2,4,512,256]{3,2,1,0:T(8,128)(2,1)S(1)} %copy-done.2), custom_call_target="tpu_custom_call" | custom-call | tf_op jit(solution)/shard_map/pallas_call | solution.py:154
  11.5 3.7 %collective-permute-start = (bf16[512,512]{1,0:T(8,128)(2,1)S(1)}, bf16[512,512]{1,0:T(8,128)(2,1)S(1)}, u32[]{:S(2)}, u32[]{:S(2)}) collective-permute-start(bf16[512,512]{1,0:T(8,128)(2,1)S(1)} %get-tuple-element.48), channel_id=1, source_target_pairs={{0,1},{8,9},{1,0},{9,8},{64,65},{72,73},{65,64},{73,72},{2,3},{10,... | collective-permute-start | bytes 1572872 | tf_op jit(solution)/shard_map/ppermute | solution.py:44
  15.2 11.2 %collective-permute-done.2.refs_1_ = bf16[1024,512]{1,0:T(8,128)(2,1)S(1)} collective-permute-done((bf16[1024,512]{1,0:T(8,128)(2,1)}, bf16[1024,512]{1,0:T(8,128)(2,1)S(1)}, u32[]{:S(2)}, u32[]{:S(2)}) %collective-permute-start.2) | collective-permute-done | bytes 1048608 | tf_op jit(solution)/shard_map/ppermute | solution.py:44
  26.4 2.9 %collective-permute-done.1.refs_2_ = bf16[1024,512]{1,0:T(8,128)(2,1)S(1)} collective-permute-done((bf16[1024,512]{1,0:T(8,128)(2,1)}, bf16[1024,512]{1,0:T(8,128)(2,1)S(1)}, u32[]{:S(2)}, u32[]{:S(2)}) %collective-permute-start.1) | collective-permute-done | bytes 1048608 | tf_op jit(solution)/shard_map/ppermute | solution.py:44
  29.4 3.7 %collective-permute-start.7 = (bf16[1024,512]{1,0:T(8,128)(2,1)}, bf16[1024,512]{1,0:T(8,128)(2,1)S(1)}, u32[]{:S(2)}, u32[]{:S(2)}) collective-permute-start(bf16[1024,512]{1,0:T(8,128)(2,1)} %refs_5_.2), channel_id=1, source_target_pairs={{0,1},{8,9},{1,0},{9,8},{64,65},{72,73},{65,64},{73,72},{2,3},{10,... | collective-permute-start | bytes 3145736 | tf_op jit(solution)/shard_map/ppermute | solution.py:44
  33.1 2.7 %collective-permute-start.4 = (bf16[512,512]{1,0:T(8,128)(2,1)S(1)}, bf16[512,512]{1,0:T(8,128)(2,1)S(1)}, u32[]{:S(2)}, u32[]{:S(2)}) collective-permute-start(bf16[512,512]{1,0:T(8,128)(2,1)S(1)} %slice.9), channel_id=1, source_target_pairs={{0,6},{8,14},{1,7},{9,15},{64,70},{72,78},{65,71},{73,79},{2,0},{1... | collective-permute-start | bytes 1572872 | tf_op jit(solution)/shard_map/ppermute | solution.py:44
  35.8 0.1 shard_map.171
  35.9 14.5 %all_to_all.10.parts = bf16[4,128,512]{2,1,0:T(8,128)(2,1)S(1)} all-to-all(bf16[4,128,512]{2,1,0:T(8,128)(2,1)S(1)} %bitcast.18), channel_id=1, replica_groups={{0,2,4,6},{1,3,5,7},{8,10,12,14},{9,11,13,15},{16,18,20,22},{17,19,21,2..., dimensions={0} | all-to-all | bytes 1048576 | tf_op jit(solution)/shard_map/all_to_all | solution.py:48
  50.4 0.1 shard_map.172
  50.5 3.1 %shard_map.173 = (bf16[2,768,256]{2,1,0:T(8,128)(2,1)S(1)}, bf16[2,768,256]{2,1,0:T(8,128)(2,1)S(1)}) custom-call(s32[6]{0:T(128)S(1)} %stack.68.where, bf16[1024,512]{1,0:T(8,128)(2,1)S(1)} %copy-done.1, bf16[1024,512]{1,0:T(8,128)(2,1)S(1)} %collective-permute-done.2.refs_1_, bf16[1024,512]{1,0:T(8,128)(2,1)S(1)} %collective-permute-done.1.refs_2_, ...), custom_call_target="tpu_custom_call" | custom-call | tf_op jit(solution)/shard_map/pallas_call | solution.py:103
  53.6 3.9 %collective-permute-start.5 = (bf16[2,768,256]{2,1,0:T(8,128)(2,1)S(1)}, bf16[2,768,256]{2,1,0:T(8,128)(2,1)S(1)}, u32[]{:S(2)}, u32[]{:S(2)}) collective-permute-start(bf16[2,768,256]{2,1,0:T(8,128)(2,1)S(1)} %get-tuple-element.55), channel_id=1, source_target_pairs={{0,8},{8,0},{1,9},{9,1},{64,72},{72,64},{65,73},{73,65},{2,10},{10... | collective-permute-start | bytes 2359304 | tf_op jit(solution)/shard_map/ppermute | solution.py:44
  57.6 2.4 %shard_map.175 = (bf16[2,768,256]{2,1,0:T(8,128)(2,1)S(1)}, bf16[2,768,256]{2,1,0:T(8,128)(2,1)S(1)}) custom-call(s32[6]{0:T(128)S(1)} %stack.68.where, bf16[1024,512]{1,0:T(8,128)(2,1)S(1)} %copy-done.1, bf16[1024,512]{1,0:T(8,128)(2,1)S(1)} %collective-permute-done.2.refs_1_, bf16[1024,512]{1,0:T(8,128)(2,1)S(1)} %collective-permute-done.1.refs_2_, ...), custom_call_target="tpu_custom_call" | custom-call | tf_op jit(solution)/shard_map/pallas_call | solution.py:103
  60.0 0.1 collective-permute-start.8
  60.1 2.8 %collective-permute-start.17 = (bf16[128,512]{1,0:T(8,128)(2,1)S(1)}, bf16[128,512]{1,0:T(8,128)(2,1)S(1)}, u32[]{:S(2)}, u32[]{:S(2)}) collective-permute-start(bf16[128,512]{1,0:T(8,128)(2,1)S(1)} %shard_map.172), channel_id=1, source_target_pairs={{0,1},{8,9},{1,0},{9,8},{64,65},{72,73},{65,64},{73,72},{2,3},{10,... | collective-permute-start | bytes 393224 | tf_op jit(solution)/shard_map/ppermute | solution.py:44
  62.9 2.0 %shard_map.174 = (bf16[2,256,256]{2,1,0:T(8,128)(2,1)S(1)}, bf16[2,256,256]{2,1,0:T(8,128)(2,1)S(1)}) custom-call(s32[6]{0:T(128)S(1)} %stack.68.where, bf16[512,512]{1,0:T(8,128)(2,1)S(1)} %collective-permute-done.3.refs_0_, bf16[512,512]{1,0:T(8,128)(2,1)S(1)} %collective-permute-done.4.refs_1_, bf16[1024,512]{1,0:T(8,128)(2,1)} %refs_5_.2), custom_call_target="tpu_custom_call" | custom-call | tf_op jit(solution)/shard_map/pallas_call | solution.py:103
  64.9 0.4 collective-permute-start.6
  65.4 1.3 shard_map.176
  66.7 0.2 collective-permute-start.9
  67.0 2.2 %collective-permute-start.20 = (bf16[2,128,512]{2,1,0:T(8,128)(2,1)S(1)}, bf16[2,128,512]{2,1,0:T(8,128)(2,1)S(1)}, u32[]{:S(2)}, u32[]{:S(2)}) collective-permute-start(bf16[2,128,512]{2,1,0:T(8,128)(2,1)S(1)} %pad_maximum_fusion.2.refs_0_), channel_id=1, source_target_pairs={{0,6},{8,14},{1,7},{9,15},{64,70},{72,78},{65,71},{73,79},{2,0},{1... | collective-permute-start | bytes 786440 | tf_op jit(solution)/shard_map/ppermute | solution.py:44
  69.1 0.7 collective-permute-start.18
  69.8 2.0 %shard_map.177 = (bf16[1024,256]{1,0:T(8,128)(2,1)S(1)}, bf16[1024,256]{1,0:T(8,128)(2,1)}, bf16[1024,256]{1,0:T(8,128)(2,1)S(1)}, bf16[1024,256]{1,0:T(8,128)(2,1)}) custom-call(s32[6]{0:T(128)S(1)} %stack.68.where, bf16[2,768,256]{2,1,0:T(8,128)(2,1)S(1)} %get-tuple-element.54.refs_0_, bf16[2,768,256]{2,1,0:T(8,128)(2,1)S(1)} %collective-permute-done.5.refs_1_, ...), custom_call_target="tpu_custom_call" | custom-call | tf_op jit(solution)/shard_map/pallas_call | solution.py:131
  71.8 1.2 collective-permute-start.10
  73.1 1.5 collective-permute-start.11
  74.5 2.4 %collective-permute-start.12 = (bf16[1024,256]{1,0:T(8,128)(2,1)S(1)}, bf16[1024,256]{1,0:T(8,128)(2,1)S(1)}, u32[]{:S(2)}, u32[]{:S(2)}) collective-permute-start(bf16[1024,256]{1,0:T(8,128)(2,1)S(1)} %get-tuple-element.68), channel_id=1, source_target_pairs={{0,32},{8,40},{1,33},{9,41},{64,96},{72,104},{65,97},{73,105},{2,3... | collective-permute-start | bytes 1572872 | tf_op jit(solution)/shard_map/ppermute | solution.py:44
  77.0 0.0 collective-permute-done.19.refs_2_
  77.0 7.0 %collective-permute-done.18.refs_1_ = bf16[2,128,512]{2,1,0:T(8,128)(2,1)S(1)} collective-permute-done((bf16[2,128,512]{2,1,0:T(8,128)(2,1)S(1)}, bf16[2,128,512]{2,1,0:T(8,128)(2,1)S(1)}, u32[]{:S(2)}, u32[]{:S(2)}) %collective-permute-start.18) | collective-permute-done | bytes 262176 | tf_op jit(solution)/shard_map/ppermute | solution.py:44
  84.0 2.8 %shard_map.179 = bf16[16,2,32,256]{3,2,1,0:T(8,128)(2,1)} custom-call(s32[6]{0:T(128)S(1)} %stack.68.where, bf16[2,128,512]{2,1,0:T(8,128)(2,1)S(1)} %pad_maximum_fusion.2.refs_0_, bf16[2,128,512]{2,1,0:T(8,128)(2,1)S(1)} %collective-permute-done.18.refs_1_, bf16[2,128,512]{2,1,0:T(8,128)(2,1)S(1)} %collective-permute-done.19.refs_2_, ...), custom_call_target="tpu_custom_call" | custom-call | tf_op jit(solution)/shard_map/pallas_call | solution.py:226
  86.9 5.6 %all-to-all-start.1 = ((bf16[16,2,32,256]{3,2,1,0:T(8,128)(2,1)}), bf16[16,2,32,256]{3,2,1,0:T(8,128)(2,1)S(1)}, u32[]{:S(2)}, u32[]{:S(2)}) async-start(bf16[16,2,32,256]{3,2,1,0:T(8,128)(2,1)} %shard_map.179), calls=%async_computation.1 | async-start | bytes 1048576 | tf_op jit(solution)/shard_map/all_to_all | solution.py:458
  92.5 4.6 %collective-permute-done.12.refs_3_ = bf16[1024,256]{1,0:T(8,128)(2,1)S(1)} collective-permute-done((bf16[1024,256]{1,0:T(8,128)(2,1)S(1)}, bf16[1024,256]{1,0:T(8,128)(2,1)S(1)}, u32[]{:S(2)}, u32[]{:S(2)}) %collective-permute-start.12) | collective-permute-done | bytes 524320 | tf_op jit(solution)/shard_map/ppermute | solution.py:44
  97.1 1.4 shard_map.178
  98.5 1.7 %collective-permute-start.13 = (bf16[256,256]{1,0:T(8,128)(2,1)}, bf16[256,256]{1,0:T(8,128)(2,1)S(1)}, u32[]{:S(2)}, u32[]{:S(2)}) collective-permute-start(bf16[256,256]{1,0:T(8,128)(2,1)} %get-tuple-element.69), channel_id=1, source_target_pairs={{0,0},{8,8},{1,16},{9,24},{64,64},{72,72},{65,80},{73,88},{2,2},{1... | collective-permute-start | bytes 393224 | tf_op jit(solution)/shard_map/ppermute | solution.py:44
  100.2 0.7 collective-permute-start.14
  101.0 5.8 %collective-permute-start.15 = (bf16[256,256]{1,0:T(8,128)(2,1)}, bf16[256,256]{1,0:T(8,128)(2,1)S(1)}, u32[]{:S(2)}, u32[]{:S(2)}) collective-permute-start(bf16[256,256]{1,0:T(8,128)(2,1)} %get-tuple-element.71), channel_id=1, source_target_pairs={{0,32},{8,40},{1,48},{9,56},{64,96},{72,104},{65,112},{73,120},{2,... | collective-permute-start | bytes 393224 | tf_op jit(solution)/shard_map/ppermute | solution.py:44
  106.8 0.4 collective-permute-start.16
  107.9 0.1 pad_maximum_fusion.3.fixes
  108.0 0.0 copy-start.7
  108.0 0.9 copy-done.7
  108.9 0.9 copy-done.8
  109.9 1.9 %shard_map.180 = (f32[2,4,32,256]{3,2,1,0:T(8,128)}, f32[2,4,32,256]{3,2,1,0:T(8,128)}, f32[2,4,32,256]{3,2,1,0:T(8,128)}, bf16[256,256]{1,0:T(8,128)(2,1)S(1)}) custom-call(s32[16]{0:T(128)S(1)} %copy-done.9, f32[2]{0:T(128)S(1)} %pad_maximum_fusion.3.fixes, bf16[16,2,32,256]{3,2,1,0:T(8,128)(2,1)S(1)} %all-to-all-done.1.got, ...), custom_call_target="tpu_custom_call" | custom-call | tf_op jit(solution)/shard_map/pallas_call | solution.py:269
  111.8 1.0 collective-permute-done.16.refs_3_
  112.9 2.2 %shard_map.181 = (f32[256,512]{1,0:T(8,128)}, f32[256,512]{1,0:T(8,128)}, f32[256,512]{1,0:T(8,128)}, bf16[768,256]{1,0:T(8,128)(2,1)S(1)}) custom-call(s32[6]{0:T(128)S(1)} %stack.68.where, f32[2]{0:T(128)S(1)} %pad_maximum_fusion.3.fixes, bf16[256,256]{1,0:T(8,128)(2,1)S(1)} %collective-permute-done.13.refs_0_, ...), custom_call_target="tpu_custom_call" | custom-call | tf_op jit(solution)/shard_map/pallas_call | solution.py:333
  115.1 0.9 collective-permute-start.22
  116.1 1.5 collective-permute-start.21
  117.5 1.2 collective-permute-start.28
  118.8 0.3 collective-permute-start.27
  119.0 3.6 %collective-permute-done.22 = bf16[768,256]{1,0:T(8,128)(2,1)S(1)} collective-permute-done((bf16[768,256]{1,0:T(8,128)(2,1)S(1)}, bf16[768,256]{1,0:T(8,128)(2,1)S(1)}, u32[]{:S(2)}, u32[]{:S(2)}) %collective-permute-start.22) | collective-permute-done | bytes 393248 | tf_op jit(solution)/shard_map/ppermute | solution.py:44
  122.6 0.9 collective-permute-start.24
  123.5 0.5 collective-permute-start.23
  124.1 0.2 collective-permute-done.21
  124.3 0.5 collective-permute-start.25
  124.8 3.4 %collective-permute-done.28 = bf16[768,256]{1,0:T(8,128)(2,1)S(1)} collective-permute-done((bf16[768,256]{1,0:T(8,128)(2,1)S(1)}, bf16[768,256]{1,0:T(8,128)(2,1)S(1)}, u32[]{:S(2)}, u32[]{:S(2)}) %collective-permute-start.28) | collective-permute-done | bytes 393248 | tf_op jit(solution)/shard_map/ppermute | solution.py:44
  128.3 1.3 collective-permute-done.27
  129.6 0.2 pad_maximum_fusion.1.own
  129.8 12.2 %collective-permute-start.29 = (bf16[4,768,256]{2,1,0:T(8,128)(2,1)S(1)}, bf16[4,768,256]{2,1,0:T(8,128)(2,1)S(1)}, u32[]{:S(2)}, u32[]{:S(2)}) collective-permute-start(bf16[4,768,256]{2,1,0:T(8,128)(2,1)S(1)} %pad_maximum_fusion.1.own), channel_id=1, source_target_pairs={{0,8},{8,0},{1,9},{9,1},{64,72},{72,64},{65,73},{73,65},{2,10},{10... | collective-permute-start | bytes 4718600 | tf_op jit(solution)/shard_map/ppermute | solution.py:44
  142.0 0.2 pad_maximum_fusion.own
  142.2 4.0 %collective-permute-start.26 = (bf16[4,768,256]{2,1,0:T(8,128)(2,1)S(1)}, bf16[4,768,256]{2,1,0:T(8,128)(2,1)S(1)}, u32[]{:S(2)}, u32[]{:S(2)}) collective-permute-start(bf16[4,768,256]{2,1,0:T(8,128)(2,1)S(1)} %pad_maximum_fusion.own), channel_id=1, source_target_pairs={{0,8},{8,0},{1,9},{9,1},{64,72},{72,64},{65,73},{73,65},{2,10},{10... | collective-permute-start | bytes 4718600 | tf_op jit(solution)/shard_map/ppermute | solution.py:44
  146.2 2.7 %shard_map.182 = (bf16[16,256,512]{2,1,0:T(8,128)(2,1)}, bf16[8,16,32,256]{3,2,1,0:T(8,128)(2,1)}) custom-call(s32[6]{0:T(128)S(1)} %stack.68.where, bf16[4,768,256]{2,1,0:T(8,128)(2,1)S(1)} %pad_maximum_fusion.1.own, bf16[4,768,256]{2,1,0:T(8,128)(2,1)S(1)} %collective-permute-done.29.peer), custom_call_target="tpu_custom_call" | custom-call | tf_op jit(solution)/shard_map/pallas_call | solution.py:367
  148.9 0.3 collective-permute-done.26.peer
  149.3 2.7 %shard_map.183 = (bf16[16,256,512]{2,1,0:T(8,128)(2,1)}, bf16[8,16,32,256]{3,2,1,0:T(8,128)(2,1)}) custom-call(s32[6]{0:T(128)S(1)} %stack.68.where, bf16[4,768,256]{2,1,0:T(8,128)(2,1)S(1)} %pad_maximum_fusion.own, bf16[4,768,256]{2,1,0:T(8,128)(2,1)S(1)} %collective-permute-done.26.peer, ...), custom_call_target="tpu_custom_call", output_to_operand_aliasing={{0}: (3, {}), {1}: (4, {})} | custom-call | tf_op jit(solution)/shard_map/pallas_call | solution.py:367
  (41 shorter events, 0.2 us)
Async XLA Ops:
  0.6 25.8 %collective-permute-start.2 = (bf16[1024,512]{1,0:T(8,128)(2,1)}, bf16[1024,512]{1,0:T(8,128)(2,1)S(1)}, u32[]{:S(2)}, u32[]{:S(2)}) collective-permute-start(bf16[1024,512]{1,0:T(8,128)(2,1)} %refs_4_.2), channel_id=1, source_target_pairs={{0,6},{8,14},{1,7},{9,15},{64,70},{72,78},{65,71},{73,79},{2,0},{1... | collective-permute-start | bytes 3145736 | tf_op jit(solution)/shard_map/ppermute | solution.py:44
  4.3 25.1 %collective-permute-start.1 = (bf16[1024,512]{1,0:T(8,128)(2,1)}, bf16[1024,512]{1,0:T(8,128)(2,1)S(1)}, u32[]{:S(2)}, u32[]{:S(2)}) collective-permute-start(bf16[1024,512]{1,0:T(8,128)(2,1)} %refs_4_.2), channel_id=1, source_target_pairs={{0,2},{8,10},{1,3},{9,11},{64,66},{72,74},{65,67},{73,75},{2,4},{1... | collective-permute-start | bytes 3145736 | tf_op jit(solution)/shard_map/ppermute | solution.py:44
  6.2 1.2 copy-start
  7.5 1.6 %copy-start.2 = (bf16[2,4,512,256]{3,2,1,0:T(8,128)(2,1)S(1)}, bf16[2,4,512,256]{3,2,1,0:T(8,128)(2,1)}, u32[]{:S(2)}) copy-start(bf16[2,4,512,256]{3,2,1,0:T(8,128)(2,1)} %adapters.1) | copy-start | bytes 6291460
  11.5 17.9 %collective-permute-start = (bf16[512,512]{1,0:T(8,128)(2,1)S(1)}, bf16[512,512]{1,0:T(8,128)(2,1)S(1)}, u32[]{:S(2)}, u32[]{:S(2)}) collective-permute-start(bf16[512,512]{1,0:T(8,128)(2,1)S(1)} %get-tuple-element.48), channel_id=1, source_target_pairs={{0,1},{8,9},{1,0},{9,8},{64,65},{72,73},{65,64},{73,72},{2,3},{10,... | collective-permute-start | bytes 1572872 | tf_op jit(solution)/shard_map/ppermute | solution.py:44
  29.4 28.1 %collective-permute-start.7 = (bf16[1024,512]{1,0:T(8,128)(2,1)}, bf16[1024,512]{1,0:T(8,128)(2,1)S(1)}, u32[]{:S(2)}, u32[]{:S(2)}) collective-permute-start(bf16[1024,512]{1,0:T(8,128)(2,1)} %refs_5_.2), channel_id=1, source_target_pairs={{0,1},{8,9},{1,0},{9,8},{64,65},{72,73},{65,64},{73,72},{2,3},{10,... | collective-permute-start | bytes 3145736 | tf_op jit(solution)/shard_map/ppermute | solution.py:44
  33.1 17.4 %collective-permute-start.3 = (bf16[512,512]{1,0:T(8,128)(2,1)S(1)}, bf16[512,512]{1,0:T(8,128)(2,1)S(1)}, u32[]{:S(2)}, u32[]{:S(2)}) collective-permute-start(bf16[512,512]{1,0:T(8,128)(2,1)S(1)} %slice.8), channel_id=1, source_target_pairs={{0,2},{8,10},{1,3},{9,11},{64,66},{72,74},{65,67},{73,75},{2,4},{1... | collective-permute-start | bytes 1572872 | tf_op jit(solution)/shard_map/ppermute | solution.py:44
  33.1 17.4 %collective-permute-start.4 = (bf16[512,512]{1,0:T(8,128)(2,1)S(1)}, bf16[512,512]{1,0:T(8,128)(2,1)S(1)}, u32[]{:S(2)}, u32[]{:S(2)}) collective-permute-start(bf16[512,512]{1,0:T(8,128)(2,1)S(1)} %slice.9), channel_id=1, source_target_pairs={{0,6},{8,14},{1,7},{9,15},{64,70},{72,78},{65,71},{73,79},{2,0},{1... | collective-permute-start | bytes 1572872 | tf_op jit(solution)/shard_map/ppermute | solution.py:44
  35.8 14.7 %copy-start.1 = (bf16[1024,512]{1,0:T(8,128)(2,1)S(1)}, bf16[1024,512]{1,0:T(8,128)(2,1)}, u32[]{:S(2)}) copy-start(bf16[1024,512]{1,0:T(8,128)(2,1)} %refs_4_.2) | copy-start | bytes 3145732
  53.6 16.2 %collective-permute-start.5 = (bf16[2,768,256]{2,1,0:T(8,128)(2,1)S(1)}, bf16[2,768,256]{2,1,0:T(8,128)(2,1)S(1)}, u32[]{:S(2)}, u32[]{:S(2)}) collective-permute-start(bf16[2,768,256]{2,1,0:T(8,128)(2,1)S(1)} %get-tuple-element.55), channel_id=1, source_target_pairs={{0,8},{8,0},{1,9},{9,1},{64,72},{72,64},{65,73},{73,65},{2,10},{10... | collective-permute-start | bytes 2359304 | tf_op jit(solution)/shard_map/ppermute | solution.py:44
  60.0 9.8 %collective-permute-start.8 = (bf16[2,768,256]{2,1,0:T(8,128)(2,1)S(1)}, bf16[2,768,256]{2,1,0:T(8,128)(2,1)S(1)}, u32[]{:S(2)}, u32[]{:S(2)}) collective-permute-start(bf16[2,768,256]{2,1,0:T(8,128)(2,1)S(1)} %get-tuple-element.62), channel_id=1, source_target_pairs={{0,8},{8,0},{1,9},{9,1},{64,72},{72,64},{65,73},{73,65},{2,10},{10... | collective-permute-start | bytes 2359304 | tf_op jit(solution)/shard_map/ppermute | solution.py:44
  60.1 6.8 %collective-permute-start.17 = (bf16[128,512]{1,0:T(8,128)(2,1)S(1)}, bf16[128,512]{1,0:T(8,128)(2,1)S(1)}, u32[]{:S(2)}, u32[]{:S(2)}) collective-permute-start(bf16[128,512]{1,0:T(8,128)(2,1)S(1)} %shard_map.172), channel_id=1, source_target_pairs={{0,1},{8,9},{1,0},{9,8},{64,65},{72,73},{65,64},{73,72},{2,3},{10,... | collective-permute-start | bytes 393224 | tf_op jit(solution)/shard_map/ppermute | solution.py:44
  64.9 4.2 %collective-permute-start.6 = (bf16[2,256,256]{2,1,0:T(8,128)(2,1)S(1)}, bf16[2,256,256]{2,1,0:T(8,128)(2,1)S(1)}, u32[]{:S(2)}, u32[]{:S(2)}) collective-permute-start(bf16[2,256,256]{2,1,0:T(8,128)(2,1)S(1)} %get-tuple-element.59), channel_id=1, source_target_pairs={{0,8},{8,0},{1,9},{9,1},{64,72},{72,64},{65,73},{73,65},{2,10},{10... | collective-permute-start | bytes 786440 | tf_op jit(solution)/shard_map/ppermute | solution.py:44
  66.7 2.4 %collective-permute-start.9 = (bf16[2,256,256]{2,1,0:T(8,128)(2,1)S(1)}, bf16[2,256,256]{2,1,0:T(8,128)(2,1)S(1)}, u32[]{:S(2)}, u32[]{:S(2)}) collective-permute-start(bf16[2,256,256]{2,1,0:T(8,128)(2,1)S(1)} %get-tuple-element.64), channel_id=1, source_target_pairs={{0,8},{8,0},{1,9},{9,1},{64,72},{72,64},{65,73},{73,65},{2,10},{10... | collective-permute-start | bytes 786440 | tf_op jit(solution)/shard_map/ppermute | solution.py:44
  67.0 7.6 %collective-permute-start.20 = (bf16[2,128,512]{2,1,0:T(8,128)(2,1)S(1)}, bf16[2,128,512]{2,1,0:T(8,128)(2,1)S(1)}, u32[]{:S(2)}, u32[]{:S(2)}) collective-permute-start(bf16[2,128,512]{2,1,0:T(8,128)(2,1)S(1)} %pad_maximum_fusion.2.refs_0_), channel_id=1, source_target_pairs={{0,6},{8,14},{1,7},{9,15},{64,70},{72,78},{65,71},{73,79},{2,0},{1... | collective-permute-start | bytes 786440 | tf_op jit(solution)/shard_map/ppermute | solution.py:44
  69.1 7.9 %collective-permute-start.19 = (bf16[2,128,512]{2,1,0:T(8,128)(2,1)S(1)}, bf16[2,128,512]{2,1,0:T(8,128)(2,1)S(1)}, u32[]{:S(2)}, u32[]{:S(2)}) collective-permute-start(bf16[2,128,512]{2,1,0:T(8,128)(2,1)S(1)} %pad_maximum_fusion.2.refs_0_), channel_id=1, source_target_pairs={{0,4},{8,12},{1,5},{9,13},{64,68},{72,76},{65,69},{73,77},{2,6},{1... | collective-permute-start | bytes 786440 | tf_op jit(solution)/shard_map/ppermute | solution.py:44
  69.1 14.9 %collective-permute-start.18 = (bf16[2,128,512]{2,1,0:T(8,128)(2,1)S(1)}, bf16[2,128,512]{2,1,0:T(8,128)(2,1)S(1)}, u32[]{:S(2)}, u32[]{:S(2)}) collective-permute-start(bf16[2,128,512]{2,1,0:T(8,128)(2,1)S(1)} %pad_maximum_fusion.2.refs_0_), channel_id=1, source_target_pairs={{0,2},{8,10},{1,3},{9,11},{64,66},{72,74},{65,67},{73,75},{2,4},{1... | collective-permute-start | bytes 786440 | tf_op jit(solution)/shard_map/ppermute | solution.py:44
  71.8 20.7 %collective-permute-start.10 = (bf16[1024,256]{1,0:T(8,128)(2,1)}, bf16[1024,256]{1,0:T(8,128)(2,1)S(1)}, u32[]{:S(2)}, u32[]{:S(2)}) collective-permute-start(bf16[1024,256]{1,0:T(8,128)(2,1)} %get-tuple-element.66), channel_id=1, source_target_pairs={{0,16},{8,24},{1,17},{9,25},{64,80},{72,88},{65,81},{73,89},{2,18}... | collective-permute-start | bytes 1572872 | tf_op jit(solution)/shard_map/ppermute | solution.py:44
  73.1 19.4 %collective-permute-start.11 = (bf16[1024,256]{1,0:T(8,128)(2,1)}, bf16[1024,256]{1,0:T(8,128)(2,1)S(1)}, u32[]{:S(2)}, u32[]{:S(2)}) collective-permute-start(bf16[1024,256]{1,0:T(8,128)(2,1)} %get-tuple-element.67), channel_id=1, source_target_pairs={{0,48},{8,56},{1,49},{9,57},{64,112},{72,120},{65,113},{73,121},{2... | collective-permute-start | bytes 1572872 | tf_op jit(solution)/shard_map/ppermute | solution.py:44
  74.5 22.6 %collective-permute-start.12 = (bf16[1024,256]{1,0:T(8,128)(2,1)S(1)}, bf16[1024,256]{1,0:T(8,128)(2,1)S(1)}, u32[]{:S(2)}, u32[]{:S(2)}) collective-permute-start(bf16[1024,256]{1,0:T(8,128)(2,1)S(1)} %get-tuple-element.68), channel_id=1, source_target_pairs={{0,32},{8,40},{1,33},{9,41},{64,96},{72,104},{65,97},{73,105},{2,3... | collective-permute-start | bytes 1572872 | tf_op jit(solution)/shard_map/ppermute | solution.py:44
  86.9 21.1 %copy-start.6 = (f32[2,4,32,256]{3,2,1,0:T(8,128)S(1)}, f32[2,4,32,256]{3,2,1,0:T(8,128)}, u32[]{:S(2)}) copy-start(f32[2,4,32,256]{3,2,1,0:T(8,128)} %param.23) | copy-start | bytes 786436
  86.9 21.1 %copy-start.9 = (s32[16]{0:T(128)S(1)}, s32[16]{0:T(128)}, u32[]{:S(2)}) copy-start(s32[16]{0:T(128)} %regions.1) | copy-start | bytes 196
  86.9 21.1 %all-to-all-start.1 = ((bf16[16,2,32,256]{3,2,1,0:T(8,128)(2,1)}), bf16[16,2,32,256]{3,2,1,0:T(8,128)(2,1)S(1)}, u32[]{:S(2)}, u32[]{:S(2)}) async-start(bf16[16,2,32,256]{3,2,1,0:T(8,128)(2,1)} %shard_map.179), calls=%async_computation.1 | async-start | bytes 1048576 | tf_op jit(solution)/shard_map/all_to_all | solution.py:458
  97.1 15.8 %copy-start.3 = (f32[256,512]{1,0:T(8,128)S(1)}, f32[256,512]{1,0:T(8,128)}, u32[]{:S(2)}) copy-start(f32[256,512]{1,0:T(8,128)} %refs_4_.3) | copy-start | bytes 1572868
  98.5 14.3 %copy-start.4 = (f32[256,512]{1,0:T(8,128)S(1)}, f32[256,512]{1,0:T(8,128)}, u32[]{:S(2)}) copy-start(f32[256,512]{1,0:T(8,128)} %refs_5_.3) | copy-start | bytes 1572868
  98.5 14.3 %copy-start.5 = (f32[256,512]{1,0:T(8,128)S(1)}, f32[256,512]{1,0:T(8,128)}, u32[]{:S(2)}) copy-start(f32[256,512]{1,0:T(8,128)} %refs_6_.1) | copy-start | bytes 1572868
  98.5 13.3 %collective-permute-start.13 = (bf16[256,256]{1,0:T(8,128)(2,1)}, bf16[256,256]{1,0:T(8,128)(2,1)S(1)}, u32[]{:S(2)}, u32[]{:S(2)}) collective-permute-start(bf16[256,256]{1,0:T(8,128)(2,1)} %get-tuple-element.69), channel_id=1, source_target_pairs={{0,0},{8,8},{1,16},{9,24},{64,64},{72,72},{65,80},{73,88},{2,2},{1... | collective-permute-start | bytes 393224 | tf_op jit(solution)/shard_map/ppermute | solution.py:44
  100.2 11.6 %collective-permute-start.14 = (bf16[256,256]{1,0:T(8,128)(2,1)}, bf16[256,256]{1,0:T(8,128)(2,1)S(1)}, u32[]{:S(2)}, u32[]{:S(2)}) collective-permute-start(bf16[256,256]{1,0:T(8,128)(2,1)} %get-tuple-element.70), channel_id=1, source_target_pairs={{0,64},{8,72},{1,80},{9,88},{64,0},{72,8},{65,16},{73,24},{2,66},{... | collective-permute-start | bytes 393224 | tf_op jit(solution)/shard_map/ppermute | solution.py:44
  101.0 10.9 %collective-permute-start.15 = (bf16[256,256]{1,0:T(8,128)(2,1)}, bf16[256,256]{1,0:T(8,128)(2,1)S(1)}, u32[]{:S(2)}, u32[]{:S(2)}) collective-permute-start(bf16[256,256]{1,0:T(8,128)(2,1)} %get-tuple-element.71), channel_id=1, source_target_pairs={{0,32},{8,40},{1,48},{9,56},{64,96},{72,104},{65,112},{73,120},{2,... | collective-permute-start | bytes 393224 | tf_op jit(solution)/shard_map/ppermute | solution.py:44
  106.8 6.1 %collective-permute-start.16 = (bf16[256,256]{1,0:T(8,128)(2,1)S(1)}, bf16[256,256]{1,0:T(8,128)(2,1)S(1)}, u32[]{:S(2)}, u32[]{:S(2)}) collective-permute-start(bf16[256,256]{1,0:T(8,128)(2,1)S(1)} %get-tuple-element.72), channel_id=1, source_target_pairs={{0,96},{8,104},{1,112},{9,120},{64,32},{72,40},{65,48},{73,56},{2,... | collective-permute-start | bytes 393224 | tf_op jit(solution)/shard_map/ppermute | solution.py:44
  108.0 1.0 copy-start.7
  108.9 0.9 copy-start.8
  115.1 7.5 %collective-permute-start.22 = (bf16[768,256]{1,0:T(8,128)(2,1)S(1)}, bf16[768,256]{1,0:T(8,128)(2,1)S(1)}, u32[]{:S(2)}, u32[]{:S(2)}) collective-permute-start(bf16[768,256]{1,0:T(8,128)(2,1)S(1)} %get-tuple-element.78), channel_id=1, source_target_pairs={{0,64},{8,72},{1,65},{9,73},{64,0},{72,8},{65,1},{73,9},{2,66},{10... | collective-permute-start | bytes 1179656 | tf_op jit(solution)/shard_map/ppermute | solution.py:44
  116.1 8.2 %collective-permute-start.21 = (bf16[768,256]{1,0:T(8,128)(2,1)S(1)}, bf16[768,256]{1,0:T(8,128)(2,1)S(1)}, u32[]{:S(2)}, u32[]{:S(2)}) collective-permute-start(bf16[768,256]{1,0:T(8,128)(2,1)S(1)} %get-tuple-element.78), channel_id=1, source_target_pairs={{0,32},{8,40},{1,33},{9,41},{64,96},{72,104},{65,97},{73,105},{2,3... | collective-permute-start | bytes 1179656 | tf_op jit(solution)/shard_map/ppermute | solution.py:44
  117.5 10.7 %collective-permute-start.28 = (bf16[768,256]{1,0:T(8,128)(2,1)S(1)}, bf16[768,256]{1,0:T(8,128)(2,1)S(1)}, u32[]{:S(2)}, u32[]{:S(2)}) collective-permute-start(bf16[768,256]{1,0:T(8,128)(2,1)S(1)} %get-tuple-element.78), channel_id=1, source_target_pairs={{0,48},{8,56},{1,49},{9,57},{64,112},{72,120},{65,113},{73,121},{2... | collective-permute-start | bytes 1179656 | tf_op jit(solution)/shard_map/ppermute | solution.py:44
  118.8 10.8 %collective-permute-start.27 = (bf16[768,256]{1,0:T(8,128)(2,1)S(1)}, bf16[768,256]{1,0:T(8,128)(2,1)S(1)}, u32[]{:S(2)}, u32[]{:S(2)}) collective-permute-start(bf16[768,256]{1,0:T(8,128)(2,1)S(1)} %get-tuple-element.78), channel_id=1, source_target_pairs={{0,16},{8,24},{1,17},{9,25},{64,80},{72,88},{65,81},{73,89},{2,18}... | collective-permute-start | bytes 1179656 | tf_op jit(solution)/shard_map/ppermute | solution.py:44
  122.6 19.4 %collective-permute-start.24 = (bf16[768,256]{1,0:T(8,128)(2,1)S(1)}, bf16[768,256]{1,0:T(8,128)(2,1)S(1)}, u32[]{:S(2)}, u32[]{:S(2)}) collective-permute-start(bf16[768,256]{1,0:T(8,128)(2,1)S(1)} %collective-permute-done.22), channel_id=1, source_target_pairs={{0,48},{8,56},{1,49},{9,57},{64,112},{72,120},{65,113},{73,121},{2... | collective-permute-start | bytes 1179656 | tf_op jit(solution)/shard_map/ppermute | solution.py:44
  123.5 18.5 %collective-permute-start.23 = (bf16[768,256]{1,0:T(8,128)(2,1)S(1)}, bf16[768,256]{1,0:T(8,128)(2,1)S(1)}, u32[]{:S(2)}, u32[]{:S(2)}) collective-permute-start(bf16[768,256]{1,0:T(8,128)(2,1)S(1)} %collective-permute-done.22), channel_id=1, source_target_pairs={{0,16},{8,24},{1,17},{9,25},{64,80},{72,88},{65,81},{73,89},{2,18}... | collective-permute-start | bytes 1179656 | tf_op jit(solution)/shard_map/ppermute | solution.py:44
  124.3 17.7 %collective-permute-start.25 = (bf16[768,256]{1,0:T(8,128)(2,1)S(1)}, bf16[768,256]{1,0:T(8,128)(2,1)S(1)}, u32[]{:S(2)}, u32[]{:S(2)}) collective-permute-start(bf16[768,256]{1,0:T(8,128)(2,1)S(1)} %collective-permute-done.21), channel_id=1, source_target_pairs={{0,64},{8,72},{1,65},{9,73},{64,0},{72,8},{65,1},{73,9},{2,66},{10... | collective-permute-start | bytes 1179656 | tf_op jit(solution)/shard_map/ppermute | solution.py:44
  129.8 16.5 %collective-permute-start.29 = (bf16[4,768,256]{2,1,0:T(8,128)(2,1)S(1)}, bf16[4,768,256]{2,1,0:T(8,128)(2,1)S(1)}, u32[]{:S(2)}, u32[]{:S(2)}) collective-permute-start(bf16[4,768,256]{2,1,0:T(8,128)(2,1)S(1)} %pad_maximum_fusion.1.own), channel_id=1, source_target_pairs={{0,8},{8,0},{1,9},{9,1},{64,72},{72,64},{65,73},{73,65},{2,10},{10... | collective-permute-start | bytes 4718600 | tf_op jit(solution)/shard_map/ppermute | solution.py:44
  142.2 7.0 %collective-permute-start.26 = (bf16[4,768,256]{2,1,0:T(8,128)(2,1)S(1)}, bf16[4,768,256]{2,1,0:T(8,128)(2,1)S(1)}, u32[]{:S(2)}, u32[]{:S(2)}) collective-permute-start(bf16[4,768,256]{2,1,0:T(8,128)(2,1)S(1)} %pad_maximum_fusion.own), channel_id=1, source_target_pairs={{0,8},{8,0},{1,9},{9,1},{64,72},{72,64},{65,73},{73,65},{2,10},{10... | collective-permute-start | bytes 4718600 | tf_op jit(solution)/shard_map/ppermute | solution.py:44

commit v5 on v4

--- a/solution.py
+++ b/solution.py
@@ -15,7 +15,7 @@
 decay_rate = 0.1
 
 AXES = ("fsdp", "tp")
-X, Y, ZL, ZH, CORE, REGION = range(6)
+X, Y, ZL, ZH, CORE, FSDP = range(6)
 F32 = jnp.float32
 BF16 = jnp.bfloat16
 
@@ -137,40 +137,48 @@
     )(here, *parts)
 
 
-def low_kernel(scales, where, act, cot, adapters, keep, give):
-    rows, rank = keep.shape[0], adapters.shape[3]
-    for out, h in ((keep, where[ZH]), (give, 1 - where[ZH])):
-        part = pl.ds(pl.multiple_of(h * rows, rows), rows)
-        down = jnp.dot(act[part, :], adapters[0, 0], preferred_element_type=F32) * scales[0]
-        up = jnp.dot(cot[part, :], adapters[1, 0], preferred_element_type=F32) * scales[1]
-        out[:, :rank] = down.astype(out.dtype)
-        out[:, rank:] = up.astype(out.dtype)
-
-
-def low_parts(here, act, cot, adapters, scales):
+def low_kernel(scales, where, regions, act, cot, adapters, keep, give, acts, cots, own, sems):
+    rows, rank = keep.shape[0], own.shape[2]
+    region = regions[where[FSDP]]
+    copies = [
+        pltpu.make_async_copy(adapters.at[0, region], own.at[0], sems.at[0]),
+        pltpu.make_async_copy(act, acts, sems.at[1]),
+        pltpu.make_async_copy(adapters.at[1, region], own.at[1], sems.at[2]),
+        pltpu.make_async_copy(cot, cots, sems.at[3]),
+    ]
+    for copy in copies:
+        copy.start()
+    for side, source in enumerate((acts, cots)):
+        copies[2 * side].wait()
+        copies[2 * side + 1].wait()
+        columns = pl.ds(side * rank, rank)
+        for out, h in ((keep, where[ZH]), (give, 1 - where[ZH])):
+            part = source[pl.ds(pl.multiple_of(h * rows, rows), rows), :]
+            total = jnp.dot(part, own[side], preferred_element_type=F32) * scales[side]
+            out[:, columns] = total.astype(out.dtype)
+
+
+def low_parts(here, regions, act, cot, adapters, scales):
     rows, rank = act.shape[0] // 2, adapters.shape[3]
-    whole = pl.BlockSpec(act.shape, lambda i, where: (0, 0))
-    out = pl.BlockSpec((rows, 2 * rank), lambda i, where: (0, 0))
+    smem = pl.BlockSpec(memory_space=pltpu.SMEM)
+    hbm = pl.BlockSpec(memory_space=pltpu.HBM)
+    vmem = pl.BlockSpec(memory_space=pltpu.VMEM)
     return pl.pallas_call(
         functools.partial(low_kernel, scales),
         out_shape=(
             jax.ShapeDtypeStruct((rows, 2 * rank), F32),
             jax.ShapeDtypeStruct((rows, 2 * rank), BF16),
         ),
-        grid_spec=pltpu.PrefetchScalarGridSpec(
-            num_scalar_prefetch=1,
-            grid=(1,),
-            in_specs=[
-                whole,
-                whole,
-                pl.BlockSpec(
-                    (2, 1) + adapters.shape[2:], lambda i, where: (0, where[REGION], 0, 0)
-                ),
-            ],
-            out_specs=(out, out),
-        ),
-        compiler_params=pltpu.CompilerParams(vmem_limit_bytes=32 * 1024 * 1024),
-    )(here, act, cot, adapters)
+        in_specs=[smem, smem, hbm, hbm, hbm],
+        out_specs=(vmem, vmem),
+        scratch_shapes=[
+            pltpu.VMEM(act.shape, BF16),
+            pltpu.VMEM(cot.shape, BF16),
+            pltpu.VMEM((2,) + adapters.shape[2:], BF16),
+            pltpu.SemaphoreType.DMA((4,)),
+        ],
+        compiler_params=pltpu.CompilerParams(vmem_limit_bytes=24 * 1024 * 1024),
+    )(here, regions, act, cot, adapters)
 
 
 def low_add_kernel(keep, got, out):
@@ -240,20 +248,28 @@
     return param - learn_rate * (ratio + decay_rate * param), moment_new, second_new
 
 
-def adapter_kernel(regions, fixes, got, param, moment, second, *outs):
-    new_param, new_moment, new_second, rounded = outs
-    rows, rank = param.shape[2:]
+def adapter_kernel(regions, fixes, got, *refs):
+    states, (new_param, new_moment, new_second, rounded), held, sums, sems = (
+        refs[:3], refs[3:7], refs[7:10], refs[10], refs[11]
+    )
+    copies = [
+        pltpu.make_async_copy(state, here, sems.at[i])
+        for i, (state, here) in enumerate(zip(states, held))
+    ]
+    for copy in copies:
+        copy.start()
+    sums[...] = jnp.zeros(sums.shape, F32)
+    for f in range(got.shape[0]):
+        sums[regions[f]] += got[f].astype(F32)
+    for copy in copies:
+        copy.wait()
+    param, moment, second = held
+    rows = param.shape[2]
     for side in range(2):
-        totals = [jnp.zeros((rows, rank), F32) for _ in range(param.shape[1])]
-        for f in range(got.shape[0]):
-            term = got[f, side].astype(F32)
-            totals = [
-                total + jnp.where(regions[f] == r, 1.0, 0.0) * term
-                for r, total in enumerate(totals)
-            ]
-        for r, total in enumerate(totals):
+        for r in range(param.shape[1]):
             p, m, v = adamw_values(
-                param[side, r], moment[side, r], second[side, r], total, fixes[0], fixes[1]
+                param[side, r], moment[side, r], second[side, r], sums[r, side],
+                fixes[0], fixes[1],
             )
             new_param[side, r] = p
             new_moment[side, r] = m
@@ -262,6 +278,7 @@
 
 
 def adapter_update(regions, fixes, got, param, moment, second):
+    hbm = pl.BlockSpec(memory_space=pltpu.HBM)
     vmem = pl.BlockSpec(memory_space=pltpu.VMEM)
     smem = pl.BlockSpec(memory_space=pltpu.SMEM)
     like = jax.ShapeDtypeStruct(param.shape, F32)
@@ -269,9 +286,14 @@
     return pl.pallas_call(
         adapter_kernel,
         out_shape=(like, like, like, rounded),
-        in_specs=[smem, smem] + [vmem] * 4,
+        in_specs=[smem, smem, vmem, hbm, hbm, hbm],
         out_specs=(vmem,) * 4,
-        compiler_params=pltpu.CompilerParams(vmem_limit_bytes=32 * 1024 * 1024),
+        scratch_shapes=[pltpu.VMEM(param.shape, F32)] * 3
+        + [
+            pltpu.VMEM((param.shape[1],) + got.shape[1:], F32),
+            pltpu.SemaphoreType.DMA((3,)),
+        ],
+        compiler_params=pltpu.CompilerParams(vmem_limit_bytes=16 * 1024 * 1024),
     )(regions, fixes, got, param, moment, second)
 
 
@@ -409,8 +431,7 @@
     zl, x, c = f // 8, (f // 2) % 4, f % 2
     y, zh = t // 2, t % 2
 
-    own_region = lax.dynamic_index_in_dim(region_of, f, 0, keepdims=False)
-    here = jnp.stack([x, y, zl, zh, c, own_region]).astype(jnp.int32)
+    here = jnp.stack([x, y, zl, zh, c, f]).astype(jnp.int32)
     step_float = step_count[0].astype(F32)
     fixes = jnp.stack([
         1.0 - jnp.power(F32(beta_first), step_float),
@@ -418,7 +439,7 @@
     ])
 
     low_keep, low_give = low_parts(
-        here, activations, cotangent, adapter_copy, (inv_width, inv_rank)
+        here, region_of, activations, cotangent, adapter_copy, (inv_width, inv_rank)
     )
     low_got = move(low_give, other_zh)
 
@@ -448,7 +469,7 @@
     parts += swapped(near_acts, cot_zh) + swapped(far_acts, cot_zh)
     blocks = add_blocks(here, parts)
     low_pieces = [low_both] + [move(low_both, along_y(k)) for k in (1, 2, 3)]
-    blocks = [blocks[0]] + [move(blocks[k], along_x(k)) for k in (1, 3, 2)]
+    blocks = [blocks[0]] + [move(blocks[k], along_x(k)) for k in (3, 1, 2)]
     blocks = pick_blocks(here, blocks)
 
     parts = adapter_grads(
@@ -465,8 +486,8 @@
     )
 
     from_zl = move(piece, other_zl)
+    from_ahead = move(piece, along_x(-1))
     from_back = move(piece, along_x(1))
-    from_ahead = move(piece, along_x(-1))
     from_far = move(piece, along_x(2))
     first = jnp.stack([piece, from_zl, from_back, from_ahead])
     second = jnp.stack([

time: 153 us -> 152 us (level)
    unnamed x20 -> x22, local copies, waits for them, and re-layouts: 4.73 us -> 5.41 us
  transfers between devices with their start and end apart: 31 -> 31, of which waited for: 10 -> 8; matrix products, arithmetic and copies ran while one was open for 2% -> 0% of each run, Pallas kernels for 15% -> 15%
where the time goes in v5:
time: 152 us; the launch traced here: 151 us
  starting transfers between devices  66.5 us (44%)
  waiting for transfers between devices  35.4 us (23%)
  Pallas kernels  27.2 us (18%)
  blocking collectives  14.5 us (10%)
  local copies, waits for them, and re-layouts  5.56 us (4%)
  between operations  1.57 us (1%)
    ppermute x30, starting transfers between devices, move(): return lax.ppermute(array, AXES, pairs)  60.9 us
    ppermute x30, waiting for transfers between devices, move(): return lax.ppermute(array, AXES, pairs)  35.4 us
    all_to_all x1, blocking collectives, swap_among(): return lax.all_to_all(array, axis, 0, 0, axis_index_groups=groups)  14.5 us
    pallas_call x4, Pallas kernels, partials(): pl.pallas_call(functools.partial(partials_kernel, counts), out_shape=(jax...  8.84 us
    all_to_all x1, starting transfers between devices, shards(): got = lax.all_to_all(parts, 'fsdp', 0, 0)  5.61 us
    pallas_call x2, Pallas kernels, place_blocks(): pl.pallas_call(functools.partial(place_kernel, slots), out_shape=shapes,...  5.41 us
    unnamed x22, local copies, waits for them, and re-layouts  5.41 us
  transfers between devices with their start and end apart: 31, of which 8 were waited for; matrix products, arithmetic and copies ran while one was open for 0% of the time, Pallas kernels for 15%

profile of v5, /device:TPU:1, one launch (start us, length us, event | category | flops | bytes accessed | tf_op | source)
XLA Modules:
  0.0 151.3 jit_solution(5600838897849373786)
XLA Ops:
  0.6 3.6 %collective-permute-start.2 = (bf16[1024,512]{1,0:T(8,128)(2,1)}, bf16[1024,512]{1,0:T(8,128)(2,1)S(1)}, u32[]{:S(2)}, u32[]{:S(2)}) collective-permute-start(bf16[1024,512]{1,0:T(8,128)(2,1)} %refs_4_.2), channel_id=1, source_target_pairs={{0,6},{8,14},{1,7},{9,15},{64,70},{72,78},{65,71},{73,79},{2,0},{1... | collective-permute-start | bytes 3145736 | tf_op jit(solution)/shard_map/ppermute | solution.py:44
  4.3 0.0 collective-permute-start.1
  4.3 0.1 stack.71.where
  4.4 1.2 copy-done
  5.6 1.6 %copy-done.2 = bf16[2,4,512,256]{3,2,1,0:T(8,128)(2,1)S(1)} copy-done((bf16[2,4,512,256]{3,2,1,0:T(8,128)(2,1)S(1)}, bf16[2,4,512,256]{3,2,1,0:T(8,128)(2,1)}, u32[]{:S(2)}) %copy-start.2) | copy-done | bytes 2097176
  7.2 0.7 copy-done.9
  7.8 2.4 %shard_map.170 = (f32[512,512]{1,0:T(8,128)S(1)}, bf16[512,512]{1,0:T(8,128)(2,1)S(1)}) custom-call(s32[6]{0:T(128)S(1)} %stack.71.where, s32[16]{0:T(128)S(1)} %copy-done.9, bf16[1024,512]{1,0:T(8,128)(2,1)S(1)} %copy-done, bf16[1024,512]{1,0:T(8,128)(2,1)} %refs_5_.2, bf16[2,4,512,256]{3,2,1,0:T(8,128)(2,1)S(1)} %copy-done.2), custom_call_target="tpu_custom_call" | custom-call | tf_op jit(solution)/shard_map/pallas_call | solution.py:166
  10.2 3.7 %collective-permute-start = (bf16[512,512]{1,0:T(8,128)(2,1)S(1)}, bf16[512,512]{1,0:T(8,128)(2,1)S(1)}, u32[]{:S(2)}, u32[]{:S(2)}) collective-permute-start(bf16[512,512]{1,0:T(8,128)(2,1)S(1)} %get-tuple-element.48), channel_id=1, source_target_pairs={{0,1},{8,9},{1,0},{9,8},{64,65},{72,73},{65,64},{73,72},{2,3},{10,... | collective-permute-start | bytes 1572872 | tf_op jit(solution)/shard_map/ppermute | solution.py:44
  13.9 12.5 %collective-permute-done.2.refs_1_ = bf16[1024,512]{1,0:T(8,128)(2,1)S(1)} collective-permute-done((bf16[1024,512]{1,0:T(8,128)(2,1)}, bf16[1024,512]{1,0:T(8,128)(2,1)S(1)}, u32[]{:S(2)}, u32[]{:S(2)}) %collective-permute-start.2) | collective-permute-done | bytes 1048608 | tf_op jit(solution)/shard_map/ppermute | solution.py:44
  26.4 2.9 %collective-permute-done.1.refs_2_ = bf16[1024,512]{1,0:T(8,128)(2,1)S(1)} collective-permute-done((bf16[1024,512]{1,0:T(8,128)(2,1)}, bf16[1024,512]{1,0:T(8,128)(2,1)S(1)}, u32[]{:S(2)}, u32[]{:S(2)}) %collective-permute-start.1) | collective-permute-done | bytes 1048608 | tf_op jit(solution)/shard_map/ppermute | solution.py:44
  29.4 3.7 %collective-permute-start.7 = (bf16[1024,512]{1,0:T(8,128)(2,1)}, bf16[1024,512]{1,0:T(8,128)(2,1)S(1)}, u32[]{:S(2)}, u32[]{:S(2)}) collective-permute-start(bf16[1024,512]{1,0:T(8,128)(2,1)} %refs_5_.2), channel_id=1, source_target_pairs={{0,1},{8,9},{1,0},{9,8},{64,65},{72,73},{65,64},{73,72},{2,3},{10,... | collective-permute-start | bytes 3145736 | tf_op jit(solution)/shard_map/ppermute | solution.py:44
  33.1 2.7 %collective-permute-start.4 = (bf16[512,512]{1,0:T(8,128)(2,1)S(1)}, bf16[512,512]{1,0:T(8,128)(2,1)S(1)}, u32[]{:S(2)}, u32[]{:S(2)}) collective-permute-start(bf16[512,512]{1,0:T(8,128)(2,1)S(1)} %slice.9), channel_id=1, source_target_pairs={{0,6},{8,14},{1,7},{9,15},{64,70},{72,78},{65,71},{73,79},{2,0},{1... | collective-permute-start | bytes 1572872 | tf_op jit(solution)/shard_map/ppermute | solution.py:44
  35.8 0.1 shard_map.171
  35.9 14.5 %all_to_all.10.parts = bf16[4,128,512]{2,1,0:T(8,128)(2,1)S(1)} all-to-all(bf16[4,128,512]{2,1,0:T(8,128)(2,1)S(1)} %bitcast.19), channel_id=1, replica_groups={{0,2,4,6},{1,3,5,7},{8,10,12,14},{9,11,13,15},{16,18,20,22},{17,19,21,2..., dimensions={0} | all-to-all | bytes 1048576 | tf_op jit(solution)/shard_map/all_to_all | solution.py:48
  50.4 0.1 shard_map.172
  50.5 0.0 collective-permute-done.3.refs_0_
  50.5 0.0 collective-permute-done.4.refs_1_
  50.5 3.1 %shard_map.173 = (bf16[2,768,256]{2,1,0:T(8,128)(2,1)S(1)}, bf16[2,768,256]{2,1,0:T(8,128)(2,1)S(1)}) custom-call(s32[6]{0:T(128)S(1)} %stack.71.where, bf16[1024,512]{1,0:T(8,128)(2,1)S(1)} %copy-done.1, bf16[1024,512]{1,0:T(8,128)(2,1)S(1)} %collective-permute-done.2.refs_1_, bf16[1024,512]{1,0:T(8,128)(2,1)S(1)} %collective-permute-done.1.refs_2_, ...), custom_call_target="tpu_custom_call" | custom-call | tf_op jit(solution)/shard_map/pallas_call | solution.py:103
  53.6 3.9 %collective-permute-start.5 = (bf16[2,768,256]{2,1,0:T(8,128)(2,1)S(1)}, bf16[2,768,256]{2,1,0:T(8,128)(2,1)S(1)}, u32[]{:S(2)}, u32[]{:S(2)}) collective-permute-start(bf16[2,768,256]{2,1,0:T(8,128)(2,1)S(1)} %get-tuple-element.55), channel_id=1, source_target_pairs={{0,8},{8,0},{1,9},{9,1},{64,72},{72,64},{65,73},{73,65},{2,10},{10... | collective-permute-start | bytes 2359304 | tf_op jit(solution)/shard_map/ppermute | solution.py:44
  57.6 2.4 %shard_map.175 = (bf16[2,768,256]{2,1,0:T(8,128)(2,1)S(1)}, bf16[2,768,256]{2,1,0:T(8,128)(2,1)S(1)}) custom-call(s32[6]{0:T(128)S(1)} %stack.71.where, bf16[1024,512]{1,0:T(8,128)(2,1)S(1)} %copy-done.1, bf16[1024,512]{1,0:T(8,128)(2,1)S(1)} %collective-permute-done.2.refs_1_, bf16[1024,512]{1,0:T(8,128)(2,1)S(1)} %collective-permute-done.1.refs_2_, ...), custom_call_target="tpu_custom_call" | custom-call | tf_op jit(solution)/shard_map/pallas_call | solution.py:103
  60.0 0.1 collective-permute-start.8
  60.1 2.8 %collective-permute-start.17 = (bf16[128,512]{1,0:T(8,128)(2,1)S(1)}, bf16[128,512]{1,0:T(8,128)(2,1)S(1)}, u32[]{:S(2)}, u32[]{:S(2)}) collective-permute-start(bf16[128,512]{1,0:T(8,128)(2,1)S(1)} %shard_map.172), channel_id=1, source_target_pairs={{0,1},{8,9},{1,0},{9,8},{64,65},{72,73},{65,64},{73,72},{2,3},{10,... | collective-permute-start | bytes 393224 | tf_op jit(solution)/shard_map/ppermute | solution.py:44
  62.9 2.0 %shard_map.174 = (bf16[2,256,256]{2,1,0:T(8,128)(2,1)S(1)}, bf16[2,256,256]{2,1,0:T(8,128)(2,1)S(1)}) custom-call(s32[6]{0:T(128)S(1)} %stack.71.where, bf16[512,512]{1,0:T(8,128)(2,1)S(1)} %collective-permute-done.3.refs_0_, bf16[512,512]{1,0:T(8,128)(2,1)S(1)} %collective-permute-done.4.refs_1_, bf16[1024,512]{1,0:T(8,128)(2,1)} %refs_5_.2), custom_call_target="tpu_custom_call" | custom-call | tf_op jit(solution)/shard_map/pallas_call | solution.py:103
  64.9 0.4 collective-permute-start.6
  65.4 1.3 shard_map.176
  66.7 0.2 collective-permute-start.9
  66.9 0.0 collective-permute-done.17
  67.0 2.2 %collective-permute-start.20 = (bf16[2,128,512]{2,1,0:T(8,128)(2,1)S(1)}, bf16[2,128,512]{2,1,0:T(8,128)(2,1)S(1)}, u32[]{:S(2)}, u32[]{:S(2)}) collective-permute-start(bf16[2,128,512]{2,1,0:T(8,128)(2,1)S(1)} %pad_maximum_fusion.2.refs_0_), channel_id=1, source_target_pairs={{0,6},{8,14},{1,7},{9,15},{64,70},{72,78},{65,71},{73,79},{2,0},{1... | collective-permute-start | bytes 786440 | tf_op jit(solution)/shard_map/ppermute | solution.py:44
  69.1 0.7 collective-permute-start.18
  69.8 2.0 %shard_map.177 = (bf16[1024,256]{1,0:T(8,128)(2,1)S(1)}, bf16[1024,256]{1,0:T(8,128)(2,1)}, bf16[1024,256]{1,0:T(8,128)(2,1)S(1)}, bf16[1024,256]{1,0:T(8,128)(2,1)}) custom-call(s32[6]{0:T(128)S(1)} %stack.71.where, bf16[2,768,256]{2,1,0:T(8,128)(2,1)S(1)} %get-tuple-element.54.refs_0_, bf16[2,768,256]{2,1,0:T(8,128)(2,1)S(1)} %collective-permute-done.5.refs_1_, ...), custom_call_target="tpu_custom_call" | custom-call | tf_op jit(solution)/shard_map/pallas_call | solution.py:131
  71.8 2.5 %collective-permute-start.10 = (bf16[1024,256]{1,0:T(8,128)(2,1)}, bf16[1024,256]{1,0:T(8,128)(2,1)S(1)}, u32[]{:S(2)}, u32[]{:S(2)}) collective-permute-start(bf16[1024,256]{1,0:T(8,128)(2,1)} %get-tuple-element.66), channel_id=1, source_target_pairs={{0,48},{8,56},{1,49},{9,57},{64,112},{72,120},{65,113},{73,121},{2... | collective-permute-start | bytes 1572872 | tf_op jit(solution)/shard_map/ppermute | solution.py:44
  74.3 2.6 %collective-permute-start.12 = (bf16[1024,256]{1,0:T(8,128)(2,1)S(1)}, bf16[1024,256]{1,0:T(8,128)(2,1)S(1)}, u32[]{:S(2)}, u32[]{:S(2)}) collective-permute-start(bf16[1024,256]{1,0:T(8,128)(2,1)S(1)} %get-tuple-element.68), channel_id=1, source_target_pairs={{0,32},{8,40},{1,33},{9,41},{64,96},{72,104},{65,97},{73,105},{2,3... | collective-permute-start | bytes 1572872 | tf_op jit(solution)/shard_map/ppermute | solution.py:44
  77.0 0.0 collective-permute-done.19.refs_2_
  77.0 7.0 %collective-permute-done.18.refs_1_ = bf16[2,128,512]{2,1,0:T(8,128)(2,1)S(1)} collective-permute-done((bf16[2,128,512]{2,1,0:T(8,128)(2,1)S(1)}, bf16[2,128,512]{2,1,0:T(8,128)(2,1)S(1)}, u32[]{:S(2)}, u32[]{:S(2)}) %collective-permute-start.18) | collective-permute-done | bytes 262176 | tf_op jit(solution)/shard_map/ppermute | solution.py:44
  84.0 2.8 %shard_map.179 = bf16[16,2,32,256]{3,2,1,0:T(8,128)(2,1)} custom-call(s32[6]{0:T(128)S(1)} %stack.71.where, bf16[2,128,512]{2,1,0:T(8,128)(2,1)S(1)} %pad_maximum_fusion.2.refs_0_, bf16[2,128,512]{2,1,0:T(8,128)(2,1)S(1)} %collective-permute-done.18.refs_1_, bf16[2,128,512]{2,1,0:T(8,128)(2,1)S(1)} %collective-permute-done.19.refs_2_, ...), custom_call_target="tpu_custom_call" | custom-call | tf_op jit(solution)/shard_map/pallas_call | solution.py:234
  86.9 5.6 %all-to-all-start.1 = ((bf16[16,2,32,256]{3,2,1,0:T(8,128)(2,1)}), bf16[16,2,32,256]{3,2,1,0:T(8,128)(2,1)S(1)}, u32[]{:S(2)}, u32[]{:S(2)}) async-start(bf16[16,2,32,256]{3,2,1,0:T(8,128)(2,1)} %shard_map.179), calls=%async_computation.1 | async-start | bytes 1048576 | tf_op jit(solution)/shard_map/all_to_all | solution.py:479
  92.5 4.9 %collective-permute-done.12.refs_3_ = bf16[1024,256]{1,0:T(8,128)(2,1)S(1)} collective-permute-done((bf16[1024,256]{1,0:T(8,128)(2,1)S(1)}, bf16[1024,256]{1,0:T(8,128)(2,1)S(1)}, u32[]{:S(2)}, u32[]{:S(2)}) %collective-permute-start.12) | collective-permute-done | bytes 524320 | tf_op jit(solution)/shard_map/ppermute | solution.py:44
  97.4 1.4 shard_map.178
  98.9 1.7 %collective-permute-start.13 = (bf16[256,256]{1,0:T(8,128)(2,1)}, bf16[256,256]{1,0:T(8,128)(2,1)S(1)}, u32[]{:S(2)}, u32[]{:S(2)}) collective-permute-start(bf16[256,256]{1,0:T(8,128)(2,1)} %get-tuple-element.69), channel_id=1, source_target_pairs={{0,0},{8,8},{1,16},{9,24},{64,64},{72,72},{65,80},{73,88},{2,2},{1... | collective-permute-start | bytes 393224 | tf_op jit(solution)/shard_map/ppermute | solution.py:44
  100.5 0.7 collective-permute-start.14
  101.3 4.8 %collective-permute-start.15 = (bf16[256,256]{1,0:T(8,128)(2,1)}, bf16[256,256]{1,0:T(8,128)(2,1)S(1)}, u32[]{:S(2)}, u32[]{:S(2)}) collective-permute-start(bf16[256,256]{1,0:T(8,128)(2,1)} %get-tuple-element.71), channel_id=1, source_target_pairs={{0,32},{8,40},{1,48},{9,56},{64,96},{72,104},{65,112},{73,120},{2,... | collective-permute-start | bytes 393224 | tf_op jit(solution)/shard_map/ppermute | solution.py:44
  106.1 0.1 collective-permute-start.16
  107.0 0.1 pad_maximum_fusion.3.fixes
  107.1 0.0 copy-start.7
  107.1 0.9 copy-done.7
  108.0 0.9 copy-done.8
  109.0 1.8 %shard_map.180 = (f32[2,4,32,256]{3,2,1,0:T(8,128)}, f32[2,4,32,256]{3,2,1,0:T(8,128)}, f32[2,4,32,256]{3,2,1,0:T(8,128)}, bf16[256,256]{1,0:T(8,128)(2,1)S(1)}) custom-call(s32[16]{0:T(128)S(1)} %copy-done.10, f32[2]{0:T(128)S(1)} %pad_maximum_fusion.3.fixes, bf16[16,2,32,256]{3,2,1,0:T(8,128)(2,1)S(1)} %all-to-all-done.1.got, ...), custom_call_target="tpu_custom_call" | custom-call | tf_op jit(solution)/shard_map/pallas_call | solution.py:286
  110.8 1.1 collective-permute-done.16.refs_3_
  112.0 2.2 %shard_map.181 = (f32[256,512]{1,0:T(8,128)}, f32[256,512]{1,0:T(8,128)}, f32[256,512]{1,0:T(8,128)}, bf16[768,256]{1,0:T(8,128)(2,1)S(1)}) custom-call(s32[6]{0:T(128)S(1)} %stack.71.where, f32[2]{0:T(128)S(1)} %pad_maximum_fusion.3.fixes, bf16[256,256]{1,0:T(8,128)(2,1)S(1)} %collective-permute-done.13.refs_0_, ...), custom_call_target="tpu_custom_call" | custom-call | tf_op jit(solution)/shard_map/pallas_call | solution.py:355
  114.2 0.8 collective-permute-start.22
  115.0 2.5 %collective-permute-start.21 = (bf16[768,256]{1,0:T(8,128)(2,1)S(1)}, bf16[768,256]{1,0:T(8,128)(2,1)S(1)}, u32[]{:S(2)}, u32[]{:S(2)}) collective-permute-start(bf16[768,256]{1,0:T(8,128)(2,1)S(1)} %get-tuple-element.78), channel_id=1, source_target_pairs={{0,32},{8,40},{1,33},{9,41},{64,96},{72,104},{65,97},{73,105},{2,3... | collective-permute-start | bytes 1179656 | tf_op jit(solution)/shard_map/ppermute | solution.py:44
  117.5 2.3 %collective-permute-start.28 = (bf16[768,256]{1,0:T(8,128)(2,1)S(1)}, bf16[768,256]{1,0:T(8,128)(2,1)S(1)}, u32[]{:S(2)}, u32[]{:S(2)}) collective-permute-start(bf16[768,256]{1,0:T(8,128)(2,1)S(1)} %get-tuple-element.78), channel_id=1, source_target_pairs={{0,48},{8,56},{1,49},{9,57},{64,112},{72,120},{65,113},{73,121},{2... | collective-permute-start | bytes 1179656 | tf_op jit(solution)/shard_map/ppermute | solution.py:44
  119.8 3.0 %collective-permute-done.22 = bf16[768,256]{1,0:T(8,128)(2,1)S(1)} collective-permute-done((bf16[768,256]{1,0:T(8,128)(2,1)S(1)}, bf16[768,256]{1,0:T(8,128)(2,1)S(1)}, u32[]{:S(2)}, u32[]{:S(2)}) %collective-permute-start.22) | collective-permute-done | bytes 393248 | tf_op jit(solution)/shard_map/ppermute | solution.py:44
  122.8 0.9 collective-permute-start.24
  123.7 0.6 collective-permute-start.23
  124.3 0.6 collective-permute-start.25
  125.0 3.5 %collective-permute-done.28 = bf16[768,256]{1,0:T(8,128)(2,1)S(1)} collective-permute-done((bf16[768,256]{1,0:T(8,128)(2,1)S(1)}, bf16[768,256]{1,0:T(8,128)(2,1)S(1)}, u32[]{:S(2)}, u32[]{:S(2)}) %collective-permute-start.28) | collective-permute-done | bytes 393248 | tf_op jit(solution)/shard_map/ppermute | solution.py:44
  128.4 0.2 pad_maximum_fusion.1.own
  128.6 12.7 %collective-permute-start.29 = (bf16[4,768,256]{2,1,0:T(8,128)(2,1)S(1)}, bf16[4,768,256]{2,1,0:T(8,128)(2,1)S(1)}, u32[]{:S(2)}, u32[]{:S(2)}) collective-permute-start(bf16[4,768,256]{2,1,0:T(8,128)(2,1)S(1)} %pad_maximum_fusion.1.own), channel_id=1, source_target_pairs={{0,8},{8,0},{1,9},{9,1},{64,72},{72,64},{65,73},{73,65},{2,10},{10... | collective-permute-start | bytes 4718600 | tf_op jit(solution)/shard_map/ppermute | solution.py:44
  141.3 0.2 pad_maximum_fusion.own
  141.5 4.0 %collective-permute-start.26 = (bf16[4,768,256]{2,1,0:T(8,128)(2,1)S(1)}, bf16[4,768,256]{2,1,0:T(8,128)(2,1)S(1)}, u32[]{:S(2)}, u32[]{:S(2)}) collective-permute-start(bf16[4,768,256]{2,1,0:T(8,128)(2,1)S(1)} %pad_maximum_fusion.own), channel_id=1, source_target_pairs={{0,8},{8,0},{1,9},{9,1},{64,72},{72,64},{65,73},{73,65},{2,10},{10... | collective-permute-start | bytes 4718600 | tf_op jit(solution)/shard_map/ppermute | solution.py:44
  145.5 2.7 %shard_map.182 = (bf16[16,256,512]{2,1,0:T(8,128)(2,1)}, bf16[8,16,32,256]{3,2,1,0:T(8,128)(2,1)}) custom-call(s32[6]{0:T(128)S(1)} %stack.71.where, bf16[4,768,256]{2,1,0:T(8,128)(2,1)S(1)} %pad_maximum_fusion.1.own, bf16[4,768,256]{2,1,0:T(8,128)(2,1)S(1)} %collective-permute-done.29.peer), custom_call_target="tpu_custom_call" | custom-call | tf_op jit(solution)/shard_map/pallas_call | solution.py:389
  148.2 0.3 collective-permute-done.26.peer
  148.5 2.7 %shard_map.183 = (bf16[16,256,512]{2,1,0:T(8,128)(2,1)}, bf16[8,16,32,256]{3,2,1,0:T(8,128)(2,1)}) custom-call(s32[6]{0:T(128)S(1)} %stack.71.where, bf16[4,768,256]{2,1,0:T(8,128)(2,1)S(1)} %pad_maximum_fusion.own, bf16[4,768,256]{2,1,0:T(8,128)(2,1)S(1)} %collective-permute-done.26.peer, ...), custom_call_target="tpu_custom_call", output_to_operand_aliasing={{0}: (3, {}), {1}: (4, {})} | custom-call | tf_op jit(solution)/shard_map/pallas_call | solution.py:389
  (42 shorter events, 0.2 us)
Async XLA Ops:
  0.6 25.8 %collective-permute-start.2 = (bf16[1024,512]{1,0:T(8,128)(2,1)}, bf16[1024,512]{1,0:T(8,128)(2,1)S(1)}, u32[]{:S(2)}, u32[]{:S(2)}) collective-permute-start(bf16[1024,512]{1,0:T(8,128)(2,1)} %refs_4_.2), channel_id=1, source_target_pairs={{0,6},{8,14},{1,7},{9,15},{64,70},{72,78},{65,71},{73,79},{2,0},{1... | collective-permute-start | bytes 3145736 | tf_op jit(solution)/shard_map/ppermute | solution.py:44
  4.3 25.1 %collective-permute-start.1 = (bf16[1024,512]{1,0:T(8,128)(2,1)}, bf16[1024,512]{1,0:T(8,128)(2,1)S(1)}, u32[]{:S(2)}, u32[]{:S(2)}) collective-permute-start(bf16[1024,512]{1,0:T(8,128)(2,1)} %refs_4_.2), channel_id=1, source_target_pairs={{0,2},{8,10},{1,3},{9,11},{64,66},{72,74},{65,67},{73,75},{2,4},{1... | collective-permute-start | bytes 3145736 | tf_op jit(solution)/shard_map/ppermute | solution.py:44
  4.4 1.2 copy-start
  5.6 1.6 %copy-start.2 = (bf16[2,4,512,256]{3,2,1,0:T(8,128)(2,1)S(1)}, bf16[2,4,512,256]{3,2,1,0:T(8,128)(2,1)}, u32[]{:S(2)}) copy-start(bf16[2,4,512,256]{3,2,1,0:T(8,128)(2,1)} %adapters.1) | copy-start | bytes 6291460
  7.2 0.7 copy-start.9
  10.2 19.2 %collective-permute-start = (bf16[512,512]{1,0:T(8,128)(2,1)S(1)}, bf16[512,512]{1,0:T(8,128)(2,1)S(1)}, u32[]{:S(2)}, u32[]{:S(2)}) collective-permute-start(bf16[512,512]{1,0:T(8,128)(2,1)S(1)} %get-tuple-element.48), channel_id=1, source_target_pairs={{0,1},{8,9},{1,0},{9,8},{64,65},{72,73},{65,64},{73,72},{2,3},{10,... | collective-permute-start | bytes 1572872 | tf_op jit(solution)/shard_map/ppermute | solution.py:44
  29.4 28.1 %collective-permute-start.7 = (bf16[1024,512]{1,0:T(8,128)(2,1)}, bf16[1024,512]{1,0:T(8,128)(2,1)S(1)}, u32[]{:S(2)}, u32[]{:S(2)}) collective-permute-start(bf16[1024,512]{1,0:T(8,128)(2,1)} %refs_5_.2), channel_id=1, source_target_pairs={{0,1},{8,9},{1,0},{9,8},{64,65},{72,73},{65,64},{73,72},{2,3},{10,... | collective-permute-start | bytes 3145736 | tf_op jit(solution)/shard_map/ppermute | solution.py:44
  33.1 17.4 %collective-permute-start.3 = (bf16[512,512]{1,0:T(8,128)(2,1)S(1)}, bf16[512,512]{1,0:T(8,128)(2,1)S(1)}, u32[]{:S(2)}, u32[]{:S(2)}) collective-permute-start(bf16[512,512]{1,0:T(8,128)(2,1)S(1)} %slice.8), channel_id=1, source_target_pairs={{0,2},{8,10},{1,3},{9,11},{64,66},{72,74},{65,67},{73,75},{2,4},{1... | collective-permute-start | bytes 1572872 | tf_op jit(solution)/shard_map/ppermute | solution.py:44
  33.1 17.4 %collective-permute-start.4 = (bf16[512,512]{1,0:T(8,128)(2,1)S(1)}, bf16[512,512]{1,0:T(8,128)(2,1)S(1)}, u32[]{:S(2)}, u32[]{:S(2)}) collective-permute-start(bf16[512,512]{1,0:T(8,128)(2,1)S(1)} %slice.9), channel_id=1, source_target_pairs={{0,6},{8,14},{1,7},{9,15},{64,70},{72,78},{65,71},{73,79},{2,0},{1... | collective-permute-start | bytes 1572872 | tf_op jit(solution)/shard_map/ppermute | solution.py:44
  35.8 14.7 %copy-start.1 = (bf16[1024,512]{1,0:T(8,128)(2,1)S(1)}, bf16[1024,512]{1,0:T(8,128)(2,1)}, u32[]{:S(2)}) copy-start(bf16[1024,512]{1,0:T(8,128)(2,1)} %refs_4_.2) | copy-start | bytes 3145732
  53.6 16.2 %collective-permute-start.5 = (bf16[2,768,256]{2,1,0:T(8,128)(2,1)S(1)}, bf16[2,768,256]{2,1,0:T(8,128)(2,1)S(1)}, u32[]{:S(2)}, u32[]{:S(2)}) collective-permute-start(bf16[2,768,256]{2,1,0:T(8,128)(2,1)S(1)} %get-tuple-element.55), channel_id=1, source_target_pairs={{0,8},{8,0},{1,9},{9,1},{64,72},{72,64},{65,73},{73,65},{2,10},{10... | collective-permute-start | bytes 2359304 | tf_op jit(solution)/shard_map/ppermute | solution.py:44
  60.0 9.8 %collective-permute-start.8 = (bf16[2,768,256]{2,1,0:T(8,128)(2,1)S(1)}, bf16[2,768,256]{2,1,0:T(8,128)(2,1)S(1)}, u32[]{:S(2)}, u32[]{:S(2)}) collective-permute-start(bf16[2,768,256]{2,1,0:T(8,128)(2,1)S(1)} %get-tuple-element.62), channel_id=1, source_target_pairs={{0,8},{8,0},{1,9},{9,1},{64,72},{72,64},{65,73},{73,65},{2,10},{10... | collective-permute-start | bytes 2359304 | tf_op jit(solution)/shard_map/ppermute | solution.py:44
  60.1 6.8 %collective-permute-start.17 = (bf16[128,512]{1,0:T(8,128)(2,1)S(1)}, bf16[128,512]{1,0:T(8,128)(2,1)S(1)}, u32[]{:S(2)}, u32[]{:S(2)}) collective-permute-start(bf16[128,512]{1,0:T(8,128)(2,1)S(1)} %shard_map.172), channel_id=1, source_target_pairs={{0,1},{8,9},{1,0},{9,8},{64,65},{72,73},{65,64},{73,72},{2,3},{10,... | collective-permute-start | bytes 393224 | tf_op jit(solution)/shard_map/ppermute | solution.py:44
  64.9 4.2 %collective-permute-start.6 = (bf16[2,256,256]{2,1,0:T(8,128)(2,1)S(1)}, bf16[2,256,256]{2,1,0:T(8,128)(2,1)S(1)}, u32[]{:S(2)}, u32[]{:S(2)}) collective-permute-start(bf16[2,256,256]{2,1,0:T(8,128)(2,1)S(1)} %get-tuple-element.59), channel_id=1, source_target_pairs={{0,8},{8,0},{1,9},{9,1},{64,72},{72,64},{65,73},{73,65},{2,10},{10... | collective-permute-start | bytes 786440 | tf_op jit(solution)/shard_map/ppermute | solution.py:44
  66.7 2.4 %collective-permute-start.9 = (bf16[2,256,256]{2,1,0:T(8,128)(2,1)S(1)}, bf16[2,256,256]{2,1,0:T(8,128)(2,1)S(1)}, u32[]{:S(2)}, u32[]{:S(2)}) collective-permute-start(bf16[2,256,256]{2,1,0:T(8,128)(2,1)S(1)} %get-tuple-element.64), channel_id=1, source_target_pairs={{0,8},{8,0},{1,9},{9,1},{64,72},{72,64},{65,73},{73,65},{2,10},{10... | collective-permute-start | bytes 786440 | tf_op jit(solution)/shard_map/ppermute | solution.py:44
  67.0 7.4 %collective-permute-start.20 = (bf16[2,128,512]{2,1,0:T(8,128)(2,1)S(1)}, bf16[2,128,512]{2,1,0:T(8,128)(2,1)S(1)}, u32[]{:S(2)}, u32[]{:S(2)}) collective-permute-start(bf16[2,128,512]{2,1,0:T(8,128)(2,1)S(1)} %pad_maximum_fusion.2.refs_0_), channel_id=1, source_target_pairs={{0,6},{8,14},{1,7},{9,15},{64,70},{72,78},{65,71},{73,79},{2,0},{1... | collective-permute-start | bytes 786440 | tf_op jit(solution)/shard_map/ppermute | solution.py:44
  69.1 7.9 %collective-permute-start.19 = (bf16[2,128,512]{2,1,0:T(8,128)(2,1)S(1)}, bf16[2,128,512]{2,1,0:T(8,128)(2,1)S(1)}, u32[]{:S(2)}, u32[]{:S(2)}) collective-permute-start(bf16[2,128,512]{2,1,0:T(8,128)(2,1)S(1)} %pad_maximum_fusion.2.refs_0_), channel_id=1, source_target_pairs={{0,4},{8,12},{1,5},{9,13},{64,68},{72,76},{65,69},{73,77},{2,6},{1... | collective-permute-start | bytes 786440 | tf_op jit(solution)/shard_map/ppermute | solution.py:44
  69.1 14.9 %collective-permute-start.18 = (bf16[2,128,512]{2,1,0:T(8,128)(2,1)S(1)}, bf16[2,128,512]{2,1,0:T(8,128)(2,1)S(1)}, u32[]{:S(2)}, u32[]{:S(2)}) collective-permute-start(bf16[2,128,512]{2,1,0:T(8,128)(2,1)S(1)} %pad_maximum_fusion.2.refs_0_), channel_id=1, source_target_pairs={{0,2},{8,10},{1,3},{9,11},{64,66},{72,74},{65,67},{73,75},{2,4},{1... | collective-permute-start | bytes 786440 | tf_op jit(solution)/shard_map/ppermute | solution.py:44
  71.8 20.7 %collective-permute-start.10 = (bf16[1024,256]{1,0:T(8,128)(2,1)}, bf16[1024,256]{1,0:T(8,128)(2,1)S(1)}, u32[]{:S(2)}, u32[]{:S(2)}) collective-permute-start(bf16[1024,256]{1,0:T(8,128)(2,1)} %get-tuple-element.66), channel_id=1, source_target_pairs={{0,48},{8,56},{1,49},{9,57},{64,112},{72,120},{65,113},{73,121},{2... | collective-permute-start | bytes 1572872 | tf_op jit(solution)/shard_map/ppermute | solution.py:44
  74.3 18.2 %collective-permute-start.11 = (bf16[1024,256]{1,0:T(8,128)(2,1)}, bf16[1024,256]{1,0:T(8,128)(2,1)S(1)}, u32[]{:S(2)}, u32[]{:S(2)}) collective-permute-start(bf16[1024,256]{1,0:T(8,128)(2,1)} %get-tuple-element.67), channel_id=1, source_target_pairs={{0,16},{8,24},{1,17},{9,25},{64,80},{72,88},{65,81},{73,89},{2,18}... | collective-permute-start | bytes 1572872 | tf_op jit(solution)/shard_map/ppermute | solution.py:44
  74.3 23.1 %collective-permute-start.12 = (bf16[1024,256]{1,0:T(8,128)(2,1)S(1)}, bf16[1024,256]{1,0:T(8,128)(2,1)S(1)}, u32[]{:S(2)}, u32[]{:S(2)}) collective-permute-start(bf16[1024,256]{1,0:T(8,128)(2,1)S(1)} %get-tuple-element.68), channel_id=1, source_target_pairs={{0,32},{8,40},{1,33},{9,41},{64,96},{72,104},{65,97},{73,105},{2,3... | collective-permute-start | bytes 1572872 | tf_op jit(solution)/shard_map/ppermute | solution.py:44
  86.9 20.2 %copy-start.6 = (f32[2,4,32,256]{3,2,1,0:T(8,128)S(1)}, f32[2,4,32,256]{3,2,1,0:T(8,128)}, u32[]{:S(2)}) copy-start(f32[2,4,32,256]{3,2,1,0:T(8,128)} %refs_0_.5) | copy-start | bytes 786436
  86.9 20.2 %copy-start.10 = (s32[16]{0:T(128)S(1)}, s32[16]{0:T(128)}, u32[]{:S(2)}) copy-start(s32[16]{0:T(128)} %regions.3) | copy-start | bytes 196
  86.9 20.2 %all-to-all-start.1 = ((bf16[16,2,32,256]{3,2,1,0:T(8,128)(2,1)}), bf16[16,2,32,256]{3,2,1,0:T(8,128)(2,1)S(1)}, u32[]{:S(2)}, u32[]{:S(2)}) async-start(bf16[16,2,32,256]{3,2,1,0:T(8,128)(2,1)} %shard_map.179), calls=%async_computation.1 | async-start | bytes 1048576 | tf_op jit(solution)/shard_map/all_to_all | solution.py:479
  97.4 14.5 %copy-start.3 = (f32[256,512]{1,0:T(8,128)S(1)}, f32[256,512]{1,0:T(8,128)}, u32[]{:S(2)}) copy-start(f32[256,512]{1,0:T(8,128)} %refs_4_.3) | copy-start | bytes 1572868
  98.9 13.1 %copy-start.4 = (f32[256,512]{1,0:T(8,128)S(1)}, f32[256,512]{1,0:T(8,128)}, u32[]{:S(2)}) copy-start(f32[256,512]{1,0:T(8,128)} %refs_5_.3) | copy-start | bytes 1572868
  98.9 13.1 %copy-start.5 = (f32[256,512]{1,0:T(8,128)S(1)}, f32[256,512]{1,0:T(8,128)}, u32[]{:S(2)}) copy-start(f32[256,512]{1,0:T(8,128)} %refs_6_.1) | copy-start | bytes 1572868
  98.9 11.9 %collective-permute-start.13 = (bf16[256,256]{1,0:T(8,128)(2,1)}, bf16[256,256]{1,0:T(8,128)(2,1)S(1)}, u32[]{:S(2)}, u32[]{:S(2)}) collective-permute-start(bf16[256,256]{1,0:T(8,128)(2,1)} %get-tuple-element.69), channel_id=1, source_target_pairs={{0,0},{8,8},{1,16},{9,24},{64,64},{72,72},{65,80},{73,88},{2,2},{1... | collective-permute-start | bytes 393224 | tf_op jit(solution)/shard_map/ppermute | solution.py:44
  100.5 10.2 %collective-permute-start.14 = (bf16[256,256]{1,0:T(8,128)(2,1)}, bf16[256,256]{1,0:T(8,128)(2,1)S(1)}, u32[]{:S(2)}, u32[]{:S(2)}) collective-permute-start(bf16[256,256]{1,0:T(8,128)(2,1)} %get-tuple-element.70), channel_id=1, source_target_pairs={{0,64},{8,72},{1,80},{9,88},{64,0},{72,8},{65,16},{73,24},{2,66},{... | collective-permute-start | bytes 393224 | tf_op jit(solution)/shard_map/ppermute | solution.py:44
  101.3 9.5 %collective-permute-start.15 = (bf16[256,256]{1,0:T(8,128)(2,1)}, bf16[256,256]{1,0:T(8,128)(2,1)S(1)}, u32[]{:S(2)}, u32[]{:S(2)}) collective-permute-start(bf16[256,256]{1,0:T(8,128)(2,1)} %get-tuple-element.71), channel_id=1, source_target_pairs={{0,32},{8,40},{1,48},{9,56},{64,96},{72,104},{65,112},{73,120},{2,... | collective-permute-start | bytes 393224 | tf_op jit(solution)/shard_map/ppermute | solution.py:44
  106.1 5.8 %collective-permute-start.16 = (bf16[256,256]{1,0:T(8,128)(2,1)S(1)}, bf16[256,256]{1,0:T(8,128)(2,1)S(1)}, u32[]{:S(2)}, u32[]{:S(2)}) collective-permute-start(bf16[256,256]{1,0:T(8,128)(2,1)S(1)} %get-tuple-element.72), channel_id=1, source_target_pairs={{0,96},{8,104},{1,112},{9,120},{64,32},{72,40},{65,48},{73,56},{2,... | collective-permute-start | bytes 393224 | tf_op jit(solution)/shard_map/ppermute | solution.py:44
  107.1 1.0 copy-start.7
  108.0 0.9 copy-start.8
  114.2 8.6 %collective-permute-start.22 = (bf16[768,256]{1,0:T(8,128)(2,1)S(1)}, bf16[768,256]{1,0:T(8,128)(2,1)S(1)}, u32[]{:S(2)}, u32[]{:S(2)}) collective-permute-start(bf16[768,256]{1,0:T(8,128)(2,1)S(1)} %get-tuple-element.78), channel_id=1, source_target_pairs={{0,64},{8,72},{1,65},{9,73},{64,0},{72,8},{65,1},{73,9},{2,66},{10... | collective-permute-start | bytes 1179656 | tf_op jit(solution)/shard_map/ppermute | solution.py:44
  115.0 9.3 %collective-permute-start.21 = (bf16[768,256]{1,0:T(8,128)(2,1)S(1)}, bf16[768,256]{1,0:T(8,128)(2,1)S(1)}, u32[]{:S(2)}, u32[]{:S(2)}) collective-permute-start(bf16[768,256]{1,0:T(8,128)(2,1)S(1)} %get-tuple-element.78), channel_id=1, source_target_pairs={{0,32},{8,40},{1,33},{9,41},{64,96},{72,104},{65,97},{73,105},{2,3... | collective-permute-start | bytes 1179656 | tf_op jit(solution)/shard_map/ppermute | solution.py:44
  117.5 10.9 %collective-permute-start.28 = (bf16[768,256]{1,0:T(8,128)(2,1)S(1)}, bf16[768,256]{1,0:T(8,128)(2,1)S(1)}, u32[]{:S(2)}, u32[]{:S(2)}) collective-permute-start(bf16[768,256]{1,0:T(8,128)(2,1)S(1)} %get-tuple-element.78), channel_id=1, source_target_pairs={{0,48},{8,56},{1,49},{9,57},{64,112},{72,120},{65,113},{73,121},{2... | collective-permute-start | bytes 1179656 | tf_op jit(solution)/shard_map/ppermute | solution.py:44
  119.8 8.6 %collective-permute-start.27 = (bf16[768,256]{1,0:T(8,128)(2,1)S(1)}, bf16[768,256]{1,0:T(8,128)(2,1)S(1)}, u32[]{:S(2)}, u32[]{:S(2)}) collective-permute-start(bf16[768,256]{1,0:T(8,128)(2,1)S(1)} %get-tuple-element.78), channel_id=1, source_target_pairs={{0,16},{8,24},{1,17},{9,25},{64,80},{72,88},{65,81},{73,89},{2,18}... | collective-permute-start | bytes 1179656 | tf_op jit(solution)/shard_map/ppermute | solution.py:44
  122.8 18.5 %collective-permute-start.24 = (bf16[768,256]{1,0:T(8,128)(2,1)S(1)}, bf16[768,256]{1,0:T(8,128)(2,1)S(1)}, u32[]{:S(2)}, u32[]{:S(2)}) collective-permute-start(bf16[768,256]{1,0:T(8,128)(2,1)S(1)} %collective-permute-done.22), channel_id=1, source_target_pairs={{0,48},{8,56},{1,49},{9,57},{64,112},{72,120},{65,113},{73,121},{2... | collective-permute-start | bytes 1179656 | tf_op jit(solution)/shard_map/ppermute | solution.py:44
  123.7 17.6 %collective-permute-start.23 = (bf16[768,256]{1,0:T(8,128)(2,1)S(1)}, bf16[768,256]{1,0:T(8,128)(2,1)S(1)}, u32[]{:S(2)}, u32[]{:S(2)}) collective-permute-start(bf16[768,256]{1,0:T(8,128)(2,1)S(1)} %collective-permute-done.22), channel_id=1, source_target_pairs={{0,16},{8,24},{1,17},{9,25},{64,80},{72,88},{65,81},{73,89},{2,18}... | collective-permute-start | bytes 1179656 | tf_op jit(solution)/shard_map/ppermute | solution.py:44
  124.3 17.0 %collective-permute-start.25 = (bf16[768,256]{1,0:T(8,128)(2,1)S(1)}, bf16[768,256]{1,0:T(8,128)(2,1)S(1)}, u32[]{:S(2)}, u32[]{:S(2)}) collective-permute-start(bf16[768,256]{1,0:T(8,128)(2,1)S(1)} %collective-permute-done.21), channel_id=1, source_target_pairs={{0,64},{8,72},{1,65},{9,73},{64,0},{72,8},{65,1},{73,9},{2,66},{10... | collective-permute-start | bytes 1179656 | tf_op jit(solution)/shard_map/ppermute | solution.py:44
  128.6 16.9 %collective-permute-start.29 = (bf16[4,768,256]{2,1,0:T(8,128)(2,1)S(1)}, bf16[4,768,256]{2,1,0:T(8,128)(2,1)S(1)}, u32[]{:S(2)}, u32[]{:S(2)}) collective-permute-start(bf16[4,768,256]{2,1,0:T(8,128)(2,1)S(1)} %pad_maximum_fusion.1.own), channel_id=1, source_target_pairs={{0,8},{8,0},{1,9},{9,1},{64,72},{72,64},{65,73},{73,65},{2,10},{10... | collective-permute-start | bytes 4718600 | tf_op jit(solution)/shard_map/ppermute | solution.py:44
  141.5 7.0 %collective-permute-start.26 = (bf16[4,768,256]{2,1,0:T(8,128)(2,1)S(1)}, bf16[4,768,256]{2,1,0:T(8,128)(2,1)S(1)}, u32[]{:S(2)}, u32[]{:S(2)}) collective-permute-start(bf16[4,768,256]{2,1,0:T(8,128)(2,1)S(1)} %pad_maximum_fusion.own), channel_id=1, source_target_pairs={{0,8},{8,0},{1,9},{9,1},{64,72},{72,64},{65,73},{73,65},{2,10},{10... | collective-permute-start | bytes 4718600 | tf_op jit(solution)/shard_map/ppermute | solution.py:44

commit v6 on v5

--- a/solution.py
+++ b/solution.py
@@ -490,12 +490,9 @@
     from_back = move(piece, along_x(1))
     from_far = move(piece, along_x(2))
     first = jnp.stack([piece, from_zl, from_back, from_ahead])
-    second = jnp.stack([
-        from_far,
-        move(from_zl, along_x(1)),
-        move(from_zl, along_x(-1)),
-        move(from_far, other_zl),
-    ])
+    zl_ahead = move(from_zl, along_x(-1))
+    zl_back = move(from_zl, along_x(1))
+    second = jnp.stack([from_far, zl_back, zl_ahead, move(from_far, other_zl)])
 
     outs = ()
     for slots, blocks in (

time: 152 us -> 152 us (level)
  no operation moved by 1% of the time
where the time goes in v6:
time: 152 us; the launch traced here: 151 us
  starting transfers between devices  66.5 us (44%)
  waiting for transfers between devices  35.4 us (23%)
  Pallas kernels  27.2 us (18%)
  blocking collectives  14.5 us (10%)
  local copies, waits for them, and re-layouts  5.56 us (4%)
  between operations  1.57 us (1%)
    ppermute x30, starting transfers between devices, move(): return lax.ppermute(array, AXES, pairs)  60.9 us
    ppermute x30, waiting for transfers between devices, move(): return lax.ppermute(array, AXES, pairs)  35.4 us
    all_to_all x1, blocking collectives, swap_among(): return lax.all_to_all(array, axis, 0, 0, axis_index_groups=groups)  14.5 us
    pallas_call x4, Pallas kernels, partials(): pl.pallas_call(functools.partial(partials_kernel, counts), out_shape=(jax...  8.84 us
    all_to_all x1, starting transfers between devices, shards(): got = lax.all_to_all(parts, 'fsdp', 0, 0)  5.61 us
    pallas_call x2, Pallas kernels, place_blocks(): pl.pallas_call(functools.partial(place_kernel, slots), out_shape=shapes,...  5.41 us
    unnamed x22, local copies, waits for them, and re-layouts  5.41 us
  transfers between devices with their start and end apart: 31, of which 8 were waited for; matrix products, arithmetic and copies ran while one was open for 0% of the time, Pallas kernels for 15%

profile of v6, /device:TPU:1, one launch (start us, length us, event | category | flops | bytes accessed | tf_op | source)
XLA Modules:
  0.0 151.3 jit_solution(5600838897849373786)
XLA Ops:
  0.6 3.6 %collective-permute-start.2 = (bf16[1024,512]{1,0:T(8,128)(2,1)}, bf16[1024,512]{1,0:T(8,128)(2,1)S(1)}, u32[]{:S(2)}, u32[]{:S(2)}) collective-permute-start(bf16[1024,512]{1,0:T(8,128)(2,1)} %refs_4_.2), channel_id=1, source_target_pairs={{0,6},{8,14},{1,7},{9,15},{64,70},{72,78},{65,71},{73,79},{2,0},{1... | collective-permute-start | bytes 3145736 | tf_op jit(solution)/shard_map/ppermute | solution.py:44
  4.3 0.0 collective-permute-start.1
  4.3 0.1 stack.71.where
  4.4 1.2 copy-done
  5.6 1.6 %copy-done.2 = bf16[2,4,512,256]{3,2,1,0:T(8,128)(2,1)S(1)} copy-done((bf16[2,4,512,256]{3,2,1,0:T(8,128)(2,1)S(1)}, bf16[2,4,512,256]{3,2,1,0:T(8,128)(2,1)}, u32[]{:S(2)}) %copy-start.2) | copy-done | bytes 2097176
  7.2 0.7 copy-done.9
  7.8 2.4 %shard_map.170 = (f32[512,512]{1,0:T(8,128)S(1)}, bf16[512,512]{1,0:T(8,128)(2,1)S(1)}) custom-call(s32[6]{0:T(128)S(1)} %stack.71.where, s32[16]{0:T(128)S(1)} %copy-done.9, bf16[1024,512]{1,0:T(8,128)(2,1)S(1)} %copy-done, bf16[1024,512]{1,0:T(8,128)(2,1)} %refs_5_.2, bf16[2,4,512,256]{3,2,1,0:T(8,128)(2,1)S(1)} %copy-done.2), custom_call_target="tpu_custom_call" | custom-call | tf_op jit(solution)/shard_map/pallas_call | solution.py:166
  10.2 3.7 %collective-permute-start = (bf16[512,512]{1,0:T(8,128)(2,1)S(1)}, bf16[512,512]{1,0:T(8,128)(2,1)S(1)}, u32[]{:S(2)}, u32[]{:S(2)}) collective-permute-start(bf16[512,512]{1,0:T(8,128)(2,1)S(1)} %get-tuple-element.48), channel_id=1, source_target_pairs={{0,1},{8,9},{1,0},{9,8},{64,65},{72,73},{65,64},{73,72},{2,3},{10,... | collective-permute-start | bytes 1572872 | tf_op jit(solution)/shard_map/ppermute | solution.py:44
  13.9 12.5 %collective-permute-done.2.refs_1_ = bf16[1024,512]{1,0:T(8,128)(2,1)S(1)} collective-permute-done((bf16[1024,512]{1,0:T(8,128)(2,1)}, bf16[1024,512]{1,0:T(8,128)(2,1)S(1)}, u32[]{:S(2)}, u32[]{:S(2)}) %collective-permute-start.2) | collective-permute-done | bytes 1048608 | tf_op jit(solution)/shard_map/ppermute | solution.py:44
  26.4 2.9 %collective-permute-done.1.refs_2_ = bf16[1024,512]{1,0:T(8,128)(2,1)S(1)} collective-permute-done((bf16[1024,512]{1,0:T(8,128)(2,1)}, bf16[1024,512]{1,0:T(8,128)(2,1)S(1)}, u32[]{:S(2)}, u32[]{:S(2)}) %collective-permute-start.1) | collective-permute-done | bytes 1048608 | tf_op jit(solution)/shard_map/ppermute | solution.py:44
  29.4 3.7 %collective-permute-start.7 = (bf16[1024,512]{1,0:T(8,128)(2,1)}, bf16[1024,512]{1,0:T(8,128)(2,1)S(1)}, u32[]{:S(2)}, u32[]{:S(2)}) collective-permute-start(bf16[1024,512]{1,0:T(8,128)(2,1)} %refs_5_.2), channel_id=1, source_target_pairs={{0,1},{8,9},{1,0},{9,8},{64,65},{72,73},{65,64},{73,72},{2,3},{10,... | collective-permute-start | bytes 3145736 | tf_op jit(solution)/shard_map/ppermute | solution.py:44
  33.1 2.7 %collective-permute-start.4 = (bf16[512,512]{1,0:T(8,128)(2,1)S(1)}, bf16[512,512]{1,0:T(8,128)(2,1)S(1)}, u32[]{:S(2)}, u32[]{:S(2)}) collective-permute-start(bf16[512,512]{1,0:T(8,128)(2,1)S(1)} %slice.9), channel_id=1, source_target_pairs={{0,6},{8,14},{1,7},{9,15},{64,70},{72,78},{65,71},{73,79},{2,0},{1... | collective-permute-start | bytes 1572872 | tf_op jit(solution)/shard_map/ppermute | solution.py:44
  35.8 0.1 shard_map.171
  35.9 14.5 %all_to_all.10.parts = bf16[4,128,512]{2,1,0:T(8,128)(2,1)S(1)} all-to-all(bf16[4,128,512]{2,1,0:T(8,128)(2,1)S(1)} %bitcast.19), channel_id=1, replica_groups={{0,2,4,6},{1,3,5,7},{8,10,12,14},{9,11,13,15},{16,18,20,22},{17,19,21,2..., dimensions={0} | all-to-all | bytes 1048576 | tf_op jit(solution)/shard_map/all_to_all | solution.py:48
  50.4 0.1 shard_map.172
  50.5 0.0 collective-permute-done.3.refs_0_
  50.5 0.0 collective-permute-done.4.refs_1_
  50.5 3.1 %shard_map.173 = (bf16[2,768,256]{2,1,0:T(8,128)(2,1)S(1)}, bf16[2,768,256]{2,1,0:T(8,128)(2,1)S(1)}) custom-call(s32[6]{0:T(128)S(1)} %stack.71.where, bf16[1024,512]{1,0:T(8,128)(2,1)S(1)} %copy-done.1, bf16[1024,512]{1,0:T(8,128)(2,1)S(1)} %collective-permute-done.2.refs_1_, bf16[1024,512]{1,0:T(8,128)(2,1)S(1)} %collective-permute-done.1.refs_2_, ...), custom_call_target="tpu_custom_call" | custom-call | tf_op jit(solution)/shard_map/pallas_call | solution.py:103
  53.6 3.9 %collective-permute-start.5 = (bf16[2,768,256]{2,1,0:T(8,128)(2,1)S(1)}, bf16[2,768,256]{2,1,0:T(8,128)(2,1)S(1)}, u32[]{:S(2)}, u32[]{:S(2)}) collective-permute-start(bf16[2,768,256]{2,1,0:T(8,128)(2,1)S(1)} %get-tuple-element.55), channel_id=1, source_target_pairs={{0,8},{8,0},{1,9},{9,1},{64,72},{72,64},{65,73},{73,65},{2,10},{10... | collective-permute-start | bytes 2359304 | tf_op jit(solution)/shard_map/ppermute | solution.py:44
  57.6 2.4 %shard_map.175 = (bf16[2,768,256]{2,1,0:T(8,128)(2,1)S(1)}, bf16[2,768,256]{2,1,0:T(8,128)(2,1)S(1)}) custom-call(s32[6]{0:T(128)S(1)} %stack.71.where, bf16[1024,512]{1,0:T(8,128)(2,1)S(1)} %copy-done.1, bf16[1024,512]{1,0:T(8,128)(2,1)S(1)} %collective-permute-done.2.refs_1_, bf16[1024,512]{1,0:T(8,128)(2,1)S(1)} %collective-permute-done.1.refs_2_, ...), custom_call_target="tpu_custom_call" | custom-call | tf_op jit(solution)/shard_map/pallas_call | solution.py:103
  60.0 0.1 collective-permute-start.8
  60.1 2.8 %collective-permute-start.17 = (bf16[128,512]{1,0:T(8,128)(2,1)S(1)}, bf16[128,512]{1,0:T(8,128)(2,1)S(1)}, u32[]{:S(2)}, u32[]{:S(2)}) collective-permute-start(bf16[128,512]{1,0:T(8,128)(2,1)S(1)} %shard_map.172), channel_id=1, source_target_pairs={{0,1},{8,9},{1,0},{9,8},{64,65},{72,73},{65,64},{73,72},{2,3},{10,... | collective-permute-start | bytes 393224 | tf_op jit(solution)/shard_map/ppermute | solution.py:44
  62.9 2.0 %shard_map.174 = (bf16[2,256,256]{2,1,0:T(8,128)(2,1)S(1)}, bf16[2,256,256]{2,1,0:T(8,128)(2,1)S(1)}) custom-call(s32[6]{0:T(128)S(1)} %stack.71.where, bf16[512,512]{1,0:T(8,128)(2,1)S(1)} %collective-permute-done.3.refs_0_, bf16[512,512]{1,0:T(8,128)(2,1)S(1)} %collective-permute-done.4.refs_1_, bf16[1024,512]{1,0:T(8,128)(2,1)} %refs_5_.2), custom_call_target="tpu_custom_call" | custom-call | tf_op jit(solution)/shard_map/pallas_call | solution.py:103
  64.9 0.4 collective-permute-start.6
  65.4 1.3 shard_map.176
  66.7 0.2 collective-permute-start.9
  66.9 0.0 collective-permute-done.17
  67.0 2.2 %collective-permute-start.20 = (bf16[2,128,512]{2,1,0:T(8,128)(2,1)S(1)}, bf16[2,128,512]{2,1,0:T(8,128)(2,1)S(1)}, u32[]{:S(2)}, u32[]{:S(2)}) collective-permute-start(bf16[2,128,512]{2,1,0:T(8,128)(2,1)S(1)} %pad_maximum_fusion.2.refs_0_), channel_id=1, source_target_pairs={{0,6},{8,14},{1,7},{9,15},{64,70},{72,78},{65,71},{73,79},{2,0},{1... | collective-permute-start | bytes 786440 | tf_op jit(solution)/shard_map/ppermute | solution.py:44
  69.1 0.7 collective-permute-start.18
  69.8 2.0 %shard_map.177 = (bf16[1024,256]{1,0:T(8,128)(2,1)S(1)}, bf16[1024,256]{1,0:T(8,128)(2,1)}, bf16[1024,256]{1,0:T(8,128)(2,1)S(1)}, bf16[1024,256]{1,0:T(8,128)(2,1)}) custom-call(s32[6]{0:T(128)S(1)} %stack.71.where, bf16[2,768,256]{2,1,0:T(8,128)(2,1)S(1)} %get-tuple-element.54.refs_0_, bf16[2,768,256]{2,1,0:T(8,128)(2,1)S(1)} %collective-permute-done.5.refs_1_, ...), custom_call_target="tpu_custom_call" | custom-call | tf_op jit(solution)/shard_map/pallas_call | solution.py:131
  71.8 2.5 %collective-permute-start.10 = (bf16[1024,256]{1,0:T(8,128)(2,1)}, bf16[1024,256]{1,0:T(8,128)(2,1)S(1)}, u32[]{:S(2)}, u32[]{:S(2)}) collective-permute-start(bf16[1024,256]{1,0:T(8,128)(2,1)} %get-tuple-element.66), channel_id=1, source_target_pairs={{0,48},{8,56},{1,49},{9,57},{64,112},{72,120},{65,113},{73,121},{2... | collective-permute-start | bytes 1572872 | tf_op jit(solution)/shard_map/ppermute | solution.py:44
  74.3 2.6 %collective-permute-start.12 = (bf16[1024,256]{1,0:T(8,128)(2,1)S(1)}, bf16[1024,256]{1,0:T(8,128)(2,1)S(1)}, u32[]{:S(2)}, u32[]{:S(2)}) collective-permute-start(bf16[1024,256]{1,0:T(8,128)(2,1)S(1)} %get-tuple-element.68), channel_id=1, source_target_pairs={{0,32},{8,40},{1,33},{9,41},{64,96},{72,104},{65,97},{73,105},{2,3... | collective-permute-start | bytes 1572872 | tf_op jit(solution)/shard_map/ppermute | solution.py:44
  77.0 0.0 collective-permute-done.19.refs_2_
  77.0 7.0 %collective-permute-done.18.refs_1_ = bf16[2,128,512]{2,1,0:T(8,128)(2,1)S(1)} collective-permute-done((bf16[2,128,512]{2,1,0:T(8,128)(2,1)S(1)}, bf16[2,128,512]{2,1,0:T(8,128)(2,1)S(1)}, u32[]{:S(2)}, u32[]{:S(2)}) %collective-permute-start.18) | collective-permute-done | bytes 262176 | tf_op jit(solution)/shard_map/ppermute | solution.py:44
  84.0 2.8 %shard_map.179 = bf16[16,2,32,256]{3,2,1,0:T(8,128)(2,1)} custom-call(s32[6]{0:T(128)S(1)} %stack.71.where, bf16[2,128,512]{2,1,0:T(8,128)(2,1)S(1)} %pad_maximum_fusion.2.refs_0_, bf16[2,128,512]{2,1,0:T(8,128)(2,1)S(1)} %collective-permute-done.18.refs_1_, bf16[2,128,512]{2,1,0:T(8,128)(2,1)S(1)} %collective-permute-done.19.refs_2_, ...), custom_call_target="tpu_custom_call" | custom-call | tf_op jit(solution)/shard_map/pallas_call | solution.py:234
  86.9 5.6 %all-to-all-start.1 = ((bf16[16,2,32,256]{3,2,1,0:T(8,128)(2,1)}), bf16[16,2,32,256]{3,2,1,0:T(8,128)(2,1)S(1)}, u32[]{:S(2)}, u32[]{:S(2)}) async-start(bf16[16,2,32,256]{3,2,1,0:T(8,128)(2,1)} %shard_map.179), calls=%async_computation.1 | async-start | bytes 1048576 | tf_op jit(solution)/shard_map/all_to_all | solution.py:479
  92.5 4.9 %collective-permute-done.12.refs_3_ = bf16[1024,256]{1,0:T(8,128)(2,1)S(1)} collective-permute-done((bf16[1024,256]{1,0:T(8,128)(2,1)S(1)}, bf16[1024,256]{1,0:T(8,128)(2,1)S(1)}, u32[]{:S(2)}, u32[]{:S(2)}) %collective-permute-start.12) | collective-permute-done | bytes 524320 | tf_op jit(solution)/shard_map/ppermute | solution.py:44
  97.4 1.4 shard_map.178
  98.9 1.7 %collective-permute-start.13 = (bf16[256,256]{1,0:T(8,128)(2,1)}, bf16[256,256]{1,0:T(8,128)(2,1)S(1)}, u32[]{:S(2)}, u32[]{:S(2)}) collective-permute-start(bf16[256,256]{1,0:T(8,128)(2,1)} %get-tuple-element.69), channel_id=1, source_target_pairs={{0,0},{8,8},{1,16},{9,24},{64,64},{72,72},{65,80},{73,88},{2,2},{1... | collective-permute-start | bytes 393224 | tf_op jit(solution)/shard_map/ppermute | solution.py:44
  100.5 0.7 collective-permute-start.14
  101.3 4.8 %collective-permute-start.15 = (bf16[256,256]{1,0:T(8,128)(2,1)}, bf16[256,256]{1,0:T(8,128)(2,1)S(1)}, u32[]{:S(2)}, u32[]{:S(2)}) collective-permute-start(bf16[256,256]{1,0:T(8,128)(2,1)} %get-tuple-element.71), channel_id=1, source_target_pairs={{0,32},{8,40},{1,48},{9,56},{64,96},{72,104},{65,112},{73,120},{2,... | collective-permute-start | bytes 393224 | tf_op jit(solution)/shard_map/ppermute | solution.py:44
  106.1 0.1 collective-permute-start.16
  107.0 0.1 pad_maximum_fusion.3.fixes
  107.1 0.0 copy-start.7
  107.1 0.9 copy-done.7
  108.0 0.9 copy-done.8
  109.0 1.8 %shard_map.180 = (f32[2,4,32,256]{3,2,1,0:T(8,128)}, f32[2,4,32,256]{3,2,1,0:T(8,128)}, f32[2,4,32,256]{3,2,1,0:T(8,128)}, bf16[256,256]{1,0:T(8,128)(2,1)S(1)}) custom-call(s32[16]{0:T(128)S(1)} %copy-done.10, f32[2]{0:T(128)S(1)} %pad_maximum_fusion.3.fixes, bf16[16,2,32,256]{3,2,1,0:T(8,128)(2,1)S(1)} %all-to-all-done.1.got, ...), custom_call_target="tpu_custom_call" | custom-call | tf_op jit(solution)/shard_map/pallas_call | solution.py:286
  110.8 1.1 collective-permute-done.16.refs_3_
  112.0 2.2 %shard_map.181 = (f32[256,512]{1,0:T(8,128)}, f32[256,512]{1,0:T(8,128)}, f32[256,512]{1,0:T(8,128)}, bf16[768,256]{1,0:T(8,128)(2,1)S(1)}) custom-call(s32[6]{0:T(128)S(1)} %stack.71.where, f32[2]{0:T(128)S(1)} %pad_maximum_fusion.3.fixes, bf16[256,256]{1,0:T(8,128)(2,1)S(1)} %collective-permute-done.13.refs_0_, ...), custom_call_target="tpu_custom_call" | custom-call | tf_op jit(solution)/shard_map/pallas_call | solution.py:355
  114.2 0.8 collective-permute-start.22
  115.0 2.5 %collective-permute-start.21 = (bf16[768,256]{1,0:T(8,128)(2,1)S(1)}, bf16[768,256]{1,0:T(8,128)(2,1)S(1)}, u32[]{:S(2)}, u32[]{:S(2)}) collective-permute-start(bf16[768,256]{1,0:T(8,128)(2,1)S(1)} %get-tuple-element.78), channel_id=1, source_target_pairs={{0,32},{8,40},{1,33},{9,41},{64,96},{72,104},{65,97},{73,105},{2,3... | collective-permute-start | bytes 1179656 | tf_op jit(solution)/shard_map/ppermute | solution.py:44
  117.5 2.3 %collective-permute-start.28 = (bf16[768,256]{1,0:T(8,128)(2,1)S(1)}, bf16[768,256]{1,0:T(8,128)(2,1)S(1)}, u32[]{:S(2)}, u32[]{:S(2)}) collective-permute-start(bf16[768,256]{1,0:T(8,128)(2,1)S(1)} %get-tuple-element.78), channel_id=1, source_target_pairs={{0,48},{8,56},{1,49},{9,57},{64,112},{72,120},{65,113},{73,121},{2... | collective-permute-start | bytes 1179656 | tf_op jit(solution)/shard_map/ppermute | solution.py:44
  119.8 3.0 %collective-permute-done.22 = bf16[768,256]{1,0:T(8,128)(2,1)S(1)} collective-permute-done((bf16[768,256]{1,0:T(8,128)(2,1)S(1)}, bf16[768,256]{1,0:T(8,128)(2,1)S(1)}, u32[]{:S(2)}, u32[]{:S(2)}) %collective-permute-start.22) | collective-permute-done | bytes 393248 | tf_op jit(solution)/shard_map/ppermute | solution.py:44
  122.8 0.9 collective-permute-start.24
  123.7 0.6 collective-permute-start.23
  124.3 0.6 collective-permute-start.25
  125.0 3.5 %collective-permute-done.28 = bf16[768,256]{1,0:T(8,128)(2,1)S(1)} collective-permute-done((bf16[768,256]{1,0:T(8,128)(2,1)S(1)}, bf16[768,256]{1,0:T(8,128)(2,1)S(1)}, u32[]{:S(2)}, u32[]{:S(2)}) %collective-permute-start.28) | collective-permute-done | bytes 393248 | tf_op jit(solution)/shard_map/ppermute | solution.py:44
  128.4 0.2 pad_maximum_fusion.1.own
  128.6 12.7 %collective-permute-start.29 = (bf16[4,768,256]{2,1,0:T(8,128)(2,1)S(1)}, bf16[4,768,256]{2,1,0:T(8,128)(2,1)S(1)}, u32[]{:S(2)}, u32[]{:S(2)}) collective-permute-start(bf16[4,768,256]{2,1,0:T(8,128)(2,1)S(1)} %pad_maximum_fusion.1.own), channel_id=1, source_target_pairs={{0,8},{8,0},{1,9},{9,1},{64,72},{72,64},{65,73},{73,65},{2,10},{10... | collective-permute-start | bytes 4718600 | tf_op jit(solution)/shard_map/ppermute | solution.py:44
  141.3 0.2 pad_maximum_fusion.own
  141.5 4.0 %collective-permute-start.26 = (bf16[4,768,256]{2,1,0:T(8,128)(2,1)S(1)}, bf16[4,768,256]{2,1,0:T(8,128)(2,1)S(1)}, u32[]{:S(2)}, u32[]{:S(2)}) collective-permute-start(bf16[4,768,256]{2,1,0:T(8,128)(2,1)S(1)} %pad_maximum_fusion.own), channel_id=1, source_target_pairs={{0,8},{8,0},{1,9},{9,1},{64,72},{72,64},{65,73},{73,65},{2,10},{10... | collective-permute-start | bytes 4718600 | tf_op jit(solution)/shard_map/ppermute | solution.py:44
  145.5 2.7 %shard_map.182 = (bf16[16,256,512]{2,1,0:T(8,128)(2,1)}, bf16[8,16,32,256]{3,2,1,0:T(8,128)(2,1)}) custom-call(s32[6]{0:T(128)S(1)} %stack.71.where, bf16[4,768,256]{2,1,0:T(8,128)(2,1)S(1)} %pad_maximum_fusion.1.own, bf16[4,768,256]{2,1,0:T(8,128)(2,1)S(1)} %collective-permute-done.29.peer), custom_call_target="tpu_custom_call" | custom-call | tf_op jit(solution)/shard_map/pallas_call | solution.py:389
  148.2 0.3 collective-permute-done.26.peer
  148.5 2.7 %shard_map.183 = (bf16[16,256,512]{2,1,0:T(8,128)(2,1)}, bf16[8,16,32,256]{3,2,1,0:T(8,128)(2,1)}) custom-call(s32[6]{0:T(128)S(1)} %stack.71.where, bf16[4,768,256]{2,1,0:T(8,128)(2,1)S(1)} %pad_maximum_fusion.own, bf16[4,768,256]{2,1,0:T(8,128)(2,1)S(1)} %collective-permute-done.26.peer, ...), custom_call_target="tpu_custom_call", output_to_operand_aliasing={{0}: (3, {}), {1}: (4, {})} | custom-call | tf_op jit(solution)/shard_map/pallas_call | solution.py:389
  (42 shorter events, 0.2 us)
Async XLA Ops:
  0.6 25.8 %collective-permute-start.2 = (bf16[1024,512]{1,0:T(8,128)(2,1)}, bf16[1024,512]{1,0:T(8,128)(2,1)S(1)}, u32[]{:S(2)}, u32[]{:S(2)}) collective-permute-start(bf16[1024,512]{1,0:T(8,128)(2,1)} %refs_4_.2), channel_id=1, source_target_pairs={{0,6},{8,14},{1,7},{9,15},{64,70},{72,78},{65,71},{73,79},{2,0},{1... | collective-permute-start | bytes 3145736 | tf_op jit(solution)/shard_map/ppermute | solution.py:44
  4.3 25.1 %collective-permute-start.1 = (bf16[1024,512]{1,0:T(8,128)(2,1)}, bf16[1024,512]{1,0:T(8,128)(2,1)S(1)}, u32[]{:S(2)}, u32[]{:S(2)}) collective-permute-start(bf16[1024,512]{1,0:T(8,128)(2,1)} %refs_4_.2), channel_id=1, source_target_pairs={{0,2},{8,10},{1,3},{9,11},{64,66},{72,74},{65,67},{73,75},{2,4},{1... | collective-permute-start | bytes 3145736 | tf_op jit(solution)/shard_map/ppermute | solution.py:44
  4.4 1.2 copy-start
  5.6 1.6 %copy-start.2 = (bf16[2,4,512,256]{3,2,1,0:T(8,128)(2,1)S(1)}, bf16[2,4,512,256]{3,2,1,0:T(8,128)(2,1)}, u32[]{:S(2)}) copy-start(bf16[2,4,512,256]{3,2,1,0:T(8,128)(2,1)} %adapters.1) | copy-start | bytes 6291460
  7.2 0.7 copy-start.9
  10.2 19.2 %collective-permute-start = (bf16[512,512]{1,0:T(8,128)(2,1)S(1)}, bf16[512,512]{1,0:T(8,128)(2,1)S(1)}, u32[]{:S(2)}, u32[]{:S(2)}) collective-permute-start(bf16[512,512]{1,0:T(8,128)(2,1)S(1)} %get-tuple-element.48), channel_id=1, source_target_pairs={{0,1},{8,9},{1,0},{9,8},{64,65},{72,73},{65,64},{73,72},{2,3},{10,... | collective-permute-start | bytes 1572872 | tf_op jit(solution)/shard_map/ppermute | solution.py:44
  29.4 28.1 %collective-permute-start.7 = (bf16[1024,512]{1,0:T(8,128)(2,1)}, bf16[1024,512]{1,0:T(8,128)(2,1)S(1)}, u32[]{:S(2)}, u32[]{:S(2)}) collective-permute-start(bf16[1024,512]{1,0:T(8,128)(2,1)} %refs_5_.2), channel_id=1, source_target_pairs={{0,1},{8,9},{1,0},{9,8},{64,65},{72,73},{65,64},{73,72},{2,3},{10,... | collective-permute-start | bytes 3145736 | tf_op jit(solution)/shard_map/ppermute | solution.py:44
  33.1 17.4 %collective-permute-start.3 = (bf16[512,512]{1,0:T(8,128)(2,1)S(1)}, bf16[512,512]{1,0:T(8,128)(2,1)S(1)}, u32[]{:S(2)}, u32[]{:S(2)}) collective-permute-start(bf16[512,512]{1,0:T(8,128)(2,1)S(1)} %slice.8), channel_id=1, source_target_pairs={{0,2},{8,10},{1,3},{9,11},{64,66},{72,74},{65,67},{73,75},{2,4},{1... | collective-permute-start | bytes 1572872 | tf_op jit(solution)/shard_map/ppermute | solution.py:44
  33.1 17.4 %collective-permute-start.4 = (bf16[512,512]{1,0:T(8,128)(2,1)S(1)}, bf16[512,512]{1,0:T(8,128)(2,1)S(1)}, u32[]{:S(2)}, u32[]{:S(2)}) collective-permute-start(bf16[512,512]{1,0:T(8,128)(2,1)S(1)} %slice.9), channel_id=1, source_target_pairs={{0,6},{8,14},{1,7},{9,15},{64,70},{72,78},{65,71},{73,79},{2,0},{1... | collective-permute-start | bytes 1572872 | tf_op jit(solution)/shard_map/ppermute | solution.py:44
  35.8 14.7 %copy-start.1 = (bf16[1024,512]{1,0:T(8,128)(2,1)S(1)}, bf16[1024,512]{1,0:T(8,128)(2,1)}, u32[]{:S(2)}) copy-start(bf16[1024,512]{1,0:T(8,128)(2,1)} %refs_4_.2) | copy-start | bytes 3145732
  53.6 16.2 %collective-permute-start.5 = (bf16[2,768,256]{2,1,0:T(8,128)(2,1)S(1)}, bf16[2,768,256]{2,1,0:T(8,128)(2,1)S(1)}, u32[]{:S(2)}, u32[]{:S(2)}) collective-permute-start(bf16[2,768,256]{2,1,0:T(8,128)(2,1)S(1)} %get-tuple-element.55), channel_id=1, source_target_pairs={{0,8},{8,0},{1,9},{9,1},{64,72},{72,64},{65,73},{73,65},{2,10},{10... | collective-permute-start | bytes 2359304 | tf_op jit(solution)/shard_map/ppermute | solution.py:44
  60.0 9.8 %collective-permute-start.8 = (bf16[2,768,256]{2,1,0:T(8,128)(2,1)S(1)}, bf16[2,768,256]{2,1,0:T(8,128)(2,1)S(1)}, u32[]{:S(2)}, u32[]{:S(2)}) collective-permute-start(bf16[2,768,256]{2,1,0:T(8,128)(2,1)S(1)} %get-tuple-element.62), channel_id=1, source_target_pairs={{0,8},{8,0},{1,9},{9,1},{64,72},{72,64},{65,73},{73,65},{2,10},{10... | collective-permute-start | bytes 2359304 | tf_op jit(solution)/shard_map/ppermute | solution.py:44
  60.1 6.8 %collective-permute-start.17 = (bf16[128,512]{1,0:T(8,128)(2,1)S(1)}, bf16[128,512]{1,0:T(8,128)(2,1)S(1)}, u32[]{:S(2)}, u32[]{:S(2)}) collective-permute-start(bf16[128,512]{1,0:T(8,128)(2,1)S(1)} %shard_map.172), channel_id=1, source_target_pairs={{0,1},{8,9},{1,0},{9,8},{64,65},{72,73},{65,64},{73,72},{2,3},{10,... | collective-permute-start | bytes 393224 | tf_op jit(solution)/shard_map/ppermute | solution.py:44
  64.9 4.2 %collective-permute-start.6 = (bf16[2,256,256]{2,1,0:T(8,128)(2,1)S(1)}, bf16[2,256,256]{2,1,0:T(8,128)(2,1)S(1)}, u32[]{:S(2)}, u32[]{:S(2)}) collective-permute-start(bf16[2,256,256]{2,1,0:T(8,128)(2,1)S(1)} %get-tuple-element.59), channel_id=1, source_target_pairs={{0,8},{8,0},{1,9},{9,1},{64,72},{72,64},{65,73},{73,65},{2,10},{10... | collective-permute-start | bytes 786440 | tf_op jit(solution)/shard_map/ppermute | solution.py:44
  66.7 2.4 %collective-permute-start.9 = (bf16[2,256,256]{2,1,0:T(8,128)(2,1)S(1)}, bf16[2,256,256]{2,1,0:T(8,128)(2,1)S(1)}, u32[]{:S(2)}, u32[]{:S(2)}) collective-permute-start(bf16[2,256,256]{2,1,0:T(8,128)(2,1)S(1)} %get-tuple-element.64), channel_id=1, source_target_pairs={{0,8},{8,0},{1,9},{9,1},{64,72},{72,64},{65,73},{73,65},{2,10},{10... | collective-permute-start | bytes 786440 | tf_op jit(solution)/shard_map/ppermute | solution.py:44
  67.0 7.4 %collective-permute-start.20 = (bf16[2,128,512]{2,1,0:T(8,128)(2,1)S(1)}, bf16[2,128,512]{2,1,0:T(8,128)(2,1)S(1)}, u32[]{:S(2)}, u32[]{:S(2)}) collective-permute-start(bf16[2,128,512]{2,1,0:T(8,128)(2,1)S(1)} %pad_maximum_fusion.2.refs_0_), channel_id=1, source_target_pairs={{0,6},{8,14},{1,7},{9,15},{64,70},{72,78},{65,71},{73,79},{2,0},{1... | collective-permute-start | bytes 786440 | tf_op jit(solution)/shard_map/ppermute | solution.py:44
  69.1 7.9 %collective-permute-start.19 = (bf16[2,128,512]{2,1,0:T(8,128)(2,1)S(1)}, bf16[2,128,512]{2,1,0:T(8,128)(2,1)S(1)}, u32[]{:S(2)}, u32[]{:S(2)}) collective-permute-start(bf16[2,128,512]{2,1,0:T(8,128)(2,1)S(1)} %pad_maximum_fusion.2.refs_0_), channel_id=1, source_target_pairs={{0,4},{8,12},{1,5},{9,13},{64,68},{72,76},{65,69},{73,77},{2,6},{1... | collective-permute-start | bytes 786440 | tf_op jit(solution)/shard_map/ppermute | solution.py:44
  69.1 14.9 %collective-permute-start.18 = (bf16[2,128,512]{2,1,0:T(8,128)(2,1)S(1)}, bf16[2,128,512]{2,1,0:T(8,128)(2,1)S(1)}, u32[]{:S(2)}, u32[]{:S(2)}) collective-permute-start(bf16[2,128,512]{2,1,0:T(8,128)(2,1)S(1)} %pad_maximum_fusion.2.refs_0_), channel_id=1, source_target_pairs={{0,2},{8,10},{1,3},{9,11},{64,66},{72,74},{65,67},{73,75},{2,4},{1... | collective-permute-start | bytes 786440 | tf_op jit(solution)/shard_map/ppermute | solution.py:44
  71.8 20.7 %collective-permute-start.10 = (bf16[1024,256]{1,0:T(8,128)(2,1)}, bf16[1024,256]{1,0:T(8,128)(2,1)S(1)}, u32[]{:S(2)}, u32[]{:S(2)}) collective-permute-start(bf16[1024,256]{1,0:T(8,128)(2,1)} %get-tuple-element.66), channel_id=1, source_target_pairs={{0,48},{8,56},{1,49},{9,57},{64,112},{72,120},{65,113},{73,121},{2... | collective-permute-start | bytes 1572872 | tf_op jit(solution)/shard_map/ppermute | solution.py:44
  74.3 18.2 %collective-permute-start.11 = (bf16[1024,256]{1,0:T(8,128)(2,1)}, bf16[1024,256]{1,0:T(8,128)(2,1)S(1)}, u32[]{:S(2)}, u32[]{:S(2)}) collective-permute-start(bf16[1024,256]{1,0:T(8,128)(2,1)} %get-tuple-element.67), channel_id=1, source_target_pairs={{0,16},{8,24},{1,17},{9,25},{64,80},{72,88},{65,81},{73,89},{2,18}... | collective-permute-start | bytes 1572872 | tf_op jit(solution)/shard_map/ppermute | solution.py:44
  74.3 23.1 %collective-permute-start.12 = (bf16[1024,256]{1,0:T(8,128)(2,1)S(1)}, bf16[1024,256]{1,0:T(8,128)(2,1)S(1)}, u32[]{:S(2)}, u32[]{:S(2)}) collective-permute-start(bf16[1024,256]{1,0:T(8,128)(2,1)S(1)} %get-tuple-element.68), channel_id=1, source_target_pairs={{0,32},{8,40},{1,33},{9,41},{64,96},{72,104},{65,97},{73,105},{2,3... | collective-permute-start | bytes 1572872 | tf_op jit(solution)/shard_map/ppermute | solution.py:44
  86.9 20.2 %copy-start.6 = (f32[2,4,32,256]{3,2,1,0:T(8,128)S(1)}, f32[2,4,32,256]{3,2,1,0:T(8,128)}, u32[]{:S(2)}) copy-start(f32[2,4,32,256]{3,2,1,0:T(8,128)} %refs_0_.5) | copy-start | bytes 786436
  86.9 20.2 %copy-start.10 = (s32[16]{0:T(128)S(1)}, s32[16]{0:T(128)}, u32[]{:S(2)}) copy-start(s32[16]{0:T(128)} %regions.3) | copy-start | bytes 196
  86.9 20.2 %all-to-all-start.1 = ((bf16[16,2,32,256]{3,2,1,0:T(8,128)(2,1)}), bf16[16,2,32,256]{3,2,1,0:T(8,128)(2,1)S(1)}, u32[]{:S(2)}, u32[]{:S(2)}) async-start(bf16[16,2,32,256]{3,2,1,0:T(8,128)(2,1)} %shard_map.179), calls=%async_computation.1 | async-start | bytes 1048576 | tf_op jit(solution)/shard_map/all_to_all | solution.py:479
  97.4 14.5 %copy-start.3 = (f32[256,512]{1,0:T(8,128)S(1)}, f32[256,512]{1,0:T(8,128)}, u32[]{:S(2)}) copy-start(f32[256,512]{1,0:T(8,128)} %refs_4_.3) | copy-start | bytes 1572868
  98.9 13.1 %copy-start.4 = (f32[256,512]{1,0:T(8,128)S(1)}, f32[256,512]{1,0:T(8,128)}, u32[]{:S(2)}) copy-start(f32[256,512]{1,0:T(8,128)} %refs_5_.3) | copy-start | bytes 1572868
  98.9 13.1 %copy-start.5 = (f32[256,512]{1,0:T(8,128)S(1)}, f32[256,512]{1,0:T(8,128)}, u32[]{:S(2)}) copy-start(f32[256,512]{1,0:T(8,128)} %refs_6_.1) | copy-start | bytes 1572868
  98.9 11.9 %collective-permute-start.13 = (bf16[256,256]{1,0:T(8,128)(2,1)}, bf16[256,256]{1,0:T(8,128)(2,1)S(1)}, u32[]{:S(2)}, u32[]{:S(2)}) collective-permute-start(bf16[256,256]{1,0:T(8,128)(2,1)} %get-tuple-element.69), channel_id=1, source_target_pairs={{0,0},{8,8},{1,16},{9,24},{64,64},{72,72},{65,80},{73,88},{2,2},{1... | collective-permute-start | bytes 393224 | tf_op jit(solution)/shard_map/ppermute | solution.py:44
  100.5 10.2 %collective-permute-start.14 = (bf16[256,256]{1,0:T(8,128)(2,1)}, bf16[256,256]{1,0:T(8,128)(2,1)S(1)}, u32[]{:S(2)}, u32[]{:S(2)}) collective-permute-start(bf16[256,256]{1,0:T(8,128)(2,1)} %get-tuple-element.70), channel_id=1, source_target_pairs={{0,64},{8,72},{1,80},{9,88},{64,0},{72,8},{65,16},{73,24},{2,66},{... | collective-permute-start | bytes 393224 | tf_op jit(solution)/shard_map/ppermute | solution.py:44
  101.3 9.5 %collective-permute-start.15 = (bf16[256,256]{1,0:T(8,128)(2,1)}, bf16[256,256]{1,0:T(8,128)(2,1)S(1)}, u32[]{:S(2)}, u32[]{:S(2)}) collective-permute-start(bf16[256,256]{1,0:T(8,128)(2,1)} %get-tuple-element.71), channel_id=1, source_target_pairs={{0,32},{8,40},{1,48},{9,56},{64,96},{72,104},{65,112},{73,120},{2,... | collective-permute-start | bytes 393224 | tf_op jit(solution)/shard_map/ppermute | solution.py:44
  106.1 5.8 %collective-permute-start.16 = (bf16[256,256]{1,0:T(8,128)(2,1)S(1)}, bf16[256,256]{1,0:T(8,128)(2,1)S(1)}, u32[]{:S(2)}, u32[]{:S(2)}) collective-permute-start(bf16[256,256]{1,0:T(8,128)(2,1)S(1)} %get-tuple-element.72), channel_id=1, source_target_pairs={{0,96},{8,104},{1,112},{9,120},{64,32},{72,40},{65,48},{73,56},{2,... | collective-permute-start | bytes 393224 | tf_op jit(solution)/shard_map/ppermute | solution.py:44
  107.1 1.0 copy-start.7
  108.0 0.9 copy-start.8
  114.2 8.6 %collective-permute-start.22 = (bf16[768,256]{1,0:T(8,128)(2,1)S(1)}, bf16[768,256]{1,0:T(8,128)(2,1)S(1)}, u32[]{:S(2)}, u32[]{:S(2)}) collective-permute-start(bf16[768,256]{1,0:T(8,128)(2,1)S(1)} %get-tuple-element.78), channel_id=1, source_target_pairs={{0,64},{8,72},{1,65},{9,73},{64,0},{72,8},{65,1},{73,9},{2,66},{10... | collective-permute-start | bytes 1179656 | tf_op jit(solution)/shard_map/ppermute | solution.py:44
  115.0 9.3 %collective-permute-start.21 = (bf16[768,256]{1,0:T(8,128)(2,1)S(1)}, bf16[768,256]{1,0:T(8,128)(2,1)S(1)}, u32[]{:S(2)}, u32[]{:S(2)}) collective-permute-start(bf16[768,256]{1,0:T(8,128)(2,1)S(1)} %get-tuple-element.78), channel_id=1, source_target_pairs={{0,32},{8,40},{1,33},{9,41},{64,96},{72,104},{65,97},{73,105},{2,3... | collective-permute-start | bytes 1179656 | tf_op jit(solution)/shard_map/ppermute | solution.py:44
  117.5 10.9 %collective-permute-start.28 = (bf16[768,256]{1,0:T(8,128)(2,1)S(1)}, bf16[768,256]{1,0:T(8,128)(2,1)S(1)}, u32[]{:S(2)}, u32[]{:S(2)}) collective-permute-start(bf16[768,256]{1,0:T(8,128)(2,1)S(1)} %get-tuple-element.78), channel_id=1, source_target_pairs={{0,48},{8,56},{1,49},{9,57},{64,112},{72,120},{65,113},{73,121},{2... | collective-permute-start | bytes 1179656 | tf_op jit(solution)/shard_map/ppermute | solution.py:44
  119.8 8.6 %collective-permute-start.27 = (bf16[768,256]{1,0:T(8,128)(2,1)S(1)}, bf16[768,256]{1,0:T(8,128)(2,1)S(1)}, u32[]{:S(2)}, u32[]{:S(2)}) collective-permute-start(bf16[768,256]{1,0:T(8,128)(2,1)S(1)} %get-tuple-element.78), channel_id=1, source_target_pairs={{0,16},{8,24},{1,17},{9,25},{64,80},{72,88},{65,81},{73,89},{2,18}... | collective-permute-start | bytes 1179656 | tf_op jit(solution)/shard_map/ppermute | solution.py:44
  122.8 18.5 %collective-permute-start.24 = (bf16[768,256]{1,0:T(8,128)(2,1)S(1)}, bf16[768,256]{1,0:T(8,128)(2,1)S(1)}, u32[]{:S(2)}, u32[]{:S(2)}) collective-permute-start(bf16[768,256]{1,0:T(8,128)(2,1)S(1)} %collective-permute-done.22), channel_id=1, source_target_pairs={{0,48},{8,56},{1,49},{9,57},{64,112},{72,120},{65,113},{73,121},{2... | collective-permute-start | bytes 1179656 | tf_op jit(solution)/shard_map/ppermute | solution.py:44
  123.7 17.6 %collective-permute-start.23 = (bf16[768,256]{1,0:T(8,128)(2,1)S(1)}, bf16[768,256]{1,0:T(8,128)(2,1)S(1)}, u32[]{:S(2)}, u32[]{:S(2)}) collective-permute-start(bf16[768,256]{1,0:T(8,128)(2,1)S(1)} %collective-permute-done.22), channel_id=1, source_target_pairs={{0,16},{8,24},{1,17},{9,25},{64,80},{72,88},{65,81},{73,89},{2,18}... | collective-permute-start | bytes 1179656 | tf_op jit(solution)/shard_map/ppermute | solution.py:44
  124.3 17.0 %collective-permute-start.25 = (bf16[768,256]{1,0:T(8,128)(2,1)S(1)}, bf16[768,256]{1,0:T(8,128)(2,1)S(1)}, u32[]{:S(2)}, u32[]{:S(2)}) collective-permute-start(bf16[768,256]{1,0:T(8,128)(2,1)S(1)} %collective-permute-done.21), channel_id=1, source_target_pairs={{0,64},{8,72},{1,65},{9,73},{64,0},{72,8},{65,1},{73,9},{2,66},{10... | collective-permute-start | bytes 1179656 | tf_op jit(solution)/shard_map/ppermute | solution.py:44
  128.6 16.9 %collective-permute-start.29 = (bf16[4,768,256]{2,1,0:T(8,128)(2,1)S(1)}, bf16[4,768,256]{2,1,0:T(8,128)(2,1)S(1)}, u32[]{:S(2)}, u32[]{:S(2)}) collective-permute-start(bf16[4,768,256]{2,1,0:T(8,128)(2,1)S(1)} %pad_maximum_fusion.1.own), channel_id=1, source_target_pairs={{0,8},{8,0},{1,9},{9,1},{64,72},{72,64},{65,73},{73,65},{2,10},{10... | collective-permute-start | bytes 4718600 | tf_op jit(solution)/shard_map/ppermute | solution.py:44
  141.5 7.0 %collective-permute-start.26 = (bf16[4,768,256]{2,1,0:T(8,128)(2,1)S(1)}, bf16[4,768,256]{2,1,0:T(8,128)(2,1)S(1)}, u32[]{:S(2)}, u32[]{:S(2)}) collective-permute-start(bf16[4,768,256]{2,1,0:T(8,128)(2,1)S(1)} %pad_maximum_fusion.own), channel_id=1, source_target_pairs={{0,8},{8,0},{1,9},{9,1},{64,72},{72,64},{65,73},{73,65},{2,10},{10... | collective-permute-start | bytes 4718600 | tf_op jit(solution)/shard_map/ppermute | solution.py:44
